TPU v7x, 512 devices: a whole 4x4x16 slice. The times are simulated.
512 devices in a mesh: ep: 128 (over z, y, core), tp: 4 (over x).
Axes of the slice: x: 4, y: 4, z: 16, core: 2. Of those that a mesh axis runs over, the one named last changes fastest.
Arguments:
- queries: bfloat16 [256, 128, 576], P('ep', 'tp'), may hold values from -40 to 40
- latent_cache: bfloat16 [256, 1024, 576], P('ep', 'tp'), may hold values from -4 to 4
- cache_lengths: int32 [256], P('ep'), may hold values from 128 to 1024, as said below
- moe_tokens: bfloat16 [4096, 3584], P('ep'), may hold values from -6 to 6
- expert_ids: int32 [4096, 8], P('ep'), may hold values from 0 to 127, all different within a row; in each aligned block of 32 rows (0 to 31, 32 to 63, ...) at most 4 rows name the same one
- gate_scores: float32 [4096, 8], P('ep'), may hold values from 0.05 to 1
- up_weight: bfloat16 [128, 3584, 1024], P('ep', None, 'tp'), may hold values from -0.09375 to 0.09375
- down_weight: bfloat16 [128, 1024, 3584], P('ep', 'tp'), may hold values from -0.1875 to 0.1875
Outputs:
- attention_out: bfloat16 [256, 128, 512], P('ep', 'tp')
- expert_mix: bfloat16 [4096, 3584], P('ep', 'tp')
Inputs may be any that keep to these rules, and one draw needn't show every extreme that they name: `expert_ids`: in each aligned block of 32 rows (the rows of one device) no expert is named more than 4 times; the entries of a row differ. `cache_lengths`: some sequence has all 1024 positions valid.
All inputs are finite; a program needn't handle non-finite values.
Results may differ from a plain program's by a relative error of at most 0.017.
Values may be sent and summed in bfloat16 or wider, within the bound.
No kernel may reach another device: no remote copies, remote signals or barrier semaphores. Data moves between devices by JAX's collectives and lax.ppermute only.
A program may use at most 64 MiB of HBM per device.

v0:
```python
import jax
import jax.numpy as jnp
from jax import lax
from jax.sharding import PartitionSpec as P

LATENT = 512
TOP = 8


SCALE = 192.0 ** (-0.5)
ROUTE_SCALE = 2.5
NEGATIVE = -1e30


def empty_states(seq_rows, head_count, latent):
    return (
        jnp.full((seq_rows, head_count), NEGATIVE, jnp.float32),
        jnp.zeros((seq_rows, head_count), jnp.float32),
        jnp.zeros((seq_rows, head_count, latent), jnp.float32),
    )


def fold_block(states, queries, cache_part, cache_lengths, latent):
    running_max, running_total, running_acc = states
    scores = (
        jnp.einsum("rhc,rnc->rhn", queries, cache_part, preferred_element_type=jnp.float32) * SCALE
    )
    positions = jnp.arange(cache_part.shape[1], dtype=jnp.int32)
    visible = positions[None, None, :] < cache_lengths[:, None, None]
    scores = jnp.where(visible, scores, NEGATIVE)
    new_max = jnp.maximum(running_max, jnp.max(scores, axis=-1))
    weights = jnp.where(visible, jnp.exp(scores - new_max[..., None]), 0.0)
    new_total = jnp.sum(weights, axis=-1)
    update_term = jnp.einsum(
        "rhn,rnc->rhc",
        weights.astype(jnp.bfloat16),
        cache_part[:, :, :latent],
        preferred_element_type=jnp.float32,
    )
    return (new_max, new_total, update_term)


def expert_plan(expert_ids, gate_scores, capacity, experts):
    local_rows, top_count = expert_ids.shape
    flat_ids = expert_ids.reshape(-1)
    choose = (flat_ids[:, None] == jnp.arange(experts, dtype=jnp.int32)[None, :]).astype(jnp.int32)
    earlier = jnp.cumsum(choose, axis=0) - choose
    position = jnp.sum(earlier * choose, axis=1)
    target = (flat_ids * capacity + position).reshape(local_rows, top_count)
    slot_ids = jnp.arange(experts * capacity, dtype=jnp.int32)
    matches = slot_ids[:, None, None] == target[None, :, :]
    placing = jnp.any(matches, axis=2).astype(jnp.bfloat16)
    route_weights = gate_scores / jnp.sum(gate_scores, axis=1, keepdims=True) * ROUTE_SCALE
    combine = jnp.sum(jnp.where(matches, route_weights[None, :, :], 0.0), axis=2).T
    return (placing, combine)


def shards(
    queries,
    latent_cache,
    cache_lengths,
    moe_tokens,
    expert_ids,
    gate_scores,
    up_weight,
    down_weight,
):
    seq_rows, local_heads, channels = queries.shape
    tp_count = lax.axis_size("tp")
    final_max, final_total, final_acc = fold_block(
        empty_states(seq_rows, local_heads, LATENT),
        queries,
        lax.all_gather(latent_cache, "tp", axis=1, tiled=True),
        cache_lengths,
        LATENT,
    )
    attention_out = (final_acc / final_total[..., None]).astype(jnp.bfloat16)
    ep_count = lax.axis_size("ep")
    token_rows, model_width = moe_tokens.shape
    capacity = min(token_rows, max(4, (token_rows * TOP + ep_count - 1) // ep_count))
    placing, combine = expert_plan(expert_ids, gate_scores, capacity, ep_count)
    up_local = up_weight[0]
    down_local = down_weight[0]
    columns = model_width // tp_count
    offset_cols = lax.axis_index("tp") * columns
    outgoing = (
        jnp.dot(placing, moe_tokens, preferred_element_type=jnp.float32)
        .astype(jnp.bfloat16)
        .reshape(ep_count, capacity, model_width)
    )
    received = lax.all_to_all(outgoing, "ep", split_axis=0, concat_axis=0, tiled=True)
    sources, slot_count, feature = received.shape
    flat_rows = received.reshape(sources * slot_count, feature)
    hidden = jax.nn.silu(jnp.dot(flat_rows, up_local, preferred_element_type=jnp.float32)).astype(
        jnp.bfloat16
    )
    summed = lax.psum(
        jnp.dot(hidden, down_local, preferred_element_type=jnp.float32)
        .reshape(sources, slot_count, model_width)
        .astype(jnp.bfloat16),
        "tp",
    )
    returned = lax.all_to_all(summed, "ep", split_axis=0, concat_axis=0, tiled=True)
    own_share = lax.dynamic_slice_in_dim(returned, offset_cols, columns, 2)
    mixed_rows = jnp.dot(
        combine,
        own_share.reshape(ep_count * capacity, columns).astype(jnp.float32),
        precision=lax.Precision.HIGHEST,
        preferred_element_type=jnp.float32,
    )
    expert_mix = mixed_rows.astype(jnp.bfloat16)
    return (attention_out, expert_mix)


def solution(mesh):
    placed = (
        P("ep", "tp", None),
        P("ep", "tp", None),
        P("ep"),
        P("ep", None),
        P("ep", None),
        P("ep", None),
        P("ep", None, "tp"),
        P("ep", "tp", None),
    )
    return jax.shard_map(
        shards,
        mesh=mesh,
        in_specs=placed,
        out_specs=(P("ep", "tp", None), P("ep", "tp")),
        check_vma=False,
    )
```

profile of v0, /device:TPU:33, one launch (start us, length us, event | category | flops | bytes accessed | tf_op | source)
XLA Modules:
  0.0 511.5 jit_solution(17077070194072378844)
XLA Ops:
  7.2 0.0 copy-start
  7.2 0.0 all-reduce.2.cloned.1.call-start
  7.2 0.9 copy.33
  8.1 0.1 eq.43
  8.2 0.1 eq.39
  8.3 0.1 copy.36
  8.4 0.2 fusion.19
  8.7 0.2 fusion.21
  8.9 0.1 reduce_sum.40
  9.0 0.2 fusion.14
  9.2 3.9 convolution_convert_fusion.1
  13.2 7.0 %reshape.67 = bf16[128,4,3584]{2,1,0:T(4,128)(2,1)} reshape(bf16[512,3584]{1,0:T(8,128)(2,1)} %convolution_convert_fusion.1) | data formatting | bytes 7340032 | tf_op jit(solution)/shard_map/reshape | solution.py:89
  20.2 183.3 %all_to_all.10 = bf16[128,4,3584]{2,1,0:T(4,128)(2,1)} all-to-all(bf16[128,4,3584]{2,1,0:T(4,128)(2,1)} %reshape.67), channel_id=1, replica_groups=mesh['ep'=128,'tp'=4] {'ep'}, dimensions={0} | all-to-all | bytes 7340032 | tf_op jit(solution)/shard_map/all_to_all | solution.py:91
  203.5 6.7 %reshape.68 = bf16[512,3584]{1,0:T(8,128)(2,1)} reshape(bf16[128,4,3584]{2,1,0:T(4,128)(2,1)} %all_to_all.10) | data formatting | bytes 7340032 | tf_op jit(solution)/shard_map/reshape | solution.py:93
  210.3 3.7 multiply_convert_fusion
  214.0 0.1 dot_general.24
  214.1 0.0 copy-done
  214.1 2.9 convolution_convert_fusion
  217.0 0.0 all-reduce.2.cloned.1.call-update
  217.0 95.2 %all-reduce.2.cloned.1.call-done = bf16[128,4,3584]{2,0,1:T(8,128)(2,1)} async-done(((bf16[128,4,3584]{2,0,1:T(8,128)(2,1)}), bf16[128,4,3584]{2,0,1:T(8,128)(2,1)}) %all-reduce.2.cloned.1.call-update) | async-done | bytes 3670032 | tf_op jit(solution)/shard_map/psum | solution.py:97
  312.2 6.7 %copy.40 = bf16[128,4,3584]{2,1,0:T(4,128)(2,1)} copy(bf16[128,4,3584]{2,0,1:T(8,128)(2,1)} %all-reduce.2.cloned.1.call-done) | data formatting | bytes 7340032 | tf_op jit(solution)/shard_map/psum | solution.py:97
  318.9 0.0 copy-start.2
  318.9 0.0 copy-start.3
  318.9 0.0 copy-start.1
  318.9 17.3 %all-to-all-start.1 = ((bf16[128,4,3584]{2,1,0:T(4,128)(2,1)}), bf16[128,4,3584]{2,1,0:T(4,128)(2,1)}, u32[]{:S(2)}, u32[]{:S(2)}) async-start(bf16[128,4,3584]{2,1,0:T(4,128)(2,1)} %copy.40), calls=%async_computation.1 | async-start | bytes 7340032 | tf_op jit(solution)/shard_map/all_to_all | solution.py:103
  336.2 0.0 all-gather.2.cloned.1.call-start
  336.3 0.7 all-gather.2.cloned.1.call-update
  337.0 0.0 copy-done.2
  337.0 0.1 copy.38
  337.1 0.2 select_reduce_fusion
  337.3 0.0 copy-done.3
  337.3 0.1 iota_compare_fusion.2
  337.4 44.5 %all-gather.2.cloned.1.call-done = bf16[2,1024,576]{1,2,0:T(8,128)(2,1)} async-done(((bf16[2,256,576]{1,2,0:T(8,128)(2,1)}), bf16[2,1024,576]{1,2,0:T(8,128)(2,1)}) %all-gather.2.cloned.1.call-update) | async-done | bytes 2359312 | tf_op jit(solution)/shard_map/all_gather | solution.py:73
  381.9 0.0 copy-done.1
  381.9 2.3 fusion.28
  384.2 0.2 fusion.16
  384.4 3.0 fusion.9
  387.4 112.3 %all-to-all-done.1 = bf16[128,4,3584]{2,1,0:T(4,128)(2,1)} async-done(((bf16[128,4,3584]{2,1,0:T(4,128)(2,1)}), bf16[128,4,3584]{2,1,0:T(4,128)(2,1)}, u32[]{:S(2)}, u32[]{:S(2)}) %all-to-all-start.1) | async-done | bytes 3670048 | tf_op jit(solution)/shard_map/all_to_all | solution.py:103
  499.7 1.5 constant_dynamic-slice_fusion
  501.2 1.1 reshape.69
  502.3 2.3 convolution_convert_fusion.2
  (10 shorter events, 0.1 us)
Async XLA Ops:
  7.2 206.9 %copy-start = (bf16[1,256,3584]{2,1,0:T(8,128)(2,1)S(1)}, bf16[1,256,3584]{2,1,0:T(8,128)(2,1)}, u32[]{:S(2)}) copy-start(bf16[1,256,3584]{2,1,0:T(8,128)(2,1)} %param.15) | copy-start | bytes 5505028
  7.2 305.1 %all-reduce.2.cloned.1.call-start = ((), (), s32[]{:S(2)}) async-start(), calls=%async_computation.3 | async-start | bytes 7340032 | tf_op jit(solution)/shard_map/psum | solution.py:97
  318.9 18.1 %copy-start.2 = (f32[32,8]{0,1:T(8,128)S(1)}, f32[32,8]{0,1:T(8,128)}, u32[]{:S(2)}) copy-start(f32[32,8]{0,1:T(8,128)} %param.13) | copy-start | bytes 3076
  318.9 18.4 %copy-start.3 = (s32[2]{0:T(128)S(1)}, s32[2]{0:T(128)}, u32[]{:S(2)}) copy-start(s32[2]{0:T(128)} %param.10) | copy-start | bytes 28
  318.9 63.0 %copy-start.1 = (bf16[2,32,576]{2,1,0:T(8,128)(2,1)S(1)}, bf16[2,32,576]{2,1,0:T(8,128)(2,1)}, u32[]{:S(2)}) copy-start(bf16[2,32,576]{2,1,0:T(8,128)(2,1)} %param.8) | copy-start | bytes 221188
  318.9 180.8 %all-to-all-start.1 = ((bf16[128,4,3584]{2,1,0:T(4,128)(2,1)}), bf16[128,4,3584]{2,1,0:T(4,128)(2,1)}, u32[]{:S(2)}, u32[]{:S(2)}) async-start(bf16[128,4,3584]{2,1,0:T(4,128)(2,1)} %copy.40), calls=%async_computation.1 | async-start | bytes 7340032 | tf_op jit(solution)/shard_map/all_to_all | solution.py:103
  336.2 45.7 %all-gather.2.cloned.1.call-start = ((), (), s32[]{:S(2)}) async-start(), calls=%async_computation.2 | async-start | bytes 2949120 | tf_op jit(solution)/shard_map/all_gather | solution.py:73
Sparse Core Ops, SparseCore 0:
  217.1 95.0 all-reduce.1
  339.1 42.7 all-gather.1
where the time goes:
time: 514 us; the launch traced here: 511 us
  waiting for transfers between devices  253 us (49%)
  blocking collectives  183 us (36%)
  local copies, waits for them, and re-layouts  24.5 us (5%)
  matrix products  18.2 us (4%)
  starting transfers between devices  17.4 us (3%)
  between operations  14.2 us (3%)
    all_to_all x1, blocking collectives, shards(): lax.all_to_all(outgoing, 'ep', split_axis=0, concat_axis=0, tiled=True)  183 us
    all_to_all x1, waiting for transfers between devices, shards(): lax.all_to_all(summed, 'ep', split_axis=0, concat_axis=0, tiled=True)  112 us
    psum x1, waiting for transfers between devices, shards(): lax.psum(jnp.dot(hidden, down_local, preferred_element_type=jnp.float32)....  95.2 us
    all_gather x1, waiting for transfers between devices, shards(): lax.all_gather(latent_cache, 'tp', axis=1, tiled=True)  44.5 us
    all_to_all x1, starting transfers between devices, shards(): lax.all_to_all(summed, 'ep', split_axis=0, concat_axis=0, tiled=True)  17.3 us
  transfers between devices with their start and end apart: 3, of which 3 were waited for; matrix products, arithmetic and copies ran while one was open for 1% of the time, Pallas kernels for 0%

commit v1 on v0

v1 whole, which is shorter than its diff:
```python
import functools

import jax
import jax.numpy as jnp
from jax import lax
from jax.experimental import pallas as pl
from jax.experimental.pallas import tpu as pltpu
from jax.sharding import Mesh, PartitionSpec as P

LATENT = 512
TOP = 8
CAP = 4
SCALE = 192.0 ** (-0.5)
ROUTE_SCALE = 2.5
NEGATIVE = -1e30
LANES = 128
VMEM = 32 << 20
INSIDE = pl.BlockSpec(memory_space=pltpu.VMEM)
OUTSIDE = pl.BlockSpec(memory_space=pl.ANY)

EP = ("zh", "zl", "y", "c")
NEAR = ("zl", "y", "c")
FAR = "zh"
BF = jnp.bfloat16


def cost(flops, *arrays):
    size = sum(a.size * a.dtype.itemsize for a in arrays)
    return pl.CostEstimate(flops=flops, bytes_accessed=size, transcendentals=0)


def attend_kernel(place_ref, q0, q1, q2, q3, cache_ref, out_ref):
    r = pl.program_id(0)
    keys = cache_ref[0]
    asked = [q[:, : keys.shape[0]] for q in (q0, q1, q2, q3)]
    count = asked[0].shape[0]
    scores = jnp.dot(jnp.concatenate(asked, axis=0), keys, preferred_element_type=jnp.float32) * SCALE
    positions = place_ref[2] + lax.broadcasted_iota(jnp.int32, scores.shape, 1)
    visible = positions < place_ref[r]
    scores = jnp.where(visible, scores, NEGATIVE)
    peak = jnp.max(scores, axis=1, keepdims=True)
    weights = jnp.where(visible, jnp.exp(scores - peak), 0.0)
    total = jnp.sum(weights, axis=1, keepdims=True)
    mixed = lax.dot_general(
        weights.astype(BF), keys[:LATENT], (((1,), (1,)), ((), ())), preferred_element_type=jnp.float32
    )
    mean = (mixed / jnp.where(total > 0.0, total, 1.0)).astype(BF)
    lane = lax.broadcasted_iota(jnp.int32, (scores.shape[0], LANES), 1)
    stats = jnp.zeros((scores.shape[0], LANES), jnp.float32)
    for first, value in ((0, peak), (3, total)):
        for i in range(3):
            part = value.astype(BF).astype(jnp.float32)
            stats = jnp.where(lane == first + i, part, stats)
            value = value - part
    stats = stats.astype(BF)
    for k in range(4):
        out_ref[k, 0, :, :LATENT] = mean[k * count : (k + 1) * count]
        out_ref[k, 0, :, LATENT:] = stats[k * count : (k + 1) * count]


def attend_own(asked, starts, count, cache, cache_lengths, first):
    keys = jnp.swapaxes(cache, 1, 2)
    rows, channels, positions = keys.shape
    out = jax.ShapeDtypeStruct((len(asked), rows, count, LATENT + LANES), BF)
    place = jnp.concatenate([cache_lengths, first.reshape(1).astype(jnp.int32)])

    def queries(array, start):
        return pl.BlockSpec((count, array.shape[1]), lambda r, place: (start // count + r, 0))

    return pl.pallas_call(
        attend_kernel,
        out_shape=out,
        grid_spec=pltpu.PrefetchScalarGridSpec(
            num_scalar_prefetch=1,
            grid=(rows,),
            in_specs=[queries(a, i) for a, i in zip(asked, starts)]
            + [pl.BlockSpec((1, channels, positions), lambda r, place: (r, 0, 0))],
            out_specs=pl.BlockSpec((len(asked), 1, count, LATENT + LANES), lambda r, place: (0, r, 0, 0)),
        ),
        compiler_params=pltpu.CompilerParams(vmem_limit_bytes=VMEM),
        cost_estimate=cost(4 * rows * 4 * count * channels * positions, cache, out),
        name="attend_own",
    )(place, *asked, keys)


def merge(parts):
    means = [p[..., :LATENT].astype(jnp.float32) for p in parts]
    stats = [p[..., LATENT : LATENT + 6].astype(jnp.float32) for p in parts]
    peaks = [q[..., 0] + q[..., 1] + q[..., 2] for q in stats]
    totals = [q[..., 3] + q[..., 4] + q[..., 5] for q in stats]
    peak = jnp.max(jnp.stack(peaks), axis=0)
    shares = [t * jnp.exp(p - peak) for p, t in zip(peaks, totals)]
    whole = sum(shares)
    return sum((s / whole)[..., None] * m for s, m in zip(shares, means)).astype(BF)


def routing_columns(expert_ids, gate_scores):
    route = gate_scores / jnp.sum(gate_scores, axis=1, keepdims=True) * ROUTE_SCALE
    high = lax.reduce_precision(route, 8, 7)
    low = route - high
    rows = expert_ids.shape[0]
    parts = [expert_ids.astype(BF), high.astype(BF), low.astype(BF)]
    return jnp.concatenate(parts + [jnp.zeros((rows, LANES - 3 * TOP), BF)], axis=1)


def place_kernel(first_ref, packed_ref, out_ref, held, sems, *, rows, experts, slots):
    total, wide = packed_ref.shape
    cols = wide - LANES
    ids = packed_ref[:, cols:].astype(jnp.float32).T
    own = (first_ref[0] + lax.broadcasted_iota(jnp.int32, (experts, total), 0)).astype(jnp.float32)
    named = own == ids[0:1]
    for k in range(1, TOP):
        named = named | (own == ids[k : k + 1])
    before, after = (lax.broadcasted_iota(jnp.int32, (total, total), d) for d in (0, 1))
    earlier = (before < after) & (before // rows == after // rows)
    rank = jnp.dot(
        jnp.where(named, 1.0, 0.0).astype(BF),
        jnp.where(earlier, 1.0, 0.0).astype(BF),
        preferred_element_type=jnp.float32,
    )
    block = lax.broadcasted_iota(jnp.int32, (experts, total), 1) // rows
    slot = jnp.where(named, rank + (block * CAP).astype(jnp.float32), -1.0)
    place = lax.broadcasted_iota(jnp.int32, (experts, slots, total), 1).astype(jnp.float32)
    put = jnp.where(jnp.broadcast_to(slot[:, None, :], place.shape) == place, 1.0, 0.0)
    put = put.reshape(experts * slots, total).astype(BF)
    step = held.shape[0] // sems.shape[0]
    copies = []
    for i in range(sems.shape[0]):
        part = pl.ds(i * step, step)
        moved = jnp.dot(put[i * step : (i + 1) * step], packed_ref[:, :cols], preferred_element_type=jnp.float32)
        held[part] = moved.astype(BF)
        copies.append(pltpu.make_async_copy(held.at[part], out_ref.at[part], sems.at[i]))
        copies[-1].start()
    for copy in copies:
        copy.wait()


def placed_rows(first, packed, rows, experts, slots):
    total, wide = packed.shape
    out = jax.ShapeDtypeStruct((experts * slots, wide - LANES), BF)
    return pl.pallas_call(
        functools.partial(place_kernel, rows=rows, experts=experts, slots=slots),
        out_shape=out,
        in_specs=[pl.BlockSpec(memory_space=pltpu.SMEM), INSIDE],
        out_specs=OUTSIDE,
        scratch_shapes=[pltpu.VMEM(out.shape, BF), pltpu.SemaphoreType.DMA((4,))],
        compiler_params=pltpu.CompilerParams(vmem_limit_bytes=VMEM),
        cost_estimate=cost(2 * out.size * total, packed, out),
        name="placed_rows",
    )(first.reshape(1), packed)


def shares(columns, rows, first, experts, blocks):
    ids = columns[:, :TOP].astype(jnp.float32)
    high = columns[:, TOP : 2 * TOP].astype(jnp.float32)
    low = columns[:, 2 * TOP : 3 * TOP].astype(jnp.float32)
    own = (first + jnp.arange(experts, dtype=jnp.int32)).astype(jnp.float32)
    hit = ids[:, :, None] == own[None, None, :]
    named = jnp.any(hit, axis=1)
    w_high = jnp.sum(jnp.where(hit, high[:, :, None], 0.0), axis=1)
    w_low = jnp.sum(jnp.where(hit, low[:, :, None], 0.0), axis=1)
    total = rows * blocks
    t = jnp.arange(total, dtype=jnp.int32)
    before = (t[None, :] < t[:, None]) & (t[None, :] // rows == t[:, None] // rows)
    rank = jnp.dot(before.astype(BF), named.astype(BF), preferred_element_type=jnp.float32)
    slot = rank + ((t // rows) * CAP).astype(jnp.float32)[:, None]
    slot = jnp.where(named, slot, -1.0)
    slots = jnp.arange(blocks * CAP, dtype=jnp.int32).astype(jnp.float32)
    take = slot[:, :, None] == slots[None, None, :]
    c_high = jnp.where(take, w_high[:, :, None], 0.0).astype(BF).reshape(total, -1)
    c_low = jnp.where(take, w_low[:, :, None], 0.0).astype(BF).reshape(total, -1)
    return jnp.concatenate([c_high, c_low], axis=0)


def up_kernel(rows_ref, weight_ref, out_ref, held, sems):
    copies = []
    for j in range(weight_ref.shape[0]):
        held[j] = jnp.dot(rows_ref[...], weight_ref[j], preferred_element_type=jnp.float32).astype(BF)
        copies.append(pltpu.make_async_copy(held.at[j], out_ref.at[j], sems.at[j]))
        copies[-1].start()
    for copy in copies:
        copy.wait()


def up_parts(rows, weight):
    groups, depth, width = weight.shape
    count = rows.shape[0]
    out = jax.ShapeDtypeStruct((groups, count, width), BF)
    return pl.pallas_call(
        up_kernel,
        out_shape=out,
        in_specs=[INSIDE, INSIDE],
        out_specs=OUTSIDE,
        scratch_shapes=[pltpu.VMEM(out.shape, BF), pltpu.SemaphoreType.DMA((groups,))],
        compiler_params=pltpu.CompilerParams(vmem_limit_bytes=VMEM),
        cost_estimate=cost(2 * count * depth * width * groups, rows, weight, out),
        name="up_parts",
    )(rows, weight)


def hidden_kernel(part_ref, out_ref, held, sems):
    groups, count, _ = part_ref.shape
    step = count // sems.shape[0]
    copies = []
    for i in range(sems.shape[0]):
        rows = pl.ds(i * step, step)
        value = part_ref[0, rows].astype(jnp.float32)
        for j in range(1, groups):
            value = value + part_ref[j, rows].astype(jnp.float32)
        held[rows] = (value / (1.0 + jnp.exp(-value))).astype(BF)
        for j in range(groups):
            copies.append(pltpu.make_async_copy(held.at[rows], out_ref.at[j, rows], sems.at[i, j]))
            copies[-1].start()
    for copy in copies:
        copy.wait()


def hidden_copies(part):
    return pl.pallas_call(
        hidden_kernel,
        out_shape=jax.ShapeDtypeStruct(part.shape, BF),
        in_specs=[INSIDE],
        out_specs=OUTSIDE,
        scratch_shapes=[pltpu.VMEM(part.shape[1:], BF), pltpu.SemaphoreType.DMA((2, part.shape[0]))],
        compiler_params=pltpu.CompilerParams(vmem_limit_bytes=VMEM),
        cost_estimate=cost(10 * part.size, part, part),
        name="hidden_copies",
    )(part)


def down_kernel(x_ref, hidden_ref, w0, w1, w2a, w2b, w3, out_ref, held, sems):
    groups = hidden_ref.shape[0]
    step = held.shape[0] // sems.shape[0]
    place = [lax.rem(x_ref[0] + k, groups) for k in range(groups)]
    copies = []

    def dot(left, right):
        return jnp.dot(left, right, preferred_element_type=jnp.float32)

    for i in range(sems.shape[0]):
        rows = pl.ds(i * step, step)
        total = dot(hidden_ref[place[0], rows], w0[...])
        total = total + dot(hidden_ref[place[1], rows], w1[...])
        total = total + dot(hidden_ref[place[3], rows], w3[...])
        far = hidden_ref[place[2], rows]
        depth = w0.shape[0] // 2
        total = total + dot(far[:, :depth], w2a[:depth, :])
        total = total + dot(far[:, depth:], w2b[:depth, :])
        held[rows] = total.astype(BF)
        copies.append(pltpu.make_async_copy(held.at[rows], out_ref.at[rows], sems.at[i]))
        copies[-1].start()
    for copy in copies:
        copy.wait()


def down_rows(x, hidden, own, after, far_low, far_high, before):
    out = jax.ShapeDtypeStruct((hidden.shape[1], own.shape[1]), BF)
    return pl.pallas_call(
        down_kernel,
        out_shape=out,
        in_specs=[pl.BlockSpec(memory_space=pltpu.SMEM)] + [INSIDE] * 6,
        out_specs=OUTSIDE,
        scratch_shapes=[pltpu.VMEM(out.shape, BF), pltpu.SemaphoreType.DMA((4,))],
        compiler_params=pltpu.CompilerParams(vmem_limit_bytes=VMEM),
        cost_estimate=cost(2 * hidden.size * own.shape[1], hidden, own, own, own, own, out),
        name="down_rows",
    )(x.reshape(1), hidden, own, after, far_low, far_high, before)


def shift(array, by, tp):
    return lax.ppermute(array, "tp", [(i, (i + by) % tp) for i in range(tp)])


def shards(queries, latent_cache, cache_lengths, moe_tokens, expert_ids, gate_scores, up_weight, down_weight):
    tp = lax.axis_size("tp")
    x = lax.axis_index("tp")
    rows, width = moe_tokens.shape
    cols = width // tp
    group = up_weight.shape[2]
    near = lax.axis_size(NEAR)
    far = lax.axis_size(FAR)
    slots = far * CAP

    up = lax.all_to_all(up_weight[0].reshape(tp, cols, group), "tp", 0, 0, tiled=True)

    mine = lax.dynamic_slice_in_dim(moe_tokens, x * cols, cols, 1)
    packed = jnp.concatenate([mine, routing_columns(expert_ids, gate_scores)], axis=1)
    packed = lax.all_gather(packed, FAR, axis=0, tiled=True)
    packed, up = lax.optimization_barrier((packed, up))
    first = lax.axis_index(FAR) * near
    outgoing = placed_rows(first, packed, rows, near, slots)

    weight = down_weight[0]
    half = group // 2
    held = queries.reshape(-1, queries.shape[2])
    ask = jnp.pad(held, ((0, 0), (0, cols - held.shape[1])))

    def columns_for(k, low, high):
        return lax.dynamic_slice_in_dim(weight[low:high], (x + k) % tp * cols, cols, 1)

    right = shift(jnp.concatenate([columns_for(2, 0, half), ask], axis=0), 1, tp)
    left = shift(jnp.concatenate([columns_for(2, half, group), ask], axis=0), tp - 1, tp)
    before = shift(columns_for(1, 0, group), 1, tp)
    after = shift(columns_for(tp - 1, 0, group), tp - 1, tp)
    far_right, far_left = shift(right, 1, tp), shift(left, tp - 1, tp)
    received = lax.all_to_all(outgoing.reshape(near, slots, cols), NEAR, 0, 0, tiled=True)
    received, right, left, before, after, far_right, far_left = lax.optimization_barrier(
        (received.reshape(near * slots, cols), right, left, before, after, far_right, far_left)
    )
    take = shares(packed[:, cols:], rows, first, near, far)

    part = lax.all_to_all(up_parts(received, up), "tp", 0, 0, tiled=True)
    hidden = lax.all_to_all(hidden_copies(part), "tp", 0, 0, tiled=True)

    asked, starts = [held, left, far_right, right], [0, half, half, half]
    first = x * latent_cache.shape[1]
    own = attend_own(asked, starts, queries.shape[1], latent_cache, cache_lengths, first)
    hidden, own = lax.optimization_barrier((hidden, own))
    shared = [own[0]] + [shift(own[k], k, tp) for k in range(1, tp)]
    output = down_rows(x, hidden, columns_for(0, 0, group), after, far_right, far_left, before)

    returned = lax.all_to_all(output.reshape(near, slots, cols), NEAR, 0, 0, tiled=True)
    returned, shared = lax.optimization_barrier((returned, shared))
    mixed = jnp.dot(take, returned.reshape(near * slots, cols), preferred_element_type=jnp.float32)
    mixed = (mixed[: far * rows] + mixed[far * rows :]).astype(BF).reshape(far, rows, cols)
    mixed = lax.all_to_all(mixed, FAR, 0, 0, tiled=True)
    attention_out = merge(shared)
    expert_mix = jnp.sum(mixed.astype(jnp.float32), axis=0).astype(BF)
    return (attention_out, expert_mix)


def solution(mesh):
    devices = mesh.devices
    split = Mesh(devices.reshape(4, 4, 4, 2, devices.shape[1]), EP + ("tp",))
    placed = (
        P(EP, "tp", None),
        P(EP, "tp", None),
        P(EP),
        P(EP, None),
        P(EP, None),
        P(EP, None),
        P(EP, None, "tp"),
        P(EP, "tp", None),
    )
    return jax.shard_map(
        shards,
        mesh=split,
        in_specs=placed,
        out_specs=(P(EP, "tp", None), P(EP, "tp")),
        check_vma=False,
    )
```

time: 514 us -> 183 us (0.36)
  waiting for transfers between devices: 253 us -> 48.3 us
  blocking collectives: 183 us -> 40 us
  starting transfers between devices: 17.4 us -> 68 us
  matrix products: 18.2 us -> 0.66 us
  local copies, waits for them, and re-layouts: 24.5 us -> 8.79 us
  between operations: 14.2 us -> 1.06 us
  Pallas kernels: 0 us -> 10.2 us
    all_to_all x1, blocking collectives: 183 us -> 16.3 us  [shards(): part = lax.all_to_all(up_parts(received, up), 'tp', 0, 0, tiled=True)]
    psum x1 -> x0, waiting for transfers between devices: 95.2 us -> none  [shards(): lax.psum(jnp.dot(hidden, down_local, preferred_element_type=jnp.float32)....]
    all_to_all x1 -> x5, waiting for transfers between devices: 112 us -> 37 us  [the longest x1 17.2 us: shards(): mixed = lax.all_to_all(mixed, FAR, 0, 0, tiled=True)]
    all_gather x1 -> x0, waiting for transfers between devices: 44.5 us -> none  [shards(): lax.all_gather(latent_cache, 'tp', axis=1, tiled=True)]
    ppermute x0 -> x9, starting transfers between devices: none -> 27.9 us  [shift(): return lax.ppermute(array, 'tp', [(i, (i + by) % tp) for i in range(tp)])]
    all_gather x0 -> x1, blocking collectives: none -> 23.7 us  [shards(): packed = lax.all_gather(packed, FAR, axis=0, tiled=True)]
    all_to_all x1 -> x5, starting transfers between devices: 17.3 us -> 40.1 us  [the longest x1 11.8 us: shards(): lax.all_to_all(output.reshape(near, slots, cols), NEAR, 0, 0, tiled=True)]
    dot_general x6 -> x2, matrix products: 18.2 us -> 0.66 us  [the longest x1 0.46 us: shards(): jnp.dot(take, returned.reshape(near * slots, cols), preferred_element_typ...]
  transfers between devices with their start and end apart: 3 -> 14, of which waited for: 3 -> 9; matrix products, arithmetic and copies ran while one was open for 1% -> 4% of each run, Pallas kernels for 0% -> 1%
where the time goes in v1:
time: 183 us; the launch traced here: 182 us
  starting transfers between devices  68 us (37%)
  waiting for transfers between devices  48.3 us (26%)
  blocking collectives  40 us (22%)
  Pallas kernels  10.2 us (6%)
  local copies, waits for them, and re-layouts  8.79 us (5%)
  other arithmetic  4.97 us (3%)
    ppermute x9, starting transfers between devices, shift(): return lax.ppermute(array, 'tp', [(i, (i + by) % tp) for i in range(tp)])  27.9 us
    all_gather x1, blocking collectives, shards(): packed = lax.all_gather(packed, FAR, axis=0, tiled=True)  23.7 us
    all_to_all x1, waiting for transfers between devices, shards(): mixed = lax.all_to_all(mixed, FAR, 0, 0, tiled=True)  17.2 us
    all_to_all x1, blocking collectives, shards(): part = lax.all_to_all(up_parts(received, up), 'tp', 0, 0, tiled=True)  16.3 us
    all_to_all x1, starting transfers between devices, shards(): lax.all_to_all(output.reshape(near, slots, cols), NEAR, 0, 0, tiled=True)  11.8 us
    ppermute x9, waiting for transfers between devices, shift(): return lax.ppermute(array, 'tp', [(i, (i + by) % tp) for i in range(tp)])  11.2 us
    all_to_all x1, starting transfers between devices, shards(): mixed = lax.all_to_all(mixed, FAR, 0, 0, tiled=True)  10.9 us
    all_to_all x1, waiting for transfers between devices, shards(): lax.all_to_all(output.reshape(near, slots, cols), NEAR, 0, 0, tiled=True)  10.9 us
  transfers between devices with their start and end apart: 14, of which 9 were waited for; matrix products, arithmetic and copies ran while one was open for 4% of the time, Pallas kernels for 1%

profile of v1, /device:TPU:33, one launch (start us, length us, event | category | flops | bytes accessed | tf_op | source)
XLA Modules:
  0.0 181.9 jit_solution(3069826520910043295)
XLA Ops:
  0.7 4.2 %all-to-all-start = ((bf16[4,896,256]{2,1,0:T(8,128)(2,1)}), bf16[4,896,256]{2,1,0:T(8,128)(2,1)S(1)}, u32[]{:S(2)}, u32[]{:S(2)}) async-start(bf16[4,896,256]{2,1,0:T(8,128)(2,1)} %bitcast.50), calls=%async_computation | async-start | bytes 3670016 | tf_op jit(solution)/shard_map/all_to_all | solution.py:284
  5.2 23.7 %all_gather.3.packed_ref = bf16[128,1024]{1,0:T(8,128)(2,1)S(1)} all-gather(bf16[32,1024]{1,0:T(8,128)(2,1)S(1)} %concatenate.15), channel_id=1, replica_groups=mesh['zh'=4,'zl'=4,'y'=4,'c'=2,'tp'=4] {'zh'}, dimensions={0}, use_global_device_ids=true | all-gather | bytes 327680 | tf_op jit(solution)/shard_map/all_gather | solution.py:288
  28.9 1.4 placed_rows.1
  30.3 9.5 %all-to-all-start.1 = ((bf16[32,16,896]{2,1,0:T(8,128)(2,1)}), bf16[32,16,896]{2,1,0:T(8,128)(2,1)S(1)}, u32[]{:S(2)}, u32[]{:S(2)}) async-start(bf16[32,16,896]{2,1,0:T(8,128)(2,1)} %bitcast.3), calls=%async_computation.1 | async-start | bytes 1835008 | tf_op jit(solution)/shard_map/all_to_all | solution.py:306
  39.9 1.6 fusion.28
  41.5 0.9 fusion.4
  42.5 3.4 %collective-permute-start = (bf16[192,896]{1,0:T(8,128)(2,1)}, bf16[192,896]{1,0:T(8,128)(2,1)}, u32[]{:S(2)}, u32[]{:S(2)}) collective-permute-start(bf16[192,896]{1,0:T(8,128)(2,1)} %get-tuple-element.58), channel_id=1, source_target_pairs={{0,1},{1,2},{2,3},{3,0},{4,5},{5,6},{6,7},{7,4},{8,9},{9,10},{10,1... | collective-permute-start | bytes 1032200 | tf_op jit(solution)/shard_map/ppermute | solution.py:271
  45.8 3.1 %collective-permute-start.1 = (bf16[192,896]{1,0:T(8,128)(2,1)}, bf16[192,896]{1,0:T(8,128)(2,1)}, u32[]{:S(2)}, u32[]{:S(2)}) collective-permute-start(bf16[192,896]{1,0:T(8,128)(2,1)} %get-tuple-element.57), channel_id=1, source_target_pairs={{0,3},{1,0},{2,1},{3,2},{4,7},{5,4},{6,5},{7,6},{8,11},{9,8},{10,9... | collective-permute-start | bytes 1032200 | tf_op jit(solution)/shard_map/ppermute | solution.py:271
  49.0 1.4 dynamic-slice_bitcast_fusion
  50.5 2.2 %collective-permute-start.2 = (bf16[256,896]{1,0:T(8,128)(2,1)S(1)}, bf16[256,896]{1,0:T(8,128)(2,1)S(1)}, u32[]{:S(2)}, u32[]{:S(2)}) collective-permute-start(bf16[256,896]{1,0:T(8,128)(2,1)S(1)} %get-tuple-element.46), channel_id=1, source_target_pairs={{0,1},{1,2},{2,3},{3,0},{4,5},{5,6},{6,7},{7,4},{8,9},{9,10},{10,1... | collective-permute-start | bytes 1376264 | tf_op jit(solution)/shard_map/ppermute | solution.py:271
  52.6 4.3 %collective-permute-start.3 = (bf16[256,896]{1,0:T(8,128)(2,1)S(1)}, bf16[256,896]{1,0:T(8,128)(2,1)S(1)}, u32[]{:S(2)}, u32[]{:S(2)}) collective-permute-start(bf16[256,896]{1,0:T(8,128)(2,1)S(1)} %get-tuple-element.47), channel_id=1, source_target_pairs={{0,3},{1,0},{2,1},{3,2},{4,7},{5,4},{6,5},{7,6},{8,11},{9,8},{10,9... | collective-permute-start | bytes 1376264 | tf_op jit(solution)/shard_map/ppermute | solution.py:271
  57.0 1.9 %collective-permute-start.4 = (bf16[192,896]{1,0:T(8,128)(2,1)}, bf16[192,896]{1,0:T(8,128)(2,1)S(1)}, u32[]{:S(2)}, u32[]{:S(2)}) collective-permute-start(bf16[192,896]{1,0:T(8,128)(2,1)} %collective-permute-done.q3), channel_id=1, source_target_pairs={{0,1},{1,2},{2,3},{3,0},{4,5},{5,6},{6,7},{7,4},{8,9},{9,10},{10,1... | collective-permute-start | bytes 1032200 | tf_op jit(solution)/shard_map/ppermute | solution.py:271
  58.9 4.6 %collective-permute-start.5 = (bf16[192,896]{1,0:T(8,128)(2,1)}, bf16[192,896]{1,0:T(8,128)(2,1)S(1)}, u32[]{:S(2)}, u32[]{:S(2)}) collective-permute-start(bf16[192,896]{1,0:T(8,128)(2,1)} %collective-permute-done.1.q1), channel_id=1, source_target_pairs={{0,3},{1,0},{2,1},{3,2},{4,7},{5,4},{6,5},{7,6},{8,11},{9,8},{10,9... | collective-permute-start | bytes 1032200 | tf_op jit(solution)/shard_map/ppermute | solution.py:271
  63.5 1.2 collective-permute-done.2.w3
  64.7 0.8 copy-done.5
  65.5 1.5 collective-permute-done.3.w1
  67.0 0.8 copy-done.7
  67.8 4.3 %collective-permute-done.4.q2.w2a = bf16[192,896]{1,0:T(8,128)(2,1)S(1)} collective-permute-done((bf16[192,896]{1,0:T(8,128)(2,1)}, bf16[192,896]{1,0:T(8,128)(2,1)S(1)}, u32[]{:S(2)}, u32[]{:S(2)}) %collective-permute-start.4) | collective-permute-done | bytes 344096 | tf_op jit(solution)/shard_map/ppermute | solution.py:271
  72.1 0.7 copy-done.2
  72.8 1.5 collective-permute-done.5.w2b
  74.3 0.7 copy-done.9
  75.1 2.9 %up_parts.1 = bf16[4,512,256]{2,1,0:T(8,128)(2,1)S(1)} custom-call(bf16[512,896]{1,0:T(8,128)(2,1)S(1)} %bitcast.45, bf16[4,896,256]{2,1,0:T(8,128)(2,1)S(1)} %all-to-all-done.weight_ref), custom_call_target="tpu_custom_call" | custom-call | flops 939524096 | bytes 3801088 | tf_op jit(solution)/shard_map/up_parts/pallas_call | solution.py:189
  78.0 16.3 %all_to_all.30.part_ref = bf16[4,512,256]{2,1,0:T(8,128)(2,1)S(1)} all-to-all(bf16[4,512,256]{2,1,0:T(8,128)(2,1)S(1)} %up_parts.1), channel_id=1, replica_groups=mesh['zh'=4,'zl'=4,'y'=4,'c'=2,'tp'=4] {'tp'}, dimensions={0} | all-to-all | bytes 2097152 | tf_op jit(solution)/shard_map/all_to_all | solution.py:312
  94.2 1.2 hidden_copies.1
  95.4 3.7 %all-to-all-start.3 = ((bf16[4,512,256]{2,1,0:T(8,128)(2,1)}), bf16[4,512,256]{2,1,0:T(8,128)(2,1)S(1)}, u32[]{:S(2)}, u32[]{:S(2)}) async-start(bf16[4,512,256]{2,1,0:T(8,128)(2,1)} %hidden_copies.1), calls=%async_computation.3 | async-start | bytes 2097152 | tf_op jit(solution)/shard_map/all_to_all | solution.py:313
  99.2 2.5 %attend_own.1 = bf16[4,2,32,640]{3,2,1,0:T(8,128)(2,1)S(1)} custom-call(s32[3]{0:T(128)S(1)} %pad_add_fusion.place_ref, bf16[64,576]{1,0:T(8,128)(2,1)S(1)} %bitcast.48, bf16[192,896]{1,0:T(8,128)(2,1)} %collective-permute-done.1.q1, bf16[192,896]{1,0:T(8,128)(2,1)S(1)} %copy-done.3, bf16[192,896]{1,0:T(8,128)(2,1)} %collective-permute-done.q3, ...), custom_call_target="tpu_custom_call" | custom-call | flops 150994944 | bytes 917504 | tf_op jit(solution)/shard_map/attend_own/pallas_call | solution.py:70
  101.7 8.9 %all-to-all-done.3.hidden_ref = bf16[4,512,256]{2,1,0:T(8,128)(2,1)S(1)} async-done(((bf16[4,512,256]{2,1,0:T(8,128)(2,1)}), bf16[4,512,256]{2,1,0:T(8,128)(2,1)S(1)}, u32[]{:S(2)}, u32[]{:S(2)}) %all-to-all-start.3) | async-done | bytes 1048608 | tf_op jit(solution)/shard_map/all_to_all | solution.py:313
  110.7 1.0 copy-done.6
  111.7 1.0 copy-done.8
  112.7 2.2 %down_rows.1 = bf16[512,896]{1,0:T(8,128)(2,1)} custom-call(s32[1]{0:T(128)} %bitcast.x_ref, bf16[4,512,256]{2,1,0:T(8,128)(2,1)S(1)} %all-to-all-done.3.hidden_ref, bf16[256,896]{1,0:T(8,128)(2,1)S(1)} %get-tuple-element.45.w0, bf16[256,896]{1,0:T(8,128)(2,1)S(1)} %copy-done.8, bf16[192,896]{1,0:T(8,128)(2,1)S(1)} %copy-done.3, ...), custom_call_target="tpu_custom_call" | custom-call | flops 939524096 | bytes 3801088 | tf_op jit(solution)/shard_map/down_rows/pallas_call | solution.py:258
  115.0 11.8 %all-to-all-start.4 = ((bf16[32,16,896]{2,1,0:T(8,128)(2,1)}), bf16[32,16,896]{2,1,0:T(8,128)(2,1)S(1)}, u32[]{:S(2)}, u32[]{:S(2)}) async-start(bf16[32,16,896]{2,1,0:T(8,128)(2,1)} %bitcast.13), calls=%async_computation.4 | async-start | bytes 1835008 | tf_op jit(solution)/shard_map/all_to_all | solution.py:322
  126.9 1.0 slice_convert_fusion
  128.2 0.2 fusion
  128.5 2.2 %collective-permute-start.6 = (bf16[2,32,640]{2,1,0:T(8,128)(2,1)S(1)}, bf16[2,32,640]{2,1,0:T(8,128)(2,1)S(1)}, u32[]{:S(2)}, u32[]{:S(2)}) collective-permute-start(bf16[2,32,640]{2,1,0:T(8,128)(2,1)S(1)} %get-tuple-element.52), channel_id=1, source_target_pairs={{0,1},{1,2},{2,3},{3,0},{4,5},{5,6},{6,7},{7,4},{8,9},{9,10},{10,1... | collective-permute-start | bytes 245768 | tf_op jit(solution)/shard_map/ppermute | solution.py:271
  130.7 3.7 %collective-permute-start.7 = (bf16[2,32,640]{2,1,0:T(8,128)(2,1)S(1)}, bf16[2,32,640]{2,1,0:T(8,128)(2,1)S(1)}, u32[]{:S(2)}, u32[]{:S(2)}) collective-permute-start(bf16[2,32,640]{2,1,0:T(8,128)(2,1)S(1)} %get-tuple-element.51), channel_id=1, source_target_pairs={{0,2},{1,3},{2,0},{3,1},{4,6},{5,7},{6,4},{7,5},{8,10},{9,11},{10,... | collective-permute-start | bytes 245768 | tf_op jit(solution)/shard_map/ppermute | solution.py:271
  134.4 2.5 %collective-permute-start.8 = (bf16[2,32,640]{2,1,0:T(8,128)(2,1)S(1)}, bf16[2,32,640]{2,1,0:T(8,128)(2,1)S(1)}, u32[]{:S(2)}, u32[]{:S(2)}) collective-permute-start(bf16[2,32,640]{2,1,0:T(8,128)(2,1)S(1)} %get-tuple-element.50), channel_id=1, source_target_pairs={{0,3},{1,0},{2,1},{3,2},{4,7},{5,4},{6,5},{7,6},{8,11},{9,8},{10,9... | collective-permute-start | bytes 245768 | tf_op jit(solution)/shard_map/ppermute | solution.py:271
  137.0 0.1 fusion.10
  137.2 0.2 collective-permute-done.7
  137.4 2.5 %collective-permute-done.8 = bf16[2,32,640]{2,1,0:T(8,128)(2,1)S(1)} collective-permute-done((bf16[2,32,640]{2,1,0:T(8,128)(2,1)S(1)}, bf16[2,32,640]{2,1,0:T(8,128)(2,1)S(1)}, u32[]{:S(2)}, u32[]{:S(2)}) %collective-permute-start.8) | collective-permute-done | bytes 81952 | tf_op jit(solution)/shard_map/ppermute | solution.py:271
  139.9 10.9 %all-to-all-done.4 = bf16[32,16,896]{2,1,0:T(8,128)(2,1)S(1)} async-done(((bf16[32,16,896]{2,1,0:T(8,128)(2,1)}), bf16[32,16,896]{2,1,0:T(8,128)(2,1)S(1)}, u32[]{:S(2)}, u32[]{:S(2)}) %all-to-all-start.4) | async-done | bytes 917536 | tf_op jit(solution)/shard_map/all_to_all | solution.py:322
  150.8 0.5 fusion.5
  151.3 0.7 fusion.2
  152.0 10.9 %all-to-all-start.5 = ((bf16[4,32,896]{2,1,0:T(8,128)(2,1)}), bf16[4,32,896]{2,1,0:T(8,128)(2,1)S(1)}, u32[]{:S(2)}, u32[]{:S(2)}) async-start(bf16[4,32,896]{2,1,0:T(8,128)(2,1)} %bitcast.22), calls=%async_computation.5 | async-start | bytes 458752 | tf_op jit(solution)/shard_map/all_to_all | solution.py:326
  162.9 0.2 add_add_fusion
  163.2 0.1 divide_reduce_fusion.3
  163.3 0.8 add_convert_fusion
  164.1 17.2 %all-to-all-done.5 = bf16[4,32,896]{2,1,0:T(8,128)(2,1)S(1)} async-done(((bf16[4,32,896]{2,1,0:T(8,128)(2,1)}), bf16[4,32,896]{2,1,0:T(8,128)(2,1)S(1)}, u32[]{:S(2)}, u32[]{:S(2)}) %all-to-all-start.5) | async-done | bytes 229408 | tf_op jit(solution)/shard_map/all_to_all | solution.py:326
  181.3 0.7 reduce_sum.42
  (54 shorter events, 1.1 us)
Async XLA Ops:
  0.6 4.4 %copy-start = (bf16[32,3584]{1,0:T(8,128)(2,1)S(1)}, bf16[32,3584]{1,0:T(8,128)(2,1)}, u32[]{:S(2)}) copy-start(bf16[32,3584]{1,0:T(8,128)(2,1)} %param.11) | copy-start | bytes 688132
  0.6 4.2 %copy-start.12 = (f32[32,8]{0,1:T(8,128)S(1)}, f32[32,8]{0,1:T(8,128)}, u32[]{:S(2)}) copy-start(f32[32,8]{0,1:T(8,128)} %param.13) | copy-start | bytes 3076
  0.7 4.3 %copy-start.13 = (s32[32,8]{0,1:T(8,128)S(1)}, s32[32,8]{0,1:T(8,128)}, u32[]{:S(2)}) copy-start(s32[32,8]{0,1:T(8,128)} %param.12) | copy-start | bytes 3076
  0.7 28.2 %all-to-all-start = ((bf16[4,896,256]{2,1,0:T(8,128)(2,1)}), bf16[4,896,256]{2,1,0:T(8,128)(2,1)S(1)}, u32[]{:S(2)}, u32[]{:S(2)}) async-start(bf16[4,896,256]{2,1,0:T(8,128)(2,1)} %bitcast.50), calls=%async_computation | async-start | bytes 3670016 | tf_op jit(solution)/shard_map/all_to_all | solution.py:284
  28.9 1.4 copy-start.1
  30.3 44.8 %all-to-all-start.1 = ((bf16[32,16,896]{2,1,0:T(8,128)(2,1)}), bf16[32,16,896]{2,1,0:T(8,128)(2,1)S(1)}, u32[]{:S(2)}, u32[]{:S(2)}) async-start(bf16[32,16,896]{2,1,0:T(8,128)(2,1)} %bitcast.3), calls=%async_computation.1 | async-start | bytes 1835008 | tf_op jit(solution)/shard_map/all_to_all | solution.py:306
  39.9 1.7 copy-start.11
  42.5 14.5 %collective-permute-start = (bf16[192,896]{1,0:T(8,128)(2,1)}, bf16[192,896]{1,0:T(8,128)(2,1)}, u32[]{:S(2)}, u32[]{:S(2)}) collective-permute-start(bf16[192,896]{1,0:T(8,128)(2,1)} %get-tuple-element.58), channel_id=1, source_target_pairs={{0,1},{1,2},{2,3},{3,0},{4,5},{5,6},{6,7},{7,4},{8,9},{9,10},{10,1... | collective-permute-start | bytes 1032200 | tf_op jit(solution)/shard_map/ppermute | solution.py:271
  45.8 13.1 %collective-permute-start.1 = (bf16[192,896]{1,0:T(8,128)(2,1)}, bf16[192,896]{1,0:T(8,128)(2,1)}, u32[]{:S(2)}, u32[]{:S(2)}) collective-permute-start(bf16[192,896]{1,0:T(8,128)(2,1)} %get-tuple-element.57), channel_id=1, source_target_pairs={{0,3},{1,0},{2,1},{3,2},{4,7},{5,4},{6,5},{7,6},{8,11},{9,8},{10,9... | collective-permute-start | bytes 1032200 | tf_op jit(solution)/shard_map/ppermute | solution.py:271
  50.5 14.2 %collective-permute-start.2 = (bf16[256,896]{1,0:T(8,128)(2,1)S(1)}, bf16[256,896]{1,0:T(8,128)(2,1)S(1)}, u32[]{:S(2)}, u32[]{:S(2)}) collective-permute-start(bf16[256,896]{1,0:T(8,128)(2,1)S(1)} %get-tuple-element.46), channel_id=1, source_target_pairs={{0,1},{1,2},{2,3},{3,0},{4,5},{5,6},{6,7},{7,4},{8,9},{9,10},{10,1... | collective-permute-start | bytes 1376264 | tf_op jit(solution)/shard_map/ppermute | solution.py:271
  52.6 14.3 %collective-permute-start.3 = (bf16[256,896]{1,0:T(8,128)(2,1)S(1)}, bf16[256,896]{1,0:T(8,128)(2,1)S(1)}, u32[]{:S(2)}, u32[]{:S(2)}) collective-permute-start(bf16[256,896]{1,0:T(8,128)(2,1)S(1)} %get-tuple-element.47), channel_id=1, source_target_pairs={{0,3},{1,0},{2,1},{3,2},{4,7},{5,4},{6,5},{7,6},{8,11},{9,8},{10,9... | collective-permute-start | bytes 1376264 | tf_op jit(solution)/shard_map/ppermute | solution.py:271
  57.0 15.1 %collective-permute-start.4 = (bf16[192,896]{1,0:T(8,128)(2,1)}, bf16[192,896]{1,0:T(8,128)(2,1)S(1)}, u32[]{:S(2)}, u32[]{:S(2)}) collective-permute-start(bf16[192,896]{1,0:T(8,128)(2,1)} %collective-permute-done.q3), channel_id=1, source_target_pairs={{0,1},{1,2},{2,3},{3,0},{4,5},{5,6},{6,7},{7,4},{8,9},{9,10},{10,1... | collective-permute-start | bytes 1032200 | tf_op jit(solution)/shard_map/ppermute | solution.py:271
  58.9 15.4 %collective-permute-start.5 = (bf16[192,896]{1,0:T(8,128)(2,1)}, bf16[192,896]{1,0:T(8,128)(2,1)S(1)}, u32[]{:S(2)}, u32[]{:S(2)}) collective-permute-start(bf16[192,896]{1,0:T(8,128)(2,1)} %collective-permute-done.1.q1), channel_id=1, source_target_pairs={{0,3},{1,0},{2,1},{3,2},{4,7},{5,4},{6,5},{7,6},{8,11},{9,8},{10,9... | collective-permute-start | bytes 1032200 | tf_op jit(solution)/shard_map/ppermute | solution.py:271
  64.7 0.8 copy-start.5
  67.0 0.8 copy-start.7
  72.1 0.7 copy-start.2
  74.3 0.7 copy-start.9
  94.2 4.9 %copy-start.14 = (s32[2]{0:T(128)S(1)}, s32[2]{0:T(128)}, u32[]{:S(2)}) copy-start(s32[2]{0:T(128)} %param.10) | copy-start | bytes 28
  94.2 5.0 %copy-start.3 = (bf16[192,896]{1,0:T(8,128)(2,1)S(1)}, bf16[192,896]{1,0:T(8,128)(2,1)}, u32[]{:S(2)}) copy-start(bf16[192,896]{1,0:T(8,128)(2,1)} %copy-done.2) | copy-start | bytes 1032196
  94.2 5.0 %copy-start.4 = (bf16[2,256,576]{1,2,0:T(8,128)(2,1)S(1)}, bf16[2,256,576]{1,2,0:T(8,128)(2,1)}, u32[]{:S(2)}) copy-start(bf16[2,256,576]{1,2,0:T(8,128)(2,1)} %param.9) | copy-start | bytes 1769476
  95.4 15.2 %copy-start.10 = (bf16[192,896]{1,0:T(8,128)(2,1)S(1)}, bf16[192,896]{1,0:T(8,128)(2,1)}, u32[]{:S(2)}) copy-start(bf16[192,896]{1,0:T(8,128)(2,1)} %copy-done.9) | copy-start | bytes 1032196
  95.4 15.2 %all-to-all-start.3 = ((bf16[4,512,256]{2,1,0:T(8,128)(2,1)}), bf16[4,512,256]{2,1,0:T(8,128)(2,1)S(1)}, u32[]{:S(2)}, u32[]{:S(2)}) async-start(bf16[4,512,256]{2,1,0:T(8,128)(2,1)} %hidden_copies.1), calls=%async_computation.3 | async-start | bytes 2097152 | tf_op jit(solution)/shard_map/all_to_all | solution.py:313
  110.7 1.0 copy-start.6
  111.7 1.0 copy-start.8
  115.0 35.9 %all-to-all-start.4 = ((bf16[32,16,896]{2,1,0:T(8,128)(2,1)}), bf16[32,16,896]{2,1,0:T(8,128)(2,1)S(1)}, u32[]{:S(2)}, u32[]{:S(2)}) async-start(bf16[32,16,896]{2,1,0:T(8,128)(2,1)} %bitcast.13), calls=%async_computation.4 | async-start | bytes 1835008 | tf_op jit(solution)/shard_map/all_to_all | solution.py:322
  128.5 8.7 %collective-permute-start.6 = (bf16[2,32,640]{2,1,0:T(8,128)(2,1)S(1)}, bf16[2,32,640]{2,1,0:T(8,128)(2,1)S(1)}, u32[]{:S(2)}, u32[]{:S(2)}) collective-permute-start(bf16[2,32,640]{2,1,0:T(8,128)(2,1)S(1)} %get-tuple-element.52), channel_id=1, source_target_pairs={{0,1},{1,2},{2,3},{3,0},{4,5},{5,6},{6,7},{7,4},{8,9},{9,10},{10,1... | collective-permute-start | bytes 245768 | tf_op jit(solution)/shard_map/ppermute | solution.py:271
  130.7 6.7 %collective-permute-start.7 = (bf16[2,32,640]{2,1,0:T(8,128)(2,1)S(1)}, bf16[2,32,640]{2,1,0:T(8,128)(2,1)S(1)}, u32[]{:S(2)}, u32[]{:S(2)}) collective-permute-start(bf16[2,32,640]{2,1,0:T(8,128)(2,1)S(1)} %get-tuple-element.51), channel_id=1, source_target_pairs={{0,2},{1,3},{2,0},{3,1},{4,6},{5,7},{6,4},{7,5},{8,10},{9,11},{10,... | collective-permute-start | bytes 245768 | tf_op jit(solution)/shard_map/ppermute | solution.py:271
  134.4 5.5 %collective-permute-start.8 = (bf16[2,32,640]{2,1,0:T(8,128)(2,1)S(1)}, bf16[2,32,640]{2,1,0:T(8,128)(2,1)S(1)}, u32[]{:S(2)}, u32[]{:S(2)}) collective-permute-start(bf16[2,32,640]{2,1,0:T(8,128)(2,1)S(1)} %get-tuple-element.50), channel_id=1, source_target_pairs={{0,3},{1,0},{2,1},{3,2},{4,7},{5,4},{6,5},{7,6},{8,11},{9,8},{10,9... | collective-permute-start | bytes 245768 | tf_op jit(solution)/shard_map/ppermute | solution.py:271
  152.0 29.3 %all-to-all-start.5 = ((bf16[4,32,896]{2,1,0:T(8,128)(2,1)}), bf16[4,32,896]{2,1,0:T(8,128)(2,1)S(1)}, u32[]{:S(2)}, u32[]{:S(2)}) async-start(bf16[4,32,896]{2,1,0:T(8,128)(2,1)} %bitcast.22), calls=%async_computation.5 | async-start | bytes 458752 | tf_op jit(solution)/shard_map/all_to_all | solution.py:326

commit v2 on v1

--- a/solution.py
+++ b/solution.py
@@ -14,9 +14,9 @@
 ROUTE_SCALE = 2.5
 NEGATIVE = -1e30
 LANES = 128
-VMEM = 32 << 20
+VMEM = 12 << 20
 INSIDE = pl.BlockSpec(memory_space=pltpu.VMEM)
-OUTSIDE = pl.BlockSpec(memory_space=pl.ANY)
+OUTSIDE = pl.BlockSpec(memory_space=pltpu.HBM)
 
 EP = ("zh", "zl", "y", "c")
 NEAR = ("zl", "y", "c")
@@ -32,7 +32,7 @@
 def attend_kernel(place_ref, q0, q1, q2, q3, cache_ref, out_ref):
     r = pl.program_id(0)
     keys = cache_ref[0]
-    asked = [q[:, : keys.shape[0]] for q in (q0, q1, q2, q3)]
+    asked = [q[0] for q in (q0, q1, q2, q3)]
     count = asked[0].shape[0]
     scores = jnp.dot(jnp.concatenate(asked, axis=0), keys, preferred_element_type=jnp.float32) * SCALE
     positions = place_ref[2] + lax.broadcasted_iota(jnp.int32, scores.shape, 1)
@@ -58,22 +58,19 @@
         out_ref[k, 0, :, LATENT:] = stats[k * count : (k + 1) * count]
 
 
-def attend_own(asked, starts, count, cache, cache_lengths, first):
+def attend_own(asked, cache, cache_lengths, first):
     keys = jnp.swapaxes(cache, 1, 2)
+    count = asked[0].shape[1]
     rows, channels, positions = keys.shape
     out = jax.ShapeDtypeStruct((len(asked), rows, count, LATENT + LANES), BF)
     place = jnp.concatenate([cache_lengths, first.reshape(1).astype(jnp.int32)])
-
-    def queries(array, start):
-        return pl.BlockSpec((count, array.shape[1]), lambda r, place: (start // count + r, 0))
-
     return pl.pallas_call(
         attend_kernel,
         out_shape=out,
         grid_spec=pltpu.PrefetchScalarGridSpec(
             num_scalar_prefetch=1,
             grid=(rows,),
-            in_specs=[queries(a, i) for a, i in zip(asked, starts)]
+            in_specs=[pl.BlockSpec((1, count, channels), lambda r, place: (r, 0, 0))] * len(asked)
             + [pl.BlockSpec((1, channels, positions), lambda r, place: (r, 0, 0))],
             out_specs=pl.BlockSpec((len(asked), 1, count, LATENT + LANES), lambda r, place: (0, r, 0, 0)),
         ),
@@ -172,14 +169,9 @@
     return jnp.concatenate([c_high, c_low], axis=0)
 
 
-def up_kernel(rows_ref, weight_ref, out_ref, held, sems):
-    copies = []
+def up_kernel(rows_ref, weight_ref, out_ref):
     for j in range(weight_ref.shape[0]):
-        held[j] = jnp.dot(rows_ref[...], weight_ref[j], preferred_element_type=jnp.float32).astype(BF)
-        copies.append(pltpu.make_async_copy(held.at[j], out_ref.at[j], sems.at[j]))
-        copies[-1].start()
-    for copy in copies:
-        copy.wait()
+        out_ref[j] = jnp.dot(rows_ref[...], weight_ref[j], preferred_element_type=jnp.float32).astype(BF)
 
 
 def up_parts(rows, weight):
@@ -190,29 +182,24 @@
         up_kernel,
         out_shape=out,
         in_specs=[INSIDE, INSIDE],
-        out_specs=OUTSIDE,
-        scratch_shapes=[pltpu.VMEM(out.shape, BF), pltpu.SemaphoreType.DMA((groups,))],
+        out_specs=INSIDE,
         compiler_params=pltpu.CompilerParams(vmem_limit_bytes=VMEM),
         cost_estimate=cost(2 * count * depth * width * groups, rows, weight, out),
         name="up_parts",
     )(rows, weight)
 
 
-def hidden_kernel(part_ref, out_ref, held, sems):
+def hidden_kernel(part_ref, out_ref):
     groups, count, _ = part_ref.shape
-    step = count // sems.shape[0]
-    copies = []
-    for i in range(sems.shape[0]):
+    step = count // 4
+    for i in range(4):
         rows = pl.ds(i * step, step)
         value = part_ref[0, rows].astype(jnp.float32)
         for j in range(1, groups):
             value = value + part_ref[j, rows].astype(jnp.float32)
-        held[rows] = (value / (1.0 + jnp.exp(-value))).astype(BF)
+        value = (value / (1.0 + jnp.exp(-value))).astype(BF)
         for j in range(groups):
-            copies.append(pltpu.make_async_copy(held.at[rows], out_ref.at[j, rows], sems.at[i, j]))
-            copies[-1].start()
-    for copy in copies:
-        copy.wait()
+            out_ref[j, rows] = value
 
 
 def hidden_copies(part):
@@ -220,18 +207,23 @@
         hidden_kernel,
         out_shape=jax.ShapeDtypeStruct(part.shape, BF),
         in_specs=[INSIDE],
-        out_specs=OUTSIDE,
-        scratch_shapes=[pltpu.VMEM(part.shape[1:], BF), pltpu.SemaphoreType.DMA((2, part.shape[0]))],
+        out_specs=INSIDE,
         compiler_params=pltpu.CompilerParams(vmem_limit_bytes=VMEM),
         cost_estimate=cost(10 * part.size, part, part),
         name="hidden_copies",
     )(part)
 
 
-def down_kernel(x_ref, hidden_ref, w0, w1, w2a, w2b, w3, out_ref, held, sems):
+def columns_at(weight_ref, place, cols):
+    return weight_ref.at[:, pl.ds(pl.multiple_of(place * cols, LANES), cols)]
+
+
+def down_kernel(x_ref, hidden_ref, weight_ref, w1, w2, w3, out_ref, own, held, sems, own_sem):
     groups = hidden_ref.shape[0]
     step = held.shape[0] // sems.shape[0]
     place = [lax.rem(x_ref[0] + k, groups) for k in range(groups)]
+    fetch = pltpu.make_async_copy(columns_at(weight_ref, x_ref[0], own.shape[1]), own, own_sem)
+    fetch.start()
     copies = []
 
     def dot(left, right):
@@ -239,13 +231,12 @@
 
     for i in range(sems.shape[0]):
         rows = pl.ds(i * step, step)
-        total = dot(hidden_ref[place[0], rows], w0[...])
-        total = total + dot(hidden_ref[place[1], rows], w1[...])
+        total = dot(hidden_ref[place[1], rows], w1[...])
+        total = total + dot(hidden_ref[place[2], rows], w2[...])
         total = total + dot(hidden_ref[place[3], rows], w3[...])
-        far = hidden_ref[place[2], rows]
-        depth = w0.shape[0] // 2
-        total = total + dot(far[:, :depth], w2a[:depth, :])
-        total = total + dot(far[:, depth:], w2b[:depth, :])
+        if i == 0:
+            fetch.wait()
+        total = total + dot(hidden_ref[place[0], rows], own[...])
         held[rows] = total.astype(BF)
         copies.append(pltpu.make_async_copy(held.at[rows], out_ref.at[rows], sems.at[i]))
         copies[-1].start()
@@ -253,18 +244,24 @@
         copy.wait()
 
 
-def down_rows(x, hidden, own, after, far_low, far_high, before):
+def down_rows(x, hidden, weight, after, far, before):
+    own = jax.ShapeDtypeStruct(after.shape, BF)
     out = jax.ShapeDtypeStruct((hidden.shape[1], own.shape[1]), BF)
     return pl.pallas_call(
         down_kernel,
         out_shape=out,
-        in_specs=[pl.BlockSpec(memory_space=pltpu.SMEM)] + [INSIDE] * 6,
+        in_specs=[pl.BlockSpec(memory_space=pltpu.SMEM), INSIDE, OUTSIDE] + [INSIDE] * 3,
         out_specs=OUTSIDE,
-        scratch_shapes=[pltpu.VMEM(out.shape, BF), pltpu.SemaphoreType.DMA((4,))],
+        scratch_shapes=[
+            pltpu.VMEM(own.shape, BF),
+            pltpu.VMEM(out.shape, BF),
+            pltpu.SemaphoreType.DMA((2,)),
+            pltpu.SemaphoreType.DMA(()),
+        ],
         compiler_params=pltpu.CompilerParams(vmem_limit_bytes=VMEM),
         cost_estimate=cost(2 * hidden.size * own.shape[1], hidden, own, own, own, own, out),
         name="down_rows",
-    )(x.reshape(1), hidden, own, after, far_low, far_high, before)
+    )(x.reshape(1), hidden, weight, after, far, before)
 
 
 def shift(array, by, tp):
@@ -278,8 +275,8 @@
     cols = width // tp
     group = up_weight.shape[2]
     near = lax.axis_size(NEAR)
-    far = lax.axis_size(FAR)
-    slots = far * CAP
+    away = lax.axis_size(FAR)
+    slots = away * CAP
 
     up = lax.all_to_all(up_weight[0].reshape(tp, cols, group), "tp", 0, 0, tiled=True)
 
@@ -291,38 +288,28 @@
     outgoing = placed_rows(first, packed, rows, near, slots)
 
     weight = down_weight[0]
-    half = group // 2
-    held = queries.reshape(-1, queries.shape[2])
-    ask = jnp.pad(held, ((0, 0), (0, cols - held.shape[1])))
-
-    def columns_for(k, low, high):
-        return lax.dynamic_slice_in_dim(weight[low:high], (x + k) % tp * cols, cols, 1)
-
-    right = shift(jnp.concatenate([columns_for(2, 0, half), ask], axis=0), 1, tp)
-    left = shift(jnp.concatenate([columns_for(2, half, group), ask], axis=0), tp - 1, tp)
-    before = shift(columns_for(1, 0, group), 1, tp)
-    after = shift(columns_for(tp - 1, 0, group), tp - 1, tp)
-    far_right, far_left = shift(right, 1, tp), shift(left, tp - 1, tp)
+    far, before, after = (
+        shift(lax.dynamic_slice_in_dim(weight, (x + k) % tp * cols, cols, 1), k, tp) for k in (2, 1, tp - 1)
+    )
     received = lax.all_to_all(outgoing.reshape(near, slots, cols), NEAR, 0, 0, tiled=True)
-    received, right, left, before, after, far_right, far_left = lax.optimization_barrier(
-        (received.reshape(near * slots, cols), right, left, before, after, far_right, far_left)
-    )
-    take = shares(packed[:, cols:], rows, first, near, far)
+    received, far, before, after = lax.optimization_barrier(
+        (received.reshape(near * slots, cols), far, before, after)
+    )
+    take = shares(packed[:, cols:], rows, first, near, away)
 
     part = lax.all_to_all(up_parts(received, up), "tp", 0, 0, tiled=True)
     hidden = lax.all_to_all(hidden_copies(part), "tp", 0, 0, tiled=True)
-
-    asked, starts = [held, left, far_right, right], [0, half, half, half]
-    first = x * latent_cache.shape[1]
-    own = attend_own(asked, starts, queries.shape[1], latent_cache, cache_lengths, first)
-    hidden, own = lax.optimization_barrier((hidden, own))
-    shared = [own[0]] + [shift(own[k], k, tp) for k in range(1, tp)]
-    output = down_rows(x, hidden, columns_for(0, 0, group), after, far_right, far_left, before)
+    output = down_rows(x, hidden, weight, after, far, before)
 
     returned = lax.all_to_all(output.reshape(near, slots, cols), NEAR, 0, 0, tiled=True)
-    returned, shared = lax.optimization_barrier((returned, shared))
+
+    asked = [queries] + [shift(queries, k, tp) for k in range(1, tp)]
+    own = attend_own(asked, latent_cache, cache_lengths, x * latent_cache.shape[1])
+    returned, own = lax.optimization_barrier((returned, own))
+    shared = [own[0]] + [shift(own[k], tp - k, tp) for k in range(1, tp)]
+
     mixed = jnp.dot(take, returned.reshape(near * slots, cols), preferred_element_type=jnp.float32)
-    mixed = (mixed[: far * rows] + mixed[far * rows :]).astype(BF).reshape(far, rows, cols)
+    mixed = (mixed[: away * rows] + mixed[away * rows :]).astype(BF).reshape(away, rows, cols)
     mixed = lax.all_to_all(mixed, FAR, 0, 0, tiled=True)
     attention_out = merge(shared)
     expert_mix = jnp.sum(mixed.astype(jnp.float32), axis=0).astype(BF)

time: 183 us -> 172 us (0.940)
  blocking collectives: 40 us -> 57.6 us
  waiting for transfers between devices: 48.3 us -> 35 us
  starting transfers between devices: 68 us -> 62.6 us
  local copies, waits for them, and re-layouts: 8.79 us -> 4.38 us
  Pallas kernels: 10.2 us -> 6.81 us
    all_to_all x0 -> x1, blocking collectives: none -> 15.8 us  [shards(): hidden = lax.all_to_all(hidden_copies(part), 'tp', 0, 0, tiled=True)]
    all_to_all x1, waiting for transfers between devices: 17.2 us -> 5.53 us  [shards(): mixed = lax.all_to_all(mixed, FAR, 0, 0, tiled=True)]
    all_to_all x1 -> x0, waiting for transfers between devices: 8.93 us -> none  [shards(): hidden = lax.all_to_all(hidden_copies(part), 'tp', 0, 0, tiled=True)]
    ppermute x9, waiting for transfers between devices: 11.2 us -> 19.4 us  [shift(): return lax.ppermute(array, 'tp', [(i, (i + by) % tp) for i in range(tp)])]
    all_to_all x1 -> x0, starting transfers between devices: 3.66 us -> none  [shards(): hidden = lax.all_to_all(hidden_copies(part), 'tp', 0, 0, tiled=True)]
    unnamed x31 -> x27, local copies, waits for them, and re-layouts: 5.21 us -> 2.47 us
    all_to_all x1, blocking collectives: 16.3 us -> 18.2 us  [shards(): part = lax.all_to_all(up_parts(received, up), 'tp', 0, 0, tiled=True)]
  transfers between devices with their start and end apart: 14 -> 13, of which waited for: 9 -> 8; matrix products, arithmetic and copies ran while one was open for 4% -> 2% of each run, Pallas kernels for 1% -> 1%
where the time goes in v2:
time: 172 us; the launch traced here: 171 us
  starting transfers between devices  62.6 us (36%)
  blocking collectives  57.6 us (33%)
  waiting for transfers between devices  35 us (20%)
  Pallas kernels  6.81 us (4%)
  local copies, waits for them, and re-layouts  4.38 us (3%)
  other arithmetic  3.19 us (2%)
    ppermute x9, starting transfers between devices, shift(): return lax.ppermute(array, 'tp', [(i, (i + by) % tp) for i in range(tp)])  28.2 us
    all_gather x1, blocking collectives, shards(): packed = lax.all_gather(packed, FAR, axis=0, tiled=True)  23.7 us
    ppermute x9, waiting for transfers between devices, shift(): return lax.ppermute(array, 'tp', [(i, (i + by) % tp) for i in range(tp)])  19.4 us
    all_to_all x1, blocking collectives, shards(): part = lax.all_to_all(up_parts(received, up), 'tp', 0, 0, tiled=True)  18.2 us
    all_to_all x1, blocking collectives, shards(): hidden = lax.all_to_all(hidden_copies(part), 'tp', 0, 0, tiled=True)  15.8 us
    all_to_all x1, starting transfers between devices, shards(): mixed = lax.all_to_all(mixed, FAR, 0, 0, tiled=True)  10.4 us
    all_to_all x1, starting transfers between devices, shards(): lax.all_to_all(output.reshape(near, slots, cols), NEAR, 0, 0, tiled=True)  10.4 us
    all_to_all x1, waiting for transfers between devices, shards(): lax.all_to_all(output.reshape(near, slots, cols), NEAR, 0, 0, tiled=True)  10.1 us
  transfers between devices with their start and end apart: 13, of which 8 were waited for; matrix products, arithmetic and copies ran while one was open for 2% of the time, Pallas kernels for 1%

profile of v2, /device:TPU:33, one launch (start us, length us, event | category | flops | bytes accessed | tf_op | source)
XLA Modules:
  0.0 171.3 jit_solution(13887885424804794703)
XLA Ops:
  0.7 4.2 %all-to-all-start = ((bf16[4,896,256]{2,1,0:T(8,128)(2,1)}), bf16[4,896,256]{2,1,0:T(8,128)(2,1)S(1)}, u32[]{:S(2)}, u32[]{:S(2)}) async-start(bf16[4,896,256]{2,1,0:T(8,128)(2,1)} %bitcast.45), calls=%async_computation | async-start | bytes 3670016 | tf_op jit(solution)/shard_map/all_to_all | solution.py:281
  4.9 0.1 copy.22
  5.0 0.1 fusion.19
  5.1 0.1 concatenate.9
  5.2 23.7 %all_gather.3.packed_ref = bf16[128,1024]{1,0:T(8,128)(2,1)S(1)} all-gather(bf16[32,1024]{1,0:T(8,128)(2,1)S(1)} %concatenate.9), channel_id=1, replica_groups=mesh['zh'=4,'zl'=4,'y'=4,'c'=2,'tp'=4] {'zh'}, dimensions={0}, use_global_device_ids=true | all-gather | bytes 327680 | tf_op jit(solution)/shard_map/all_gather | solution.py:285
  28.9 1.4 placed_rows.1
  30.3 9.5 %all-to-all-start.1 = ((bf16[32,16,896]{2,1,0:T(8,128)(2,1)}), bf16[32,16,896]{2,1,0:T(8,128)(2,1)S(1)}, u32[]{:S(2)}, u32[]{:S(2)}) async-start(bf16[32,16,896]{2,1,0:T(8,128)(2,1)} %bitcast.3), calls=%async_computation.1 | async-start | bytes 1835008 | tf_op jit(solution)/shard_map/all_to_all | solution.py:294
  39.9 1.4 dynamic-slice_bitcast_fusion
  41.3 4.9 %collective-permute-start = (bf16[256,896]{1,0:T(8,128)(2,1)S(1)}, bf16[256,896]{1,0:T(8,128)(2,1)S(1)}, u32[]{:S(2)}, u32[]{:S(2)}) collective-permute-start(bf16[256,896]{1,0:T(8,128)(2,1)S(1)} %get-tuple-element.31), channel_id=1, source_target_pairs={{0,2},{1,3},{2,0},{3,1},{4,6},{5,7},{6,4},{7,5},{8,10},{9,11},{10,... | collective-permute-start | bytes 1376264 | tf_op jit(solution)/shard_map/ppermute | solution.py:268
  46.2 2.2 %collective-permute-start.1 = (bf16[256,896]{1,0:T(8,128)(2,1)S(1)}, bf16[256,896]{1,0:T(8,128)(2,1)S(1)}, u32[]{:S(2)}, u32[]{:S(2)}) collective-permute-start(bf16[256,896]{1,0:T(8,128)(2,1)S(1)} %get-tuple-element.30), channel_id=1, source_target_pairs={{0,1},{1,2},{2,3},{3,0},{4,5},{5,6},{6,7},{7,4},{8,9},{9,10},{10,1... | collective-permute-start | bytes 1376264 | tf_op jit(solution)/shard_map/ppermute | solution.py:268
  48.4 4.3 %collective-permute-start.2 = (bf16[256,896]{1,0:T(8,128)(2,1)S(1)}, bf16[256,896]{1,0:T(8,128)(2,1)S(1)}, u32[]{:S(2)}, u32[]{:S(2)}) collective-permute-start(bf16[256,896]{1,0:T(8,128)(2,1)S(1)} %get-tuple-element.29), channel_id=1, source_target_pairs={{0,3},{1,0},{2,1},{3,2},{4,7},{5,4},{6,5},{7,6},{8,11},{9,8},{10,9... | collective-permute-start | bytes 1376264 | tf_op jit(solution)/shard_map/ppermute | solution.py:268
  52.7 3.8 %collective-permute-done.w2 = bf16[256,896]{1,0:T(8,128)(2,1)S(1)} collective-permute-done((bf16[256,896]{1,0:T(8,128)(2,1)S(1)}, bf16[256,896]{1,0:T(8,128)(2,1)S(1)}, u32[]{:S(2)}, u32[]{:S(2)}) %collective-permute-start) | collective-permute-done | bytes 458784 | tf_op jit(solution)/shard_map/ppermute | solution.py:268
  56.5 0.8 copy-done.3
  57.2 9.7 %collective-permute-done.1.w3 = bf16[256,896]{1,0:T(8,128)(2,1)S(1)} collective-permute-done((bf16[256,896]{1,0:T(8,128)(2,1)S(1)}, bf16[256,896]{1,0:T(8,128)(2,1)S(1)}, u32[]{:S(2)}, u32[]{:S(2)}) %collective-permute-start.1) | collective-permute-done | bytes 458784 | tf_op jit(solution)/shard_map/ppermute | solution.py:268
  67.0 0.8 copy-done.5
  67.8 0.8 copy-done.7
  68.5 1.2 up_parts.1
  69.8 18.2 %all_to_all.30.part_ref = bf16[4,512,256]{2,1,0:T(8,128)(2,1)S(1)} all-to-all(bf16[4,512,256]{2,1,0:T(8,128)(2,1)S(1)} %up_parts.1), channel_id=1, replica_groups=mesh['zh'=4,'zl'=4,'y'=4,'c'=2,'tp'=4] {'tp'}, dimensions={0} | all-to-all | bytes 2097152 | tf_op jit(solution)/shard_map/all_to_all | solution.py:300
  88.0 0.2 hidden_copies.1
  88.2 15.8 %all_to_all.31.hidden_ref = bf16[4,512,256]{2,1,0:T(8,128)(2,1)S(1)} all-to-all(bf16[4,512,256]{2,1,0:T(8,128)(2,1)S(1)} %hidden_copies.1), channel_id=1, replica_groups=mesh['zh'=4,'zl'=4,'y'=4,'c'=2,'tp'=4] {'tp'}, dimensions={0} | all-to-all | bytes 2097152 | tf_op jit(solution)/shard_map/all_to_all | solution.py:301
  104.0 2.3 %down_rows.1 = bf16[512,896]{1,0:T(8,128)(2,1)} custom-call(s32[1]{0:T(128)} %bitcast.x_ref, bf16[4,512,256]{2,1,0:T(8,128)(2,1)S(1)} %all_to_all.31.hidden_ref, bf16[256,3584]{1,0:T(8,128)(2,1)S(1)} %bitcast.41, bf16[256,896]{1,0:T(8,128)(2,1)S(1)} %copy-done.8, bf16[256,896]{1,0:T(8,128)(2,1)S(1)} %copy-done.4, bf16[256,896]{1,0:T(8,128)(2,1)S(1)} %copy-done.6), custom_call_target="tpu_custom_call" | custom-call | flops 939524096 | bytes 3801088 | tf_op jit(solution)/shard_map/down_rows/pallas_call | solution.py:250
  106.3 10.4 %all-to-all-start.4 = ((bf16[32,16,896]{2,1,0:T(8,128)(2,1)}), bf16[32,16,896]{2,1,0:T(8,128)(2,1)S(1)}, u32[]{:S(2)}, u32[]{:S(2)}) async-start(bf16[32,16,896]{2,1,0:T(8,128)(2,1)} %bitcast.9), calls=%async_computation.4 | async-start | bytes 1835008 | tf_op jit(solution)/shard_map/all_to_all | solution.py:304
  116.7 2.2 %collective-permute-start.3 = (bf16[2,32,576]{2,1,0:T(8,128)(2,1)S(1)}, bf16[2,32,576]{2,1,0:T(8,128)(2,1)S(1)}, u32[]{:S(2)}, u32[]{:S(2)}) collective-permute-start(bf16[2,32,576]{2,1,0:T(8,128)(2,1)S(1)} %copy-done.9), channel_id=1, source_target_pairs={{0,1},{1,2},{2,3},{3,0},{4,5},{5,6},{6,7},{7,4},{8,9},{9,10},{10,1... | collective-permute-start | bytes 221192 | tf_op jit(solution)/shard_map/ppermute | solution.py:268
  118.9 3.7 %collective-permute-start.4 = (bf16[2,32,576]{2,1,0:T(8,128)(2,1)S(1)}, bf16[2,32,576]{2,1,0:T(8,128)(2,1)S(1)}, u32[]{:S(2)}, u32[]{:S(2)}) collective-permute-start(bf16[2,32,576]{2,1,0:T(8,128)(2,1)S(1)} %copy-done.9), channel_id=1, source_target_pairs={{0,2},{1,3},{2,0},{3,1},{4,6},{5,7},{6,4},{7,5},{8,10},{9,11},{10,... | collective-permute-start | bytes 221192 | tf_op jit(solution)/shard_map/ppermute | solution.py:268
  122.6 2.5 %collective-permute-start.5 = (bf16[2,32,576]{2,1,0:T(8,128)(2,1)S(1)}, bf16[2,32,576]{2,1,0:T(8,128)(2,1)S(1)}, u32[]{:S(2)}, u32[]{:S(2)}) collective-permute-start(bf16[2,32,576]{2,1,0:T(8,128)(2,1)S(1)} %copy-done.9), channel_id=1, source_target_pairs={{0,3},{1,0},{2,1},{3,2},{4,7},{5,4},{6,5},{7,6},{8,11},{9,8},{10,9... | collective-permute-start | bytes 221192 | tf_op jit(solution)/shard_map/ppermute | solution.py:268
  125.2 0.1 eq.60
  125.3 0.5 collective-permute-done.4.q2
  125.9 2.2 %collective-permute-done.5.q3 = bf16[2,32,576]{2,1,0:T(8,128)(2,1)S(1)} collective-permute-done((bf16[2,32,576]{2,1,0:T(8,128)(2,1)S(1)}, bf16[2,32,576]{2,1,0:T(8,128)(2,1)S(1)}, u32[]{:S(2)}, u32[]{:S(2)}) %collective-permute-start.5) | collective-permute-done | bytes 73760 | tf_op jit(solution)/shard_map/ppermute | solution.py:268
  128.1 1.7 attend_own.1
  129.7 0.1 slice_convert_fusion
  130.0 0.1 compare_reduce_fusion
  130.1 0.1 fusion.8
  130.2 0.2 fusion
  130.4 0.2 fusion.7
  130.6 10.1 %all-to-all-done.4 = bf16[32,16,896]{2,1,0:T(8,128)(2,1)S(1)} async-done(((bf16[32,16,896]{2,1,0:T(8,128)(2,1)}), bf16[32,16,896]{2,1,0:T(8,128)(2,1)S(1)}, u32[]{:S(2)}, u32[]{:S(2)}) %all-to-all-start.4) | async-done | bytes 917536 | tf_op jit(solution)/shard_map/all_to_all | solution.py:304
  140.7 0.5 fusion.2
  141.1 0.8 fusion.1
  141.9 10.4 %all-to-all-start.5 = ((bf16[4,32,896]{2,1,0:T(8,128)(2,1)}), bf16[4,32,896]{2,1,0:T(8,128)(2,1)S(1)}, u32[]{:S(2)}, u32[]{:S(2)}) async-start(bf16[4,32,896]{2,1,0:T(8,128)(2,1)} %bitcast.20), calls=%async_computation.5 | async-start | bytes 458752 | tf_op jit(solution)/shard_map/all_to_all | solution.py:313
  152.3 2.2 %collective-permute-start.8 = (bf16[2,32,640]{2,1,0:T(8,128)(2,1)S(1)}, bf16[2,32,640]{2,1,0:T(8,128)(2,1)S(1)}, u32[]{:S(2)}, u32[]{:S(2)}) collective-permute-start(bf16[2,32,640]{2,1,0:T(8,128)(2,1)S(1)} %get-tuple-element.33), channel_id=1, source_target_pairs={{0,1},{1,2},{2,3},{3,0},{4,5},{5,6},{6,7},{7,4},{8,9},{9,10},{10,1... | collective-permute-start | bytes 245768 | tf_op jit(solution)/shard_map/ppermute | solution.py:268
  154.5 3.7 %collective-permute-start.7 = (bf16[2,32,640]{2,1,0:T(8,128)(2,1)S(1)}, bf16[2,32,640]{2,1,0:T(8,128)(2,1)S(1)}, u32[]{:S(2)}, u32[]{:S(2)}) collective-permute-start(bf16[2,32,640]{2,1,0:T(8,128)(2,1)S(1)} %get-tuple-element.34), channel_id=1, source_target_pairs={{0,2},{1,3},{2,0},{3,1},{4,6},{5,7},{6,4},{7,5},{8,10},{9,11},{10,... | collective-permute-start | bytes 245768 | tf_op jit(solution)/shard_map/ppermute | solution.py:268
  158.2 2.6 %collective-permute-start.6 = (bf16[2,32,640]{2,1,0:T(8,128)(2,1)S(1)}, bf16[2,32,640]{2,1,0:T(8,128)(2,1)S(1)}, u32[]{:S(2)}, u32[]{:S(2)}) collective-permute-start(bf16[2,32,640]{2,1,0:T(8,128)(2,1)S(1)} %get-tuple-element.35), channel_id=1, source_target_pairs={{0,3},{1,0},{2,1},{3,2},{4,7},{5,4},{6,5},{7,6},{8,11},{9,8},{10,9... | collective-permute-start | bytes 245768 | tf_op jit(solution)/shard_map/ppermute | solution.py:268
  160.8 1.3 collective-permute-done.7
  162.1 1.9 %collective-permute-done.6 = bf16[2,32,640]{2,1,0:T(8,128)(2,1)S(1)} collective-permute-done((bf16[2,32,640]{2,1,0:T(8,128)(2,1)S(1)}, bf16[2,32,640]{2,1,0:T(8,128)(2,1)S(1)}, u32[]{:S(2)}, u32[]{:S(2)}) %collective-permute-start.6) | collective-permute-done | bytes 81952 | tf_op jit(solution)/shard_map/ppermute | solution.py:268
  164.0 0.2 add_add_fusion
  164.2 0.1 divide_reduce_fusion.3
  164.4 0.8 add_convert_fusion
  165.1 5.5 %all-to-all-done.5 = bf16[4,32,896]{2,1,0:T(8,128)(2,1)S(1)} async-done(((bf16[4,32,896]{2,1,0:T(8,128)(2,1)}), bf16[4,32,896]{2,1,0:T(8,128)(2,1)S(1)}, u32[]{:S(2)}, u32[]{:S(2)}) %all-to-all-start.5) | async-done | bytes 229408 | tf_op jit(solution)/shard_map/all_to_all | solution.py:313
  170.6 0.7 reduce_sum.42
  (46 shorter events, 0.5 us)
Async XLA Ops:
  0.6 4.4 %copy-start = (bf16[32,3584]{1,0:T(8,128)(2,1)S(1)}, bf16[32,3584]{1,0:T(8,128)(2,1)}, u32[]{:S(2)}) copy-start(bf16[32,3584]{1,0:T(8,128)(2,1)} %param.11) | copy-start | bytes 688132
  0.6 4.2 %copy-start.10 = (f32[32,8]{0,1:T(8,128)S(1)}, f32[32,8]{0,1:T(8,128)}, u32[]{:S(2)}) copy-start(f32[32,8]{0,1:T(8,128)} %param.13) | copy-start | bytes 3076
  0.7 4.3 %copy-start.11 = (s32[32,8]{0,1:T(8,128)S(1)}, s32[32,8]{0,1:T(8,128)}, u32[]{:S(2)}) copy-start(s32[32,8]{0,1:T(8,128)} %param.12) | copy-start | bytes 3076
  0.7 28.2 %all-to-all-start = ((bf16[4,896,256]{2,1,0:T(8,128)(2,1)}), bf16[4,896,256]{2,1,0:T(8,128)(2,1)S(1)}, u32[]{:S(2)}, u32[]{:S(2)}) async-start(bf16[4,896,256]{2,1,0:T(8,128)(2,1)} %bitcast.45), calls=%async_computation | async-start | bytes 3670016 | tf_op jit(solution)/shard_map/all_to_all | solution.py:281
  30.3 38.3 %all-to-all-start.1 = ((bf16[32,16,896]{2,1,0:T(8,128)(2,1)}), bf16[32,16,896]{2,1,0:T(8,128)(2,1)S(1)}, u32[]{:S(2)}, u32[]{:S(2)}) async-start(bf16[32,16,896]{2,1,0:T(8,128)(2,1)} %bitcast.3), calls=%async_computation.1 | async-start | bytes 1835008 | tf_op jit(solution)/shard_map/all_to_all | solution.py:294
  41.3 15.2 %collective-permute-start = (bf16[256,896]{1,0:T(8,128)(2,1)S(1)}, bf16[256,896]{1,0:T(8,128)(2,1)S(1)}, u32[]{:S(2)}, u32[]{:S(2)}) collective-permute-start(bf16[256,896]{1,0:T(8,128)(2,1)S(1)} %get-tuple-element.31), channel_id=1, source_target_pairs={{0,2},{1,3},{2,0},{3,1},{4,6},{5,7},{6,4},{7,5},{8,10},{9,11},{10,... | collective-permute-start | bytes 1376264 | tf_op jit(solution)/shard_map/ppermute | solution.py:268
  46.2 20.8 %collective-permute-start.1 = (bf16[256,896]{1,0:T(8,128)(2,1)S(1)}, bf16[256,896]{1,0:T(8,128)(2,1)S(1)}, u32[]{:S(2)}, u32[]{:S(2)}) collective-permute-start(bf16[256,896]{1,0:T(8,128)(2,1)S(1)} %get-tuple-element.30), channel_id=1, source_target_pairs={{0,1},{1,2},{2,3},{3,0},{4,5},{5,6},{6,7},{7,4},{8,9},{9,10},{10,1... | collective-permute-start | bytes 1376264 | tf_op jit(solution)/shard_map/ppermute | solution.py:268
  48.4 19.4 %collective-permute-start.2 = (bf16[256,896]{1,0:T(8,128)(2,1)S(1)}, bf16[256,896]{1,0:T(8,128)(2,1)S(1)}, u32[]{:S(2)}, u32[]{:S(2)}) collective-permute-start(bf16[256,896]{1,0:T(8,128)(2,1)S(1)} %get-tuple-element.29), channel_id=1, source_target_pairs={{0,3},{1,0},{2,1},{3,2},{4,7},{5,4},{6,5},{7,6},{8,11},{9,8},{10,9... | collective-permute-start | bytes 1376264 | tf_op jit(solution)/shard_map/ppermute | solution.py:268
  56.5 0.8 copy-start.3
  67.0 0.8 copy-start.5
  67.8 0.8 copy-start.7
  88.0 16.0 %copy-start.1 = (bf16[1,256,3584]{2,1,0:T(8,128)(2,1)S(1)}, bf16[1,256,3584]{2,1,0:T(8,128)(2,1)}, u32[]{:S(2)}) copy-start(bf16[1,256,3584]{2,1,0:T(8,128)(2,1)} %param.15) | copy-start | bytes 5505028
  88.0 16.0 %copy-start.4 = (bf16[256,896]{1,0:T(8,128)(2,1)S(1)}, bf16[256,896]{1,0:T(8,128)(2,1)}, u32[]{:S(2)}) copy-start(bf16[256,896]{1,0:T(8,128)(2,1)} %copy-done.3) | copy-start | bytes 1376260
  88.0 16.0 %copy-start.6 = (bf16[256,896]{1,0:T(8,128)(2,1)S(1)}, bf16[256,896]{1,0:T(8,128)(2,1)}, u32[]{:S(2)}) copy-start(bf16[256,896]{1,0:T(8,128)(2,1)} %copy-done.5) | copy-start | bytes 1376260
  88.0 16.0 %copy-start.8 = (bf16[256,896]{1,0:T(8,128)(2,1)S(1)}, bf16[256,896]{1,0:T(8,128)(2,1)}, u32[]{:S(2)}) copy-start(bf16[256,896]{1,0:T(8,128)(2,1)} %copy-done.7) | copy-start | bytes 1376260
  106.3 10.4 %copy-start.9 = (bf16[2,32,576]{2,1,0:T(8,128)(2,1)S(1)}, bf16[2,32,576]{2,1,0:T(8,128)(2,1)}, u32[]{:S(2)}) copy-start(bf16[2,32,576]{2,1,0:T(8,128)(2,1)} %q0.1) | copy-start | bytes 221188
  106.3 19.0 %copy-start.12 = (s32[2]{0:T(128)S(1)}, s32[2]{0:T(128)}, u32[]{:S(2)}) copy-start(s32[2]{0:T(128)} %param.10) | copy-start | bytes 28
  106.3 21.8 %copy-start.2 = (bf16[2,256,576]{1,2,0:T(8,128)(2,1)S(1)}, bf16[2,256,576]{1,2,0:T(8,128)(2,1)}, u32[]{:S(2)}) copy-start(bf16[2,256,576]{1,2,0:T(8,128)(2,1)} %param.9) | copy-start | bytes 1769476
  106.3 34.4 %all-to-all-start.4 = ((bf16[32,16,896]{2,1,0:T(8,128)(2,1)}), bf16[32,16,896]{2,1,0:T(8,128)(2,1)S(1)}, u32[]{:S(2)}, u32[]{:S(2)}) async-start(bf16[32,16,896]{2,1,0:T(8,128)(2,1)} %bitcast.9), calls=%async_computation.4 | async-start | bytes 1835008 | tf_op jit(solution)/shard_map/all_to_all | solution.py:304
  116.7 8.6 %collective-permute-start.3 = (bf16[2,32,576]{2,1,0:T(8,128)(2,1)S(1)}, bf16[2,32,576]{2,1,0:T(8,128)(2,1)S(1)}, u32[]{:S(2)}, u32[]{:S(2)}) collective-permute-start(bf16[2,32,576]{2,1,0:T(8,128)(2,1)S(1)} %copy-done.9), channel_id=1, source_target_pairs={{0,1},{1,2},{2,3},{3,0},{4,5},{5,6},{6,7},{7,4},{8,9},{9,10},{10,1... | collective-permute-start | bytes 221192 | tf_op jit(solution)/shard_map/ppermute | solution.py:268
  118.9 7.0 %collective-permute-start.4 = (bf16[2,32,576]{2,1,0:T(8,128)(2,1)S(1)}, bf16[2,32,576]{2,1,0:T(8,128)(2,1)S(1)}, u32[]{:S(2)}, u32[]{:S(2)}) collective-permute-start(bf16[2,32,576]{2,1,0:T(8,128)(2,1)S(1)} %copy-done.9), channel_id=1, source_target_pairs={{0,2},{1,3},{2,0},{3,1},{4,6},{5,7},{6,4},{7,5},{8,10},{9,11},{10,... | collective-permute-start | bytes 221192 | tf_op jit(solution)/shard_map/ppermute | solution.py:268
  122.6 5.5 %collective-permute-start.5 = (bf16[2,32,576]{2,1,0:T(8,128)(2,1)S(1)}, bf16[2,32,576]{2,1,0:T(8,128)(2,1)S(1)}, u32[]{:S(2)}, u32[]{:S(2)}) collective-permute-start(bf16[2,32,576]{2,1,0:T(8,128)(2,1)S(1)} %copy-done.9), channel_id=1, source_target_pairs={{0,3},{1,0},{2,1},{3,2},{4,7},{5,4},{6,5},{7,6},{8,11},{9,8},{10,9... | collective-permute-start | bytes 221192 | tf_op jit(solution)/shard_map/ppermute | solution.py:268
  141.9 28.7 %all-to-all-start.5 = ((bf16[4,32,896]{2,1,0:T(8,128)(2,1)}), bf16[4,32,896]{2,1,0:T(8,128)(2,1)S(1)}, u32[]{:S(2)}, u32[]{:S(2)}) async-start(bf16[4,32,896]{2,1,0:T(8,128)(2,1)} %bitcast.20), calls=%async_computation.5 | async-start | bytes 458752 | tf_op jit(solution)/shard_map/all_to_all | solution.py:313
  152.3 8.5 %collective-permute-start.8 = (bf16[2,32,640]{2,1,0:T(8,128)(2,1)S(1)}, bf16[2,32,640]{2,1,0:T(8,128)(2,1)S(1)}, u32[]{:S(2)}, u32[]{:S(2)}) collective-permute-start(bf16[2,32,640]{2,1,0:T(8,128)(2,1)S(1)} %get-tuple-element.33), channel_id=1, source_target_pairs={{0,1},{1,2},{2,3},{3,0},{4,5},{5,6},{6,7},{7,4},{8,9},{9,10},{10,1... | collective-permute-start | bytes 245768 | tf_op jit(solution)/shard_map/ppermute | solution.py:268
  154.5 7.6 %collective-permute-start.7 = (bf16[2,32,640]{2,1,0:T(8,128)(2,1)S(1)}, bf16[2,32,640]{2,1,0:T(8,128)(2,1)S(1)}, u32[]{:S(2)}, u32[]{:S(2)}) collective-permute-start(bf16[2,32,640]{2,1,0:T(8,128)(2,1)S(1)} %get-tuple-element.34), channel_id=1, source_target_pairs={{0,2},{1,3},{2,0},{3,1},{4,6},{5,7},{6,4},{7,5},{8,10},{9,11},{10,... | collective-permute-start | bytes 245768 | tf_op jit(solution)/shard_map/ppermute | solution.py:268
  158.2 5.8 %collective-permute-start.6 = (bf16[2,32,640]{2,1,0:T(8,128)(2,1)S(1)}, bf16[2,32,640]{2,1,0:T(8,128)(2,1)S(1)}, u32[]{:S(2)}, u32[]{:S(2)}) collective-permute-start(bf16[2,32,640]{2,1,0:T(8,128)(2,1)S(1)} %get-tuple-element.35), channel_id=1, source_target_pairs={{0,3},{1,0},{2,1},{3,2},{4,7},{5,4},{6,5},{7,6},{8,11},{9,8},{10,9... | collective-permute-start | bytes 245768 | tf_op jit(solution)/shard_map/ppermute | solution.py:268

commit v3 on v2

--- a/solution.py
+++ b/solution.py
@@ -170,14 +170,17 @@
 
 
 def up_kernel(rows_ref, weight_ref, out_ref):
+    count = rows_ref.shape[0]
     for j in range(weight_ref.shape[0]):
-        out_ref[j] = jnp.dot(rows_ref[...], weight_ref[j], preferred_element_type=jnp.float32).astype(BF)
+        part = jnp.dot(rows_ref[...], weight_ref[j], preferred_element_type=jnp.float32).astype(BF)
+        for i in range(part.shape[1] // LANES):
+            out_ref[j, i * count : (i + 1) * count] = part[:, i * LANES : (i + 1) * LANES]
 
 
 def up_parts(rows, weight):
     groups, depth, width = weight.shape
     count = rows.shape[0]
-    out = jax.ShapeDtypeStruct((groups, count, width), BF)
+    out = jax.ShapeDtypeStruct((groups, count * width // LANES, LANES), BF)
     return pl.pallas_call(
         up_kernel,
         out_shape=out,
@@ -219,7 +222,7 @@
 
 
 def down_kernel(x_ref, hidden_ref, weight_ref, w1, w2, w3, out_ref, own, held, sems, own_sem):
-    groups = hidden_ref.shape[0]
+    groups, count = hidden_ref.shape[0], held.shape[0]
     step = held.shape[0] // sems.shape[0]
     place = [lax.rem(x_ref[0] + k, groups) for k in range(groups)]
     fetch = pltpu.make_async_copy(columns_at(weight_ref, x_ref[0], own.shape[1]), own, own_sem)
@@ -229,14 +232,18 @@
     def dot(left, right):
         return jnp.dot(left, right, preferred_element_type=jnp.float32)
 
+    def group(j, i):
+        halves = [hidden_ref[j, pl.ds(h * count + i * step, step)] for h in range(hidden_ref.shape[1] // count)]
+        return jnp.concatenate(halves, axis=1)
+
     for i in range(sems.shape[0]):
         rows = pl.ds(i * step, step)
-        total = dot(hidden_ref[place[1], rows], w1[...])
-        total = total + dot(hidden_ref[place[2], rows], w2[...])
-        total = total + dot(hidden_ref[place[3], rows], w3[...])
+        total = dot(group(place[1], i), w1[...])
+        total = total + dot(group(place[2], i), w2[...])
+        total = total + dot(group(place[3], i), w3[...])
         if i == 0:
             fetch.wait()
-        total = total + dot(hidden_ref[place[0], rows], own[...])
+        total = total + dot(group(place[0], i), own[...])
         held[rows] = total.astype(BF)
         copies.append(pltpu.make_async_copy(held.at[rows], out_ref.at[rows], sems.at[i]))
         copies[-1].start()
@@ -246,7 +253,7 @@
 
 def down_rows(x, hidden, weight, after, far, before):
     own = jax.ShapeDtypeStruct(after.shape, BF)
-    out = jax.ShapeDtypeStruct((hidden.shape[1], own.shape[1]), BF)
+    out = jax.ShapeDtypeStruct((hidden.shape[1] * LANES // own.shape[0], own.shape[1]), BF)
     return pl.pallas_call(
         down_kernel,
         out_shape=out,
@@ -262,6 +269,59 @@
         cost_estimate=cost(2 * hidden.size * own.shape[1], hidden, own, own, own, own, out),
         name="down_rows",
     )(x.reshape(1), hidden, weight, after, far, before)
+
+
+def mix_kernel(take_ref, rows_ref, out_ref, held, sem):
+    groups, lines, _ = held.shape
+    total = take_ref.shape[0] // 2
+    count = total // groups
+    mixed = jnp.dot(take_ref[...], rows_ref[...], preferred_element_type=jnp.float32)
+    mixed = (mixed[:total] + mixed[total:]).astype(BF)
+    for j in range(groups):
+        for i in range(lines // count):
+            part = mixed[j * count : (j + 1) * count, i * LANES : (i + 1) * LANES]
+            held[j, i * count : (i + 1) * count] = part
+    copy = pltpu.make_async_copy(held, out_ref, sem)
+    copy.start()
+    copy.wait()
+
+
+def mixed_rows(take, rows, groups):
+    total, cols = take.shape[0] // 2, rows.shape[1]
+    out = jax.ShapeDtypeStruct((groups, total // groups * cols // LANES, LANES), BF)
+    return pl.pallas_call(
+        mix_kernel,
+        out_shape=out,
+        in_specs=[INSIDE, INSIDE],
+        out_specs=OUTSIDE,
+        scratch_shapes=[pltpu.VMEM(out.shape, BF), pltpu.SemaphoreType.DMA(())],
+        compiler_params=pltpu.CompilerParams(vmem_limit_bytes=VMEM),
+        cost_estimate=cost(2 * take.size * cols, take, rows, out),
+        name="mixed_rows",
+    )(take, rows)
+
+
+def sum_kernel(parts_ref, out_ref):
+    count = out_ref.shape[0]
+    for i in range(out_ref.shape[1] // LANES):
+        rows = pl.ds(i * count, count)
+        total = parts_ref[0, rows].astype(jnp.float32)
+        for j in range(1, parts_ref.shape[0]):
+            total = total + parts_ref[j, rows].astype(jnp.float32)
+        out_ref[:, i * LANES : (i + 1) * LANES] = total.astype(BF)
+
+
+def summed(parts, rows, cols):
+    out = jax.ShapeDtypeStruct((rows, cols), BF)
+    return pl.pallas_call(
+        sum_kernel,
+        out_shape=out,
+        in_specs=[INSIDE],
+        out_specs=INSIDE,
+        compiler_params=pltpu.CompilerParams(vmem_limit_bytes=VMEM),
+        cost_estimate=cost(parts.size, parts, out),
+        name="summed",
+    )(parts)
 
 
 def shift(array, by, tp):
@@ -283,14 +343,13 @@
     mine = lax.dynamic_slice_in_dim(moe_tokens, x * cols, cols, 1)
     packed = jnp.concatenate([mine, routing_columns(expert_ids, gate_scores)], axis=1)
     packed = lax.all_gather(packed, FAR, axis=0, tiled=True)
-    packed, up = lax.optimization_barrier((packed, up))
     first = lax.axis_index(FAR) * near
     outgoing = placed_rows(first, packed, rows, near, slots)
 
     weight = down_weight[0]
-    far, before, after = (
-        shift(lax.dynamic_slice_in_dim(weight, (x + k) % tp * cols, cols, 1), k, tp) for k in (2, 1, tp - 1)
-    )
+    cut = [lax.dynamic_slice_in_dim(weight, (x + k) % tp * cols, cols, 1) for k in (2, 1, tp - 1)]
+    outgoing, up, cut = lax.optimization_barrier((outgoing, up, cut))
+    far, before, after = (shift(block, k, tp) for block, k in zip(cut, (2, 1, tp - 1)))
     received = lax.all_to_all(outgoing.reshape(near, slots, cols), NEAR, 0, 0, tiled=True)
     received, far, before, after = lax.optimization_barrier(
         (received.reshape(near * slots, cols), far, before, after)
@@ -308,11 +367,10 @@
     returned, own = lax.optimization_barrier((returned, own))
     shared = [own[0]] + [shift(own[k], tp - k, tp) for k in range(1, tp)]
 
-    mixed = jnp.dot(take, returned.reshape(near * slots, cols), preferred_element_type=jnp.float32)
-    mixed = (mixed[: away * rows] + mixed[away * rows :]).astype(BF).reshape(away, rows, cols)
+    mixed = mixed_rows(take, returned.reshape(near * slots, cols), away)
     mixed = lax.all_to_all(mixed, FAR, 0, 0, tiled=True)
     attention_out = merge(shared)
-    expert_mix = jnp.sum(mixed.astype(jnp.float32), axis=0).astype(BF)
+    expert_mix = summed(mixed, rows, cols)
     return (attention_out, expert_mix)
 
 

time: 172 us -> 169 us (0.983)
  starting transfers between devices: 62.6 us -> 58.7 us
  Pallas kernels: 6.81 us -> 8.56 us
    all_to_all x1, starting transfers between devices: 10.4 us -> 6.34 us  [shards(): mixed = lax.all_to_all(mixed, FAR, 0, 0, tiled=True)]
    pallas_call x0 -> x2, Pallas kernels: none -> 1.79 us  [the longest x1 1.13 us: mixed_rows(): pl.pallas_call(mix_kernel, out_shape=out, in_specs=[INSIDE, INSIDE], out_...]
  transfers between devices with their start and end apart: 13 -> 13, of which waited for: 8 -> 7; matrix products, arithmetic and copies ran while one was open for 2% -> 3% of each run, Pallas kernels for 1% -> 2%
where the time goes in v3:
time: 169 us; the launch traced here: 168 us
  starting transfers between devices  58.7 us (35%)
  blocking collectives  57.6 us (34%)
  waiting for transfers between devices  34.6 us (20%)
  Pallas kernels  8.56 us (5%)
  local copies, waits for them, and re-layouts  5.88 us (3%)
  other arithmetic  1.75 us (1%)
    ppermute x9, starting transfers between devices, shift(): return lax.ppermute(array, 'tp', [(i, (i + by) % tp) for i in range(tp)])  28.4 us
    all_gather x1, blocking collectives, shards(): packed = lax.all_gather(packed, FAR, axis=0, tiled=True)  23.7 us
    ppermute x9, waiting for transfers between devices, shift(): return lax.ppermute(array, 'tp', [(i, (i + by) % tp) for i in range(tp)])  18.3 us
    all_to_all x1, blocking collectives, shards(): part = lax.all_to_all(up_parts(received, up), 'tp', 0, 0, tiled=True)  18.2 us
    all_to_all x1, blocking collectives, shards(): hidden = lax.all_to_all(hidden_copies(part), 'tp', 0, 0, tiled=True)  15.8 us
    all_to_all x1, waiting for transfers between devices, shards(): lax.all_to_all(output.reshape(near, slots, cols), NEAR, 0, 0, tiled=True)  10.8 us
    all_to_all x1, starting transfers between devices, shards(): lax.all_to_all(output.reshape(near, slots, cols), NEAR, 0, 0, tiled=True)  10.4 us
    all_to_all x1, starting transfers between devices, shards(): lax.all_to_all(outgoing.reshape(near, slots, cols), NEAR, 0, 0, tiled=True)  9.52 us
  transfers between devices with their start and end apart: 13, of which 7 were waited for; matrix products, arithmetic and copies ran while one was open for 3% of the time, Pallas kernels for 2%

profile of v3, /device:TPU:33, one launch (start us, length us, event | category | flops | bytes accessed | tf_op | source)
XLA Modules:
  0.0 168.4 jit_solution(8557386388346566343)
XLA Ops:
  0.7 4.2 %all-to-all-start = ((bf16[4,896,256]{2,1,0:T(8,128)(2,1)}), bf16[4,896,256]{2,1,0:T(8,128)(2,1)S(1)}, u32[]{:S(2)}, u32[]{:S(2)}) async-start(bf16[4,896,256]{2,1,0:T(8,128)(2,1)} %bitcast.32), calls=%async_computation | async-start | bytes 3670016 | tf_op jit(solution)/shard_map/all_to_all | solution.py:341
  4.9 0.1 copy.28
  5.0 0.1 fusion.12
  5.1 0.1 concatenate.9
  5.2 23.7 %all_gather.3.packed_ref = bf16[128,1024]{1,0:T(8,128)(2,1)S(1)} all-gather(bf16[32,1024]{1,0:T(8,128)(2,1)S(1)} %concatenate.9), channel_id=1, replica_groups=mesh['zh'=4,'zl'=4,'y'=4,'c'=2,'tp'=4] {'zh'}, dimensions={0}, use_global_device_ids=true | all-gather | bytes 327680 | tf_op jit(solution)/shard_map/all_gather | solution.py:345
  28.9 1.4 placed_rows.1
  30.3 2.5 %dynamic-slice_bitcast_fusion = (bf16[256,896]{1,0:T(8,128)(2,1)}, bf16[256,896]{1,0:T(8,128)(2,1)}, bf16[256,896]{1,0:T(8,128)(2,1)}) fusion(bf16[1,256,3584]{2,1,0:T(8,128)(2,1)} %param.15, s32[]{:T(128)S(6)} %select_n.79, s32[]{:T(128)S(6)} %select_n.77, s32[]{:T(128)S(6)} %select_n.75), kind=kLoop, calls=%fused_computation.2 | loop fusion | bytes 2752524 | tf_op jit(solution)/shard_map/dynamic_slice | solution.py:350
  32.8 9.5 %all-to-all-start.1 = ((bf16[32,16,896]{2,1,0:T(8,128)(2,1)}), bf16[32,16,896]{2,1,0:T(8,128)(2,1)S(1)}, u32[]{:S(2)}, u32[]{:S(2)}) async-start(bf16[32,16,896]{2,1,0:T(8,128)(2,1)} %bitcast.6), calls=%async_computation.1 | async-start | bytes 1835008 | tf_op jit(solution)/shard_map/all_to_all | solution.py:353
  42.3 4.9 %collective-permute-start = (bf16[256,896]{1,0:T(8,128)(2,1)}, bf16[256,896]{1,0:T(8,128)(2,1)S(1)}, u32[]{:S(2)}, u32[]{:S(2)}) collective-permute-start(bf16[256,896]{1,0:T(8,128)(2,1)} %get-tuple-element.14), channel_id=1, source_target_pairs={{0,2},{1,3},{2,0},{3,1},{4,6},{5,7},{6,4},{7,5},{8,10},{9,11},{10,... | collective-permute-start | bytes 1376264 | tf_op jit(solution)/shard_map/ppermute | solution.py:328
  47.2 2.2 %collective-permute-start.1 = (bf16[256,896]{1,0:T(8,128)(2,1)}, bf16[256,896]{1,0:T(8,128)(2,1)S(1)}, u32[]{:S(2)}, u32[]{:S(2)}) collective-permute-start(bf16[256,896]{1,0:T(8,128)(2,1)} %get-tuple-element.15), channel_id=1, source_target_pairs={{0,1},{1,2},{2,3},{3,0},{4,5},{5,6},{6,7},{7,4},{8,9},{9,10},{10,1... | collective-permute-start | bytes 1376264 | tf_op jit(solution)/shard_map/ppermute | solution.py:328
  49.4 4.3 %collective-permute-start.2 = (bf16[256,896]{1,0:T(8,128)(2,1)}, bf16[256,896]{1,0:T(8,128)(2,1)S(1)}, u32[]{:S(2)}, u32[]{:S(2)}) collective-permute-start(bf16[256,896]{1,0:T(8,128)(2,1)} %get-tuple-element.16), channel_id=1, source_target_pairs={{0,3},{1,0},{2,1},{3,2},{4,7},{5,4},{6,5},{7,6},{8,11},{9,8},{10,9... | collective-permute-start | bytes 1376264 | tf_op jit(solution)/shard_map/ppermute | solution.py:328
  53.7 4.0 %collective-permute-done.w2 = bf16[256,896]{1,0:T(8,128)(2,1)S(1)} collective-permute-done((bf16[256,896]{1,0:T(8,128)(2,1)}, bf16[256,896]{1,0:T(8,128)(2,1)S(1)}, u32[]{:S(2)}, u32[]{:S(2)}) %collective-permute-start) | collective-permute-done | bytes 458784 | tf_op jit(solution)/shard_map/ppermute | solution.py:328
  57.7 0.8 copy-done.3
  58.5 9.7 %collective-permute-done.1.w3 = bf16[256,896]{1,0:T(8,128)(2,1)S(1)} collective-permute-done((bf16[256,896]{1,0:T(8,128)(2,1)}, bf16[256,896]{1,0:T(8,128)(2,1)S(1)}, u32[]{:S(2)}, u32[]{:S(2)}) %collective-permute-start.1) | collective-permute-done | bytes 458784 | tf_op jit(solution)/shard_map/ppermute | solution.py:328
  68.2 0.8 copy-done.5
  69.0 0.8 copy-done.7
  69.7 1.2 up_parts.1
  71.0 18.2 %all_to_all.30.part_ref = bf16[4,1024,128]{2,1,0:T(8,128)(2,1)S(1)} all-to-all(bf16[4,1024,128]{2,1,0:T(8,128)(2,1)S(1)} %up_parts.1), channel_id=1, replica_groups=mesh['zh'=4,'zl'=4,'y'=4,'c'=2,'tp'=4] {'tp'}, dimensions={0} | all-to-all | bytes 2097152 | tf_op jit(solution)/shard_map/all_to_all | solution.py:359
  89.2 0.2 hidden_copies.1
  89.4 15.8 %all_to_all.31.hidden_ref = bf16[4,1024,128]{2,1,0:T(8,128)(2,1)S(1)} all-to-all(bf16[4,1024,128]{2,1,0:T(8,128)(2,1)S(1)} %hidden_copies.1), channel_id=1, replica_groups=mesh['zh'=4,'zl'=4,'y'=4,'c'=2,'tp'=4] {'tp'}, dimensions={0} | all-to-all | bytes 2097152 | tf_op jit(solution)/shard_map/all_to_all | solution.py:360
  105.2 2.3 %down_rows.1 = bf16[512,896]{1,0:T(8,128)(2,1)} custom-call(s32[1]{0:T(128)} %bitcast.x_ref, bf16[4,1024,128]{2,1,0:T(8,128)(2,1)S(1)} %all_to_all.31.hidden_ref, bf16[256,3584]{1,0:T(8,128)(2,1)S(1)} %bitcast.28, bf16[256,896]{1,0:T(8,128)(2,1)S(1)} %copy-done.8, bf16[256,896]{1,0:T(8,128)(2,1)S(1)} %copy-done.4, bf16[256,896]{1,0:T(8,128)(2,1)S(1)} %copy-done.6), custom_call_target="tpu_custom_call" | custom-call | flops 939524096 | bytes 3801088 | tf_op jit(solution)/shard_map/down_rows/pallas_call | solution.py:257
  107.5 10.4 %all-to-all-start.4 = ((bf16[32,16,896]{2,1,0:T(8,128)(2,1)}), bf16[32,16,896]{2,1,0:T(8,128)(2,1)S(1)}, u32[]{:S(2)}, u32[]{:S(2)}) async-start(bf16[32,16,896]{2,1,0:T(8,128)(2,1)} %bitcast.9), calls=%async_computation.4 | async-start | bytes 1835008 | tf_op jit(solution)/shard_map/all_to_all | solution.py:363
  117.9 2.3 %collective-permute-start.3 = (bf16[2,32,576]{2,1,0:T(8,128)(2,1)S(1)}, bf16[2,32,576]{2,1,0:T(8,128)(2,1)S(1)}, u32[]{:S(2)}, u32[]{:S(2)}) collective-permute-start(bf16[2,32,576]{2,1,0:T(8,128)(2,1)S(1)} %copy-done.9), channel_id=1, source_target_pairs={{0,1},{1,2},{2,3},{3,0},{4,5},{5,6},{6,7},{7,4},{8,9},{9,10},{10,1... | collective-permute-start | bytes 221192 | tf_op jit(solution)/shard_map/ppermute | solution.py:328
  120.2 3.7 %collective-permute-start.4 = (bf16[2,32,576]{2,1,0:T(8,128)(2,1)S(1)}, bf16[2,32,576]{2,1,0:T(8,128)(2,1)S(1)}, u32[]{:S(2)}, u32[]{:S(2)}) collective-permute-start(bf16[2,32,576]{2,1,0:T(8,128)(2,1)S(1)} %copy-done.9), channel_id=1, source_target_pairs={{0,2},{1,3},{2,0},{3,1},{4,6},{5,7},{6,4},{7,5},{8,10},{9,11},{10,... | collective-permute-start | bytes 221192 | tf_op jit(solution)/shard_map/ppermute | solution.py:328
  123.9 2.5 %collective-permute-start.5 = (bf16[2,32,576]{2,1,0:T(8,128)(2,1)S(1)}, bf16[2,32,576]{2,1,0:T(8,128)(2,1)S(1)}, u32[]{:S(2)}, u32[]{:S(2)}) collective-permute-start(bf16[2,32,576]{2,1,0:T(8,128)(2,1)S(1)} %copy-done.9), channel_id=1, source_target_pairs={{0,3},{1,0},{2,1},{3,2},{4,7},{5,4},{6,5},{7,6},{8,11},{9,8},{10,9... | collective-permute-start | bytes 221192 | tf_op jit(solution)/shard_map/ppermute | solution.py:328
  126.5 0.1 slice_convert_fusion
  126.7 0.1 fusion.1
  126.9 0.1 copy.32
  127.0 0.1 compare_reduce_fusion
  127.1 0.2 fusion
  127.4 0.1 copy.30
  127.5 0.1 eq.60
  127.6 0.1 copy.34
  128.0 1.4 collective-permute-done.5.q3
  129.4 1.7 attend_own.1
  131.1 10.8 %all-to-all-done.4 = bf16[32,16,896]{2,1,0:T(8,128)(2,1)S(1)} async-done(((bf16[32,16,896]{2,1,0:T(8,128)(2,1)}), bf16[32,16,896]{2,1,0:T(8,128)(2,1)S(1)}, u32[]{:S(2)}, u32[]{:S(2)}) %all-to-all-start.4) | async-done | bytes 917536 | tf_op jit(solution)/shard_map/all_to_all | solution.py:363
  141.9 1.1 mixed_rows.1
  143.0 6.3 %all-to-all-start.5 = ((bf16[4,224,128]{2,1,0:T(8,128)(2,1)}), bf16[4,224,128]{2,1,0:T(8,128)(2,1)S(1)}, u32[]{:S(2)}, u32[]{:S(2)}) async-start(bf16[4,224,128]{2,1,0:T(8,128)(2,1)} %mixed_rows.1), calls=%async_computation.5 | async-start | bytes 458752 | tf_op jit(solution)/shard_map/all_to_all | solution.py:371
  149.4 2.2 %collective-permute-start.8 = (bf16[2,32,640]{2,1,0:T(8,128)(2,1)S(1)}, bf16[2,32,640]{2,1,0:T(8,128)(2,1)S(1)}, u32[]{:S(2)}, u32[]{:S(2)}) collective-permute-start(bf16[2,32,640]{2,1,0:T(8,128)(2,1)S(1)} %get-tuple-element.41), channel_id=1, source_target_pairs={{0,1},{1,2},{2,3},{3,0},{4,5},{5,6},{6,7},{7,4},{8,9},{9,10},{10,1... | collective-permute-start | bytes 245768 | tf_op jit(solution)/shard_map/ppermute | solution.py:328
  151.6 3.7 %collective-permute-start.7 = (bf16[2,32,640]{2,1,0:T(8,128)(2,1)S(1)}, bf16[2,32,640]{2,1,0:T(8,128)(2,1)S(1)}, u32[]{:S(2)}, u32[]{:S(2)}) collective-permute-start(bf16[2,32,640]{2,1,0:T(8,128)(2,1)S(1)} %get-tuple-element.42), channel_id=1, source_target_pairs={{0,2},{1,3},{2,0},{3,1},{4,6},{5,7},{6,4},{7,5},{8,10},{9,11},{10,... | collective-permute-start | bytes 245768 | tf_op jit(solution)/shard_map/ppermute | solution.py:328
  155.3 2.6 %collective-permute-start.6 = (bf16[2,32,640]{2,1,0:T(8,128)(2,1)S(1)}, bf16[2,32,640]{2,1,0:T(8,128)(2,1)S(1)}, u32[]{:S(2)}, u32[]{:S(2)}) collective-permute-start(bf16[2,32,640]{2,1,0:T(8,128)(2,1)S(1)} %get-tuple-element.43), channel_id=1, source_target_pairs={{0,3},{1,0},{2,1},{3,2},{4,7},{5,4},{6,5},{7,6},{8,11},{9,8},{10,9... | collective-permute-start | bytes 245768 | tf_op jit(solution)/shard_map/ppermute | solution.py:328
  157.9 1.3 collective-permute-done.7
  159.2 1.9 %collective-permute-done.6 = bf16[2,32,640]{2,1,0:T(8,128)(2,1)S(1)} collective-permute-done((bf16[2,32,640]{2,1,0:T(8,128)(2,1)S(1)}, bf16[2,32,640]{2,1,0:T(8,128)(2,1)S(1)}, u32[]{:S(2)}, u32[]{:S(2)}) %collective-permute-start.6) | collective-permute-done | bytes 81952 | tf_op jit(solution)/shard_map/ppermute | solution.py:328
  161.0 0.2 add_add_fusion
  161.3 0.1 divide_reduce_fusion.3
  161.4 0.8 add_convert_fusion
  162.2 5.5 %all-to-all-done.5.parts_ref = bf16[4,224,128]{2,1,0:T(8,128)(2,1)S(1)} async-done(((bf16[4,224,128]{2,1,0:T(8,128)(2,1)}), bf16[4,224,128]{2,1,0:T(8,128)(2,1)S(1)}, u32[]{:S(2)}, u32[]{:S(2)}) %all-to-all-start.5) | async-done | bytes 229408 | tf_op jit(solution)/shard_map/all_to_all | solution.py:371
  167.7 0.7 summed.1
  (53 shorter events, 0.7 us)
Async XLA Ops:
  0.6 4.4 %copy-start = (bf16[32,3584]{1,0:T(8,128)(2,1)S(1)}, bf16[32,3584]{1,0:T(8,128)(2,1)}, u32[]{:S(2)}) copy-start(bf16[32,3584]{1,0:T(8,128)(2,1)} %param.11) | copy-start | bytes 688132
  0.6 4.2 %copy-start.10 = (f32[32,8]{0,1:T(8,128)S(1)}, f32[32,8]{0,1:T(8,128)}, u32[]{:S(2)}) copy-start(f32[32,8]{0,1:T(8,128)} %param.13) | copy-start | bytes 3076
  0.7 4.3 %copy-start.11 = (s32[32,8]{0,1:T(8,128)S(1)}, s32[32,8]{0,1:T(8,128)}, u32[]{:S(2)}) copy-start(s32[32,8]{0,1:T(8,128)} %param.12) | copy-start | bytes 3076
  0.7 32.1 %all-to-all-start = ((bf16[4,896,256]{2,1,0:T(8,128)(2,1)}), bf16[4,896,256]{2,1,0:T(8,128)(2,1)S(1)}, u32[]{:S(2)}, u32[]{:S(2)}) async-start(bf16[4,896,256]{2,1,0:T(8,128)(2,1)} %bitcast.32), calls=%async_computation | async-start | bytes 3670016 | tf_op jit(solution)/shard_map/all_to_all | solution.py:341
  32.8 37.0 %all-to-all-start.1 = ((bf16[32,16,896]{2,1,0:T(8,128)(2,1)}), bf16[32,16,896]{2,1,0:T(8,128)(2,1)S(1)}, u32[]{:S(2)}, u32[]{:S(2)}) async-start(bf16[32,16,896]{2,1,0:T(8,128)(2,1)} %bitcast.6), calls=%async_computation.1 | async-start | bytes 1835008 | tf_op jit(solution)/shard_map/all_to_all | solution.py:353
  42.3 15.4 %collective-permute-start = (bf16[256,896]{1,0:T(8,128)(2,1)}, bf16[256,896]{1,0:T(8,128)(2,1)S(1)}, u32[]{:S(2)}, u32[]{:S(2)}) collective-permute-start(bf16[256,896]{1,0:T(8,128)(2,1)} %get-tuple-element.14), channel_id=1, source_target_pairs={{0,2},{1,3},{2,0},{3,1},{4,6},{5,7},{6,4},{7,5},{8,10},{9,11},{10,... | collective-permute-start | bytes 1376264 | tf_op jit(solution)/shard_map/ppermute | solution.py:328
  47.2 21.0 %collective-permute-start.1 = (bf16[256,896]{1,0:T(8,128)(2,1)}, bf16[256,896]{1,0:T(8,128)(2,1)S(1)}, u32[]{:S(2)}, u32[]{:S(2)}) collective-permute-start(bf16[256,896]{1,0:T(8,128)(2,1)} %get-tuple-element.15), channel_id=1, source_target_pairs={{0,1},{1,2},{2,3},{3,0},{4,5},{5,6},{6,7},{7,4},{8,9},{9,10},{10,1... | collective-permute-start | bytes 1376264 | tf_op jit(solution)/shard_map/ppermute | solution.py:328
  49.4 19.6 %collective-permute-start.2 = (bf16[256,896]{1,0:T(8,128)(2,1)}, bf16[256,896]{1,0:T(8,128)(2,1)S(1)}, u32[]{:S(2)}, u32[]{:S(2)}) collective-permute-start(bf16[256,896]{1,0:T(8,128)(2,1)} %get-tuple-element.16), channel_id=1, source_target_pairs={{0,3},{1,0},{2,1},{3,2},{4,7},{5,4},{6,5},{7,6},{8,11},{9,8},{10,9... | collective-permute-start | bytes 1376264 | tf_op jit(solution)/shard_map/ppermute | solution.py:328
  57.7 0.8 copy-start.3
  68.2 0.8 copy-start.5
  69.0 0.8 copy-start.7
  89.2 16.0 %copy-start.1 = (bf16[1,256,3584]{2,1,0:T(8,128)(2,1)S(1)}, bf16[1,256,3584]{2,1,0:T(8,128)(2,1)}, u32[]{:S(2)}) copy-start(bf16[1,256,3584]{2,1,0:T(8,128)(2,1)} %param.15) | copy-start | bytes 5505028
  89.2 16.0 %copy-start.4 = (bf16[256,896]{1,0:T(8,128)(2,1)S(1)}, bf16[256,896]{1,0:T(8,128)(2,1)}, u32[]{:S(2)}) copy-start(bf16[256,896]{1,0:T(8,128)(2,1)} %copy-done.3) | copy-start | bytes 1376260
  89.2 16.0 %copy-start.6 = (bf16[256,896]{1,0:T(8,128)(2,1)S(1)}, bf16[256,896]{1,0:T(8,128)(2,1)}, u32[]{:S(2)}) copy-start(bf16[256,896]{1,0:T(8,128)(2,1)} %copy-done.5) | copy-start | bytes 1376260
  89.2 16.0 %copy-start.8 = (bf16[256,896]{1,0:T(8,128)(2,1)S(1)}, bf16[256,896]{1,0:T(8,128)(2,1)}, u32[]{:S(2)}) copy-start(bf16[256,896]{1,0:T(8,128)(2,1)} %copy-done.7) | copy-start | bytes 1376260
  107.5 10.4 %copy-start.9 = (bf16[2,32,576]{2,1,0:T(8,128)(2,1)S(1)}, bf16[2,32,576]{2,1,0:T(8,128)(2,1)}, u32[]{:S(2)}) copy-start(bf16[2,32,576]{2,1,0:T(8,128)(2,1)} %q0.1) | copy-start | bytes 221188
  107.5 34.4 %all-to-all-start.4 = ((bf16[32,16,896]{2,1,0:T(8,128)(2,1)}), bf16[32,16,896]{2,1,0:T(8,128)(2,1)S(1)}, u32[]{:S(2)}, u32[]{:S(2)}) async-start(bf16[32,16,896]{2,1,0:T(8,128)(2,1)} %bitcast.9), calls=%async_computation.4 | async-start | bytes 1835008 | tf_op jit(solution)/shard_map/all_to_all | solution.py:363
  117.9 10.0 %copy-start.12 = (s32[2]{0:T(128)S(1)}, s32[2]{0:T(128)}, u32[]{:S(2)}) copy-start(s32[2]{0:T(128)} %param.10) | copy-start | bytes 28
  117.9 11.5 %copy-start.2 = (bf16[2,256,576]{1,2,0:T(8,128)(2,1)S(1)}, bf16[2,256,576]{1,2,0:T(8,128)(2,1)}, u32[]{:S(2)}) copy-start(bf16[2,256,576]{1,2,0:T(8,128)(2,1)} %param.9) | copy-start | bytes 1769476
  117.9 10.1 %collective-permute-start.3 = (bf16[2,32,576]{2,1,0:T(8,128)(2,1)S(1)}, bf16[2,32,576]{2,1,0:T(8,128)(2,1)S(1)}, u32[]{:S(2)}, u32[]{:S(2)}) collective-permute-start(bf16[2,32,576]{2,1,0:T(8,128)(2,1)S(1)} %copy-done.9), channel_id=1, source_target_pairs={{0,1},{1,2},{2,3},{3,0},{4,5},{5,6},{6,7},{7,4},{8,9},{9,10},{10,1... | collective-permute-start | bytes 221192 | tf_op jit(solution)/shard_map/ppermute | solution.py:328
  120.2 7.8 %collective-permute-start.4 = (bf16[2,32,576]{2,1,0:T(8,128)(2,1)S(1)}, bf16[2,32,576]{2,1,0:T(8,128)(2,1)S(1)}, u32[]{:S(2)}, u32[]{:S(2)}) collective-permute-start(bf16[2,32,576]{2,1,0:T(8,128)(2,1)S(1)} %copy-done.9), channel_id=1, source_target_pairs={{0,2},{1,3},{2,0},{3,1},{4,6},{5,7},{6,4},{7,5},{8,10},{9,11},{10,... | collective-permute-start | bytes 221192 | tf_op jit(solution)/shard_map/ppermute | solution.py:328
  123.9 5.5 %collective-permute-start.5 = (bf16[2,32,576]{2,1,0:T(8,128)(2,1)S(1)}, bf16[2,32,576]{2,1,0:T(8,128)(2,1)S(1)}, u32[]{:S(2)}, u32[]{:S(2)}) collective-permute-start(bf16[2,32,576]{2,1,0:T(8,128)(2,1)S(1)} %copy-done.9), channel_id=1, source_target_pairs={{0,3},{1,0},{2,1},{3,2},{4,7},{5,4},{6,5},{7,6},{8,11},{9,8},{10,9... | collective-permute-start | bytes 221192 | tf_op jit(solution)/shard_map/ppermute | solution.py:328
  143.0 24.7 %all-to-all-start.5 = ((bf16[4,224,128]{2,1,0:T(8,128)(2,1)}), bf16[4,224,128]{2,1,0:T(8,128)(2,1)S(1)}, u32[]{:S(2)}, u32[]{:S(2)}) async-start(bf16[4,224,128]{2,1,0:T(8,128)(2,1)} %mixed_rows.1), calls=%async_computation.5 | async-start | bytes 458752 | tf_op jit(solution)/shard_map/all_to_all | solution.py:371
  149.4 8.5 %collective-permute-start.8 = (bf16[2,32,640]{2,1,0:T(8,128)(2,1)S(1)}, bf16[2,32,640]{2,1,0:T(8,128)(2,1)S(1)}, u32[]{:S(2)}, u32[]{:S(2)}) collective-permute-start(bf16[2,32,640]{2,1,0:T(8,128)(2,1)S(1)} %get-tuple-element.41), channel_id=1, source_target_pairs={{0,1},{1,2},{2,3},{3,0},{4,5},{5,6},{6,7},{7,4},{8,9},{9,10},{10,1... | collective-permute-start | bytes 245768 | tf_op jit(solution)/shard_map/ppermute | solution.py:328
  151.6 7.6 %collective-permute-start.7 = (bf16[2,32,640]{2,1,0:T(8,128)(2,1)S(1)}, bf16[2,32,640]{2,1,0:T(8,128)(2,1)S(1)}, u32[]{:S(2)}, u32[]{:S(2)}) collective-permute-start(bf16[2,32,640]{2,1,0:T(8,128)(2,1)S(1)} %get-tuple-element.42), channel_id=1, source_target_pairs={{0,2},{1,3},{2,0},{3,1},{4,6},{5,7},{6,4},{7,5},{8,10},{9,11},{10,... | collective-permute-start | bytes 245768 | tf_op jit(solution)/shard_map/ppermute | solution.py:328
  155.3 5.8 %collective-permute-start.6 = (bf16[2,32,640]{2,1,0:T(8,128)(2,1)S(1)}, bf16[2,32,640]{2,1,0:T(8,128)(2,1)S(1)}, u32[]{:S(2)}, u32[]{:S(2)}) collective-permute-start(bf16[2,32,640]{2,1,0:T(8,128)(2,1)S(1)} %get-tuple-element.43), channel_id=1, source_target_pairs={{0,3},{1,0},{2,1},{3,2},{4,7},{5,4},{6,5},{7,6},{8,11},{9,8},{10,9... | collective-permute-start | bytes 245768 | tf_op jit(solution)/shard_map/ppermute | solution.py:328

commit v4 on v3

--- a/solution.py
+++ b/solution.py
@@ -221,29 +221,28 @@
     return weight_ref.at[:, pl.ds(pl.multiple_of(place * cols, LANES), cols)]
 
 
-def down_kernel(x_ref, hidden_ref, weight_ref, w1, w2, w3, out_ref, own, held, sems, own_sem):
+def down_kernel(x_ref, hidden_ref, weight_ref, w1, w2, w3, out_ref, near, held, near_sems, sems):
     groups, count = hidden_ref.shape[0], held.shape[0]
-    step = held.shape[0] // sems.shape[0]
+    step = count // sems.shape[0]
     place = [lax.rem(x_ref[0] + k, groups) for k in range(groups)]
-    fetch = pltpu.make_async_copy(columns_at(weight_ref, x_ref[0], own.shape[1]), own, own_sem)
-    fetch.start()
+    sources = [columns_at(weight_ref, x_ref[0], near.shape[2]), w1, w2, w3]
+    fetches = [pltpu.make_async_copy(source, near.at[k], near_sems.at[k]) for k, source in enumerate(sources)]
+    for fetch in fetches:
+        fetch.start()
     copies = []
 
-    def dot(left, right):
-        return jnp.dot(left, right, preferred_element_type=jnp.float32)
-
-    def group(j, i):
-        halves = [hidden_ref[j, pl.ds(h * count + i * step, step)] for h in range(hidden_ref.shape[1] // count)]
-        return jnp.concatenate(halves, axis=1)
+    def part(k, i):
+        parts = hidden_ref.shape[1] // count
+        lines = [hidden_ref[place[k], pl.ds(h * count + i * step, step)] for h in range(parts)]
+        return jnp.dot(jnp.concatenate(lines, axis=1), near[k], preferred_element_type=jnp.float32)
 
     for i in range(sems.shape[0]):
         rows = pl.ds(i * step, step)
-        total = dot(group(place[1], i), w1[...])
-        total = total + dot(group(place[2], i), w2[...])
-        total = total + dot(group(place[3], i), w3[...])
-        if i == 0:
-            fetch.wait()
-        total = total + dot(group(place[0], i), own[...])
+        total = None
+        for k in range(groups):
+            if i == 0:
+                fetches[k].wait()
+            total = part(k, i) if k == 0 else total + part(k, i)
         held[rows] = total.astype(BF)
         copies.append(pltpu.make_async_copy(held.at[rows], out_ref.at[rows], sems.at[i]))
         copies[-1].start()
@@ -252,21 +251,22 @@
 
 
 def down_rows(x, hidden, weight, after, far, before):
-    own = jax.ShapeDtypeStruct(after.shape, BF)
-    out = jax.ShapeDtypeStruct((hidden.shape[1] * LANES // own.shape[0], own.shape[1]), BF)
+    width, cols = after.shape
+    groups, lines, _ = hidden.shape
+    out = jax.ShapeDtypeStruct((lines * LANES // width, cols), BF)
     return pl.pallas_call(
         down_kernel,
         out_shape=out,
-        in_specs=[pl.BlockSpec(memory_space=pltpu.SMEM), INSIDE, OUTSIDE] + [INSIDE] * 3,
+        in_specs=[pl.BlockSpec(memory_space=pltpu.SMEM), INSIDE] + [OUTSIDE] * 4,
         out_specs=OUTSIDE,
         scratch_shapes=[
-            pltpu.VMEM(own.shape, BF),
+            pltpu.VMEM((groups, width, cols), BF),
             pltpu.VMEM(out.shape, BF),
+            pltpu.SemaphoreType.DMA((groups,)),
             pltpu.SemaphoreType.DMA((2,)),
-            pltpu.SemaphoreType.DMA(()),
         ],
         compiler_params=pltpu.CompilerParams(vmem_limit_bytes=VMEM),
-        cost_estimate=cost(2 * hidden.size * own.shape[1], hidden, own, own, own, own, out),
+        cost_estimate=cost(2 * hidden.size * cols, hidden, after, after, after, after, out),
         name="down_rows",
     )(x.reshape(1), hidden, weight, after, far, before)
 
@@ -351,12 +351,12 @@
     outgoing, up, cut = lax.optimization_barrier((outgoing, up, cut))
     far, before, after = (shift(block, k, tp) for block, k in zip(cut, (2, 1, tp - 1)))
     received = lax.all_to_all(outgoing.reshape(near, slots, cols), NEAR, 0, 0, tiled=True)
-    received, far, before, after = lax.optimization_barrier(
-        (received.reshape(near * slots, cols), far, before, after)
-    )
+    received = received.reshape(near * slots, cols)
     take = shares(packed[:, cols:], rows, first, near, away)
 
-    part = lax.all_to_all(up_parts(received, up), "tp", 0, 0, tiled=True)
+    part = up_parts(received, up)
+    part, far, after, before = lax.optimization_barrier((part, far, after, before))
+    part = lax.all_to_all(part, "tp", 0, 0, tiled=True)
     hidden = lax.all_to_all(hidden_copies(part), "tp", 0, 0, tiled=True)
     output = down_rows(x, hidden, weight, after, far, before)
 

time: 169 us -> 168 us (level)
  local copies, waits for them, and re-layouts: 5.88 us -> 3.48 us
    all_to_all x1, waiting for transfers between devices: 0.01 us -> 13.8 us  [shards(): lax.all_to_all(outgoing.reshape(near, slots, cols), NEAR, 0, 0, tiled=True)]
    ppermute x9, waiting for transfers between devices: 18.3 us -> 5.3 us  [shift(): return lax.ppermute(array, 'tp', [(i, (i + by) % tp) for i in range(tp)])]
    unnamed x27 -> x15, local copies, waits for them, and re-layouts: 2.47 us -> 0.12 us
  transfers between devices with their start and end apart: 13 -> 13, of which waited for: 7 -> 8; matrix products, arithmetic and copies ran while one was open for 3% -> 3% of each run, Pallas kernels for 2% -> 3%
where the time goes in v4:
time: 168 us; the launch traced here: 167 us
  starting transfers between devices  57.9 us (34%)
  blocking collectives  57.2 us (34%)
  waiting for transfers between devices  35.4 us (21%)
  Pallas kernels  9.77 us (6%)
  local copies, waits for them, and re-layouts  3.48 us (2%)
  other arithmetic  1.75 us (1%)
    ppermute x9, starting transfers between devices, shift(): return lax.ppermute(array, 'tp', [(i, (i + by) % tp) for i in range(tp)])  27.2 us
    all_gather x1, blocking collectives, shards(): packed = lax.all_gather(packed, FAR, axis=0, tiled=True)  23.7 us
    all_to_all x1, blocking collectives, shards(): part = lax.all_to_all(part, 'tp', 0, 0, tiled=True)  18.1 us
    all_to_all x1, blocking collectives, shards(): hidden = lax.all_to_all(hidden_copies(part), 'tp', 0, 0, tiled=True)  15.4 us
    all_to_all x1, waiting for transfers between devices, shards(): lax.all_to_all(outgoing.reshape(near, slots, cols), NEAR, 0, 0, tiled=True)  13.8 us
    all_to_all x1, waiting for transfers between devices, shards(): lax.all_to_all(output.reshape(near, slots, cols), NEAR, 0, 0, tiled=True)  10.8 us
    all_to_all x1, starting transfers between devices, shards(): lax.all_to_all(output.reshape(near, slots, cols), NEAR, 0, 0, tiled=True)  10.7 us
    all_to_all x1, starting transfers between devices, shards(): lax.all_to_all(outgoing.reshape(near, slots, cols), NEAR, 0, 0, tiled=True)  9.52 us
  transfers between devices with their start and end apart: 13, of which 8 were waited for; matrix products, arithmetic and copies ran while one was open for 3% of the time, Pallas kernels for 3%

profile of v4, /device:TPU:33, one launch (start us, length us, event | category | flops | bytes accessed | tf_op | source)
XLA Modules:
  0.0 166.8 jit_solution(12100355778047997694)
XLA Ops:
  0.7 4.2 %all-to-all-start = ((bf16[4,896,256]{2,1,0:T(8,128)(2,1)}), bf16[4,896,256]{2,1,0:T(8,128)(2,1)S(1)}, u32[]{:S(2)}, u32[]{:S(2)}) async-start(bf16[4,896,256]{2,1,0:T(8,128)(2,1)} %bitcast.32), calls=%async_computation | async-start | bytes 3670016 | tf_op jit(solution)/shard_map/all_to_all | solution.py:341
  4.8 0.1 copy.26
  4.9 0.1 copy.28
  5.0 0.1 fusion.12
  5.1 0.1 concatenate.9
  5.2 23.7 %all_gather.3.packed_ref = bf16[128,1024]{1,0:T(8,128)(2,1)S(1)} all-gather(bf16[32,1024]{1,0:T(8,128)(2,1)S(1)} %concatenate.9), channel_id=1, replica_groups=mesh['zh'=4,'zl'=4,'y'=4,'c'=2,'tp'=4] {'zh'}, dimensions={0}, use_global_device_ids=true | all-gather | bytes 327680 | tf_op jit(solution)/shard_map/all_gather | solution.py:345
  28.9 1.4 placed_rows.1
  30.3 2.4 %dynamic-slice_bitcast_fusion = (bf16[256,896]{1,0:T(8,128)(2,1)}, bf16[256,896]{1,0:T(8,128)(2,1)}, bf16[256,896]{1,0:T(8,128)(2,1)}) fusion(bf16[1,256,3584]{2,1,0:T(8,128)(2,1)} %param.15, s32[]{:T(128)S(6)} %select_n.79, s32[]{:T(128)S(6)} %select_n.77, s32[]{:T(128)S(6)} %select_n.75), kind=kLoop, calls=%fused_computation.2 | loop fusion | bytes 2752524 | tf_op jit(solution)/shard_map/dynamic_slice | solution.py:350
  32.7 9.5 %all-to-all-start.1 = ((bf16[32,16,896]{2,1,0:T(8,128)(2,1)}), bf16[32,16,896]{2,1,0:T(8,128)(2,1)S(1)}, u32[]{:S(2)}, u32[]{:S(2)}) async-start(bf16[32,16,896]{2,1,0:T(8,128)(2,1)} %bitcast.6), calls=%async_computation.1 | async-start | bytes 1835008 | tf_op jit(solution)/shard_map/all_to_all | solution.py:353
  42.3 4.9 %collective-permute-start = (bf16[256,896]{1,0:T(8,128)(2,1)}, bf16[256,896]{1,0:T(8,128)(2,1)}, u32[]{:S(2)}, u32[]{:S(2)}) collective-permute-start(bf16[256,896]{1,0:T(8,128)(2,1)} %get-tuple-element.15), channel_id=1, source_target_pairs={{0,2},{1,3},{2,0},{3,1},{4,6},{5,7},{6,4},{7,5},{8,10},{9,11},{10,... | collective-permute-start | bytes 1376264 | tf_op jit(solution)/shard_map/ppermute | solution.py:328
  47.1 2.8 %collective-permute-start.1 = (bf16[256,896]{1,0:T(8,128)(2,1)}, bf16[256,896]{1,0:T(8,128)(2,1)}, u32[]{:S(2)}, u32[]{:S(2)}) collective-permute-start(bf16[256,896]{1,0:T(8,128)(2,1)} %get-tuple-element.16), channel_id=1, source_target_pairs={{0,3},{1,0},{2,1},{3,2},{4,7},{5,4},{6,5},{7,6},{8,11},{9,8},{10,9... | collective-permute-start | bytes 1376264 | tf_op jit(solution)/shard_map/ppermute | solution.py:328
  49.9 2.5 %collective-permute-start.2 = (bf16[256,896]{1,0:T(8,128)(2,1)}, bf16[256,896]{1,0:T(8,128)(2,1)}, u32[]{:S(2)}, u32[]{:S(2)}) collective-permute-start(bf16[256,896]{1,0:T(8,128)(2,1)} %get-tuple-element.17), channel_id=1, source_target_pairs={{0,1},{1,2},{2,3},{3,0},{4,5},{5,6},{6,7},{7,4},{8,9},{9,10},{10,1... | collective-permute-start | bytes 1376264 | tf_op jit(solution)/shard_map/ppermute | solution.py:328
  52.4 13.8 %all-to-all-done.1 = bf16[32,16,896]{2,1,0:T(8,128)(2,1)S(1)} async-done(((bf16[32,16,896]{2,1,0:T(8,128)(2,1)}), bf16[32,16,896]{2,1,0:T(8,128)(2,1)S(1)}, u32[]{:S(2)}, u32[]{:S(2)}) %all-to-all-start.1) | async-done | bytes 917536 | tf_op jit(solution)/shard_map/all_to_all | solution.py:353
  66.3 1.2 up_parts.1
  67.5 0.3 collective-permute-done.1.w1
  67.9 0.4 collective-permute-done.2.w3
  68.3 18.1 %all_to_all.30.part_ref = bf16[4,1024,128]{2,1,0:T(8,128)(2,1)S(1)} all-to-all(bf16[4,1024,128]{2,1,0:T(8,128)(2,1)S(1)} %up_parts.1), channel_id=1, replica_groups=mesh['zh'=4,'zl'=4,'y'=4,'c'=2,'tp'=4] {'tp'}, dimensions={0} | all-to-all | bytes 2097152 | tf_op jit(solution)/shard_map/all_to_all | solution.py:359
  86.4 0.2 hidden_copies.1
  86.6 15.4 %all_to_all.31.hidden_ref = bf16[4,1024,128]{2,1,0:T(8,128)(2,1)S(1)} all-to-all(bf16[4,1024,128]{2,1,0:T(8,128)(2,1)S(1)} %hidden_copies.1), channel_id=1, replica_groups=mesh['zh'=4,'zl'=4,'y'=4,'c'=2,'tp'=4] {'tp'}, dimensions={0} | all-to-all | bytes 2097152 | tf_op jit(solution)/shard_map/all_to_all | solution.py:360
  102.1 3.4 %down_rows.1 = bf16[512,896]{1,0:T(8,128)(2,1)} custom-call(s32[1]{0:T(128)} %bitcast.x_ref, bf16[4,1024,128]{2,1,0:T(8,128)(2,1)S(1)} %all_to_all.31.hidden_ref, bf16[256,3584]{1,0:T(8,128)(2,1)S(1)} %bitcast.28, bf16[256,896]{1,0:T(8,128)(2,1)} %collective-permute-done.1.w1, bf16[256,896]{1,0:T(8,128)(2,1)} %collective-permute-done.w2, ...), custom_call_target="tpu_custom_call" | custom-call | flops 939524096 | bytes 3801088 | tf_op jit(solution)/shard_map/down_rows/pallas_call | solution.py:257
  105.5 10.7 %all-to-all-start.4 = ((bf16[32,16,896]{2,1,0:T(8,128)(2,1)}), bf16[32,16,896]{2,1,0:T(8,128)(2,1)S(1)}, u32[]{:S(2)}, u32[]{:S(2)}) async-start(bf16[32,16,896]{2,1,0:T(8,128)(2,1)} %bitcast.9), calls=%async_computation.4 | async-start | bytes 1835008 | tf_op jit(solution)/shard_map/all_to_all | solution.py:363
  116.2 2.3 %collective-permute-start.3 = (bf16[2,32,576]{2,1,0:T(8,128)(2,1)S(1)}, bf16[2,32,576]{2,1,0:T(8,128)(2,1)S(1)}, u32[]{:S(2)}, u32[]{:S(2)}) collective-permute-start(bf16[2,32,576]{2,1,0:T(8,128)(2,1)S(1)} %copy-done.3), channel_id=1, source_target_pairs={{0,1},{1,2},{2,3},{3,0},{4,5},{5,6},{6,7},{7,4},{8,9},{9,10},{10,1... | collective-permute-start | bytes 221192 | tf_op jit(solution)/shard_map/ppermute | solution.py:328
  118.6 3.7 %collective-permute-start.4 = (bf16[2,32,576]{2,1,0:T(8,128)(2,1)S(1)}, bf16[2,32,576]{2,1,0:T(8,128)(2,1)S(1)}, u32[]{:S(2)}, u32[]{:S(2)}) collective-permute-start(bf16[2,32,576]{2,1,0:T(8,128)(2,1)S(1)} %copy-done.3), channel_id=1, source_target_pairs={{0,2},{1,3},{2,0},{3,1},{4,6},{5,7},{6,4},{7,5},{8,10},{9,11},{10,... | collective-permute-start | bytes 221192 | tf_op jit(solution)/shard_map/ppermute | solution.py:328
  122.3 2.5 %collective-permute-start.5 = (bf16[2,32,576]{2,1,0:T(8,128)(2,1)S(1)}, bf16[2,32,576]{2,1,0:T(8,128)(2,1)S(1)}, u32[]{:S(2)}, u32[]{:S(2)}) collective-permute-start(bf16[2,32,576]{2,1,0:T(8,128)(2,1)S(1)} %copy-done.3), channel_id=1, source_target_pairs={{0,3},{1,0},{2,1},{3,2},{4,7},{5,4},{6,5},{7,6},{8,11},{9,8},{10,9... | collective-permute-start | bytes 221192 | tf_op jit(solution)/shard_map/ppermute | solution.py:328
  124.8 0.1 slice_convert_fusion
  125.1 0.1 fusion.1
  125.3 0.1 copy.32
  125.4 0.1 compare_reduce_fusion
  125.5 0.2 fusion
  125.7 0.1 copy.30
  125.9 0.1 eq.60
  126.0 0.1 copy.34
  126.3 0.1 pad_add_fusion.place_ref
  126.4 1.4 collective-permute-done.5.q3
  127.8 1.7 attend_own.1
  129.4 10.8 %all-to-all-done.4 = bf16[32,16,896]{2,1,0:T(8,128)(2,1)S(1)} async-done(((bf16[32,16,896]{2,1,0:T(8,128)(2,1)}), bf16[32,16,896]{2,1,0:T(8,128)(2,1)S(1)}, u32[]{:S(2)}, u32[]{:S(2)}) %all-to-all-start.4) | async-done | bytes 917536 | tf_op jit(solution)/shard_map/all_to_all | solution.py:363
  140.2 1.1 mixed_rows.1
  141.4 6.4 %all-to-all-start.5 = ((bf16[4,224,128]{2,1,0:T(8,128)(2,1)}), bf16[4,224,128]{2,1,0:T(8,128)(2,1)S(1)}, u32[]{:S(2)}, u32[]{:S(2)}) async-start(bf16[4,224,128]{2,1,0:T(8,128)(2,1)} %mixed_rows.1), calls=%async_computation.5 | async-start | bytes 458752 | tf_op jit(solution)/shard_map/all_to_all | solution.py:371
  147.8 2.2 %collective-permute-start.8 = (bf16[2,32,640]{2,1,0:T(8,128)(2,1)S(1)}, bf16[2,32,640]{2,1,0:T(8,128)(2,1)S(1)}, u32[]{:S(2)}, u32[]{:S(2)}) collective-permute-start(bf16[2,32,640]{2,1,0:T(8,128)(2,1)S(1)} %get-tuple-element.41), channel_id=1, source_target_pairs={{0,1},{1,2},{2,3},{3,0},{4,5},{5,6},{6,7},{7,4},{8,9},{9,10},{10,1... | collective-permute-start | bytes 245768 | tf_op jit(solution)/shard_map/ppermute | solution.py:328
  150.0 3.7 %collective-permute-start.7 = (bf16[2,32,640]{2,1,0:T(8,128)(2,1)S(1)}, bf16[2,32,640]{2,1,0:T(8,128)(2,1)S(1)}, u32[]{:S(2)}, u32[]{:S(2)}) collective-permute-start(bf16[2,32,640]{2,1,0:T(8,128)(2,1)S(1)} %get-tuple-element.42), channel_id=1, source_target_pairs={{0,2},{1,3},{2,0},{3,1},{4,6},{5,7},{6,4},{7,5},{8,10},{9,11},{10,... | collective-permute-start | bytes 245768 | tf_op jit(solution)/shard_map/ppermute | solution.py:328
  153.7 2.6 %collective-permute-start.6 = (bf16[2,32,640]{2,1,0:T(8,128)(2,1)S(1)}, bf16[2,32,640]{2,1,0:T(8,128)(2,1)S(1)}, u32[]{:S(2)}, u32[]{:S(2)}) collective-permute-start(bf16[2,32,640]{2,1,0:T(8,128)(2,1)S(1)} %get-tuple-element.43), channel_id=1, source_target_pairs={{0,3},{1,0},{2,1},{3,2},{4,7},{5,4},{6,5},{7,6},{8,11},{9,8},{10,9... | collective-permute-start | bytes 245768 | tf_op jit(solution)/shard_map/ppermute | solution.py:328
  156.3 1.3 collective-permute-done.7
  157.6 1.9 %collective-permute-done.6 = bf16[2,32,640]{2,1,0:T(8,128)(2,1)S(1)} collective-permute-done((bf16[2,32,640]{2,1,0:T(8,128)(2,1)S(1)}, bf16[2,32,640]{2,1,0:T(8,128)(2,1)S(1)}, u32[]{:S(2)}, u32[]{:S(2)}) %collective-permute-start.6) | collective-permute-done | bytes 81952 | tf_op jit(solution)/shard_map/ppermute | solution.py:328
  159.4 0.2 add_add_fusion
  159.7 0.1 divide_reduce_fusion.3
  159.8 0.8 add_convert_fusion
  160.6 5.5 %all-to-all-done.5.parts_ref = bf16[4,224,128]{2,1,0:T(8,128)(2,1)S(1)} async-done(((bf16[4,224,128]{2,1,0:T(8,128)(2,1)}), bf16[4,224,128]{2,1,0:T(8,128)(2,1)S(1)}, u32[]{:S(2)}, u32[]{:S(2)}) %all-to-all-start.5) | async-done | bytes 229408 | tf_op jit(solution)/shard_map/all_to_all | solution.py:371
  166.1 0.7 summed.1
  (41 shorter events, 0.5 us)
Async XLA Ops:
  0.6 4.4 %copy-start = (bf16[32,3584]{1,0:T(8,128)(2,1)S(1)}, bf16[32,3584]{1,0:T(8,128)(2,1)}, u32[]{:S(2)}) copy-start(bf16[32,3584]{1,0:T(8,128)(2,1)} %param.11) | copy-start | bytes 688132
  0.6 4.2 %copy-start.4 = (f32[32,8]{0,1:T(8,128)S(1)}, f32[32,8]{0,1:T(8,128)}, u32[]{:S(2)}) copy-start(f32[32,8]{0,1:T(8,128)} %param.13) | copy-start | bytes 3076
  0.7 4.3 %copy-start.5 = (s32[32,8]{0,1:T(8,128)S(1)}, s32[32,8]{0,1:T(8,128)}, u32[]{:S(2)}) copy-start(s32[32,8]{0,1:T(8,128)} %param.12) | copy-start | bytes 3076
  0.7 32.1 %all-to-all-start = ((bf16[4,896,256]{2,1,0:T(8,128)(2,1)}), bf16[4,896,256]{2,1,0:T(8,128)(2,1)S(1)}, u32[]{:S(2)}, u32[]{:S(2)}) async-start(bf16[4,896,256]{2,1,0:T(8,128)(2,1)} %bitcast.32), calls=%async_computation | async-start | bytes 3670016 | tf_op jit(solution)/shard_map/all_to_all | solution.py:341
  32.7 33.5 %all-to-all-start.1 = ((bf16[32,16,896]{2,1,0:T(8,128)(2,1)}), bf16[32,16,896]{2,1,0:T(8,128)(2,1)S(1)}, u32[]{:S(2)}, u32[]{:S(2)}) async-start(bf16[32,16,896]{2,1,0:T(8,128)(2,1)} %bitcast.6), calls=%async_computation.1 | async-start | bytes 1835008 | tf_op jit(solution)/shard_map/all_to_all | solution.py:353
  42.3 25.3 %collective-permute-start = (bf16[256,896]{1,0:T(8,128)(2,1)}, bf16[256,896]{1,0:T(8,128)(2,1)}, u32[]{:S(2)}, u32[]{:S(2)}) collective-permute-start(bf16[256,896]{1,0:T(8,128)(2,1)} %get-tuple-element.15), channel_id=1, source_target_pairs={{0,2},{1,3},{2,0},{3,1},{4,6},{5,7},{6,4},{7,5},{8,10},{9,11},{10,... | collective-permute-start | bytes 1376264 | tf_op jit(solution)/shard_map/ppermute | solution.py:328
  47.1 20.7 %collective-permute-start.1 = (bf16[256,896]{1,0:T(8,128)(2,1)}, bf16[256,896]{1,0:T(8,128)(2,1)}, u32[]{:S(2)}, u32[]{:S(2)}) collective-permute-start(bf16[256,896]{1,0:T(8,128)(2,1)} %get-tuple-element.16), channel_id=1, source_target_pairs={{0,3},{1,0},{2,1},{3,2},{4,7},{5,4},{6,5},{7,6},{8,11},{9,8},{10,9... | collective-permute-start | bytes 1376264 | tf_op jit(solution)/shard_map/ppermute | solution.py:328
  49.9 18.3 %collective-permute-start.2 = (bf16[256,896]{1,0:T(8,128)(2,1)}, bf16[256,896]{1,0:T(8,128)(2,1)}, u32[]{:S(2)}, u32[]{:S(2)}) collective-permute-start(bf16[256,896]{1,0:T(8,128)(2,1)} %get-tuple-element.17), channel_id=1, source_target_pairs={{0,1},{1,2},{2,3},{3,0},{4,5},{5,6},{6,7},{7,4},{8,9},{9,10},{10,1... | collective-permute-start | bytes 1376264 | tf_op jit(solution)/shard_map/ppermute | solution.py:328
  86.4 15.7 %copy-start.1 = (bf16[1,256,3584]{2,1,0:T(8,128)(2,1)S(1)}, bf16[1,256,3584]{2,1,0:T(8,128)(2,1)}, u32[]{:S(2)}) copy-start(bf16[1,256,3584]{2,1,0:T(8,128)(2,1)} %param.15) | copy-start | bytes 5505028
  105.5 10.7 %copy-start.3 = (bf16[2,32,576]{2,1,0:T(8,128)(2,1)S(1)}, bf16[2,32,576]{2,1,0:T(8,128)(2,1)}, u32[]{:S(2)}) copy-start(bf16[2,32,576]{2,1,0:T(8,128)(2,1)} %q0.1) | copy-start | bytes 221188
  105.5 34.7 %all-to-all-start.4 = ((bf16[32,16,896]{2,1,0:T(8,128)(2,1)}), bf16[32,16,896]{2,1,0:T(8,128)(2,1)S(1)}, u32[]{:S(2)}, u32[]{:S(2)}) async-start(bf16[32,16,896]{2,1,0:T(8,128)(2,1)} %bitcast.9), calls=%async_computation.4 | async-start | bytes 1835008 | tf_op jit(solution)/shard_map/all_to_all | solution.py:363
  116.2 10.0 %copy-start.6 = (s32[2]{0:T(128)S(1)}, s32[2]{0:T(128)}, u32[]{:S(2)}) copy-start(s32[2]{0:T(128)} %param.10) | copy-start | bytes 28
  116.2 11.5 %copy-start.2 = (bf16[2,256,576]{1,2,0:T(8,128)(2,1)S(1)}, bf16[2,256,576]{1,2,0:T(8,128)(2,1)}, u32[]{:S(2)}) copy-start(bf16[2,256,576]{1,2,0:T(8,128)(2,1)} %param.9) | copy-start | bytes 1769476
  116.2 10.1 %collective-permute-start.3 = (bf16[2,32,576]{2,1,0:T(8,128)(2,1)S(1)}, bf16[2,32,576]{2,1,0:T(8,128)(2,1)S(1)}, u32[]{:S(2)}, u32[]{:S(2)}) collective-permute-start(bf16[2,32,576]{2,1,0:T(8,128)(2,1)S(1)} %copy-done.3), channel_id=1, source_target_pairs={{0,1},{1,2},{2,3},{3,0},{4,5},{5,6},{6,7},{7,4},{8,9},{9,10},{10,1... | collective-permute-start | bytes 221192 | tf_op jit(solution)/shard_map/ppermute | solution.py:328
  118.6 7.8 %collective-permute-start.4 = (bf16[2,32,576]{2,1,0:T(8,128)(2,1)S(1)}, bf16[2,32,576]{2,1,0:T(8,128)(2,1)S(1)}, u32[]{:S(2)}, u32[]{:S(2)}) collective-permute-start(bf16[2,32,576]{2,1,0:T(8,128)(2,1)S(1)} %copy-done.3), channel_id=1, source_target_pairs={{0,2},{1,3},{2,0},{3,1},{4,6},{5,7},{6,4},{7,5},{8,10},{9,11},{10,... | collective-permute-start | bytes 221192 | tf_op jit(solution)/shard_map/ppermute | solution.py:328
  122.3 5.5 %collective-permute-start.5 = (bf16[2,32,576]{2,1,0:T(8,128)(2,1)S(1)}, bf16[2,32,576]{2,1,0:T(8,128)(2,1)S(1)}, u32[]{:S(2)}, u32[]{:S(2)}) collective-permute-start(bf16[2,32,576]{2,1,0:T(8,128)(2,1)S(1)} %copy-done.3), channel_id=1, source_target_pairs={{0,3},{1,0},{2,1},{3,2},{4,7},{5,4},{6,5},{7,6},{8,11},{9,8},{10,9... | collective-permute-start | bytes 221192 | tf_op jit(solution)/shard_map/ppermute | solution.py:328
  141.4 24.7 %all-to-all-start.5 = ((bf16[4,224,128]{2,1,0:T(8,128)(2,1)}), bf16[4,224,128]{2,1,0:T(8,128)(2,1)S(1)}, u32[]{:S(2)}, u32[]{:S(2)}) async-start(bf16[4,224,128]{2,1,0:T(8,128)(2,1)} %mixed_rows.1), calls=%async_computation.5 | async-start | bytes 458752 | tf_op jit(solution)/shard_map/all_to_all | solution.py:371
  147.8 8.5 %collective-permute-start.8 = (bf16[2,32,640]{2,1,0:T(8,128)(2,1)S(1)}, bf16[2,32,640]{2,1,0:T(8,128)(2,1)S(1)}, u32[]{:S(2)}, u32[]{:S(2)}) collective-permute-start(bf16[2,32,640]{2,1,0:T(8,128)(2,1)S(1)} %get-tuple-element.41), channel_id=1, source_target_pairs={{0,1},{1,2},{2,3},{3,0},{4,5},{5,6},{6,7},{7,4},{8,9},{9,10},{10,1... | collective-permute-start | bytes 245768 | tf_op jit(solution)/shard_map/ppermute | solution.py:328
  150.0 7.6 %collective-permute-start.7 = (bf16[2,32,640]{2,1,0:T(8,128)(2,1)S(1)}, bf16[2,32,640]{2,1,0:T(8,128)(2,1)S(1)}, u32[]{:S(2)}, u32[]{:S(2)}) collective-permute-start(bf16[2,32,640]{2,1,0:T(8,128)(2,1)S(1)} %get-tuple-element.42), channel_id=1, source_target_pairs={{0,2},{1,3},{2,0},{3,1},{4,6},{5,7},{6,4},{7,5},{8,10},{9,11},{10,... | collective-permute-start | bytes 245768 | tf_op jit(solution)/shard_map/ppermute | solution.py:328
  153.7 5.8 %collective-permute-start.6 = (bf16[2,32,640]{2,1,0:T(8,128)(2,1)S(1)}, bf16[2,32,640]{2,1,0:T(8,128)(2,1)S(1)}, u32[]{:S(2)}, u32[]{:S(2)}) collective-permute-start(bf16[2,32,640]{2,1,0:T(8,128)(2,1)S(1)} %get-tuple-element.43), channel_id=1, source_target_pairs={{0,3},{1,0},{2,1},{3,2},{4,7},{5,4},{6,5},{7,6},{8,11},{9,8},{10,9... | collective-permute-start | bytes 245768 | tf_op jit(solution)/shard_map/ppermute | solution.py:328

commit v5 on v4

--- a/solution.py
+++ b/solution.py
@@ -19,7 +19,8 @@
 OUTSIDE = pl.BlockSpec(memory_space=pltpu.HBM)
 
 EP = ("zh", "zl", "y", "c")
-NEAR = ("zl", "y", "c")
+NEAR = ("y", "c", "zl")
+PLANES, PLANE = 4, 8
 FAR = "zh"
 BF = jnp.bfloat16
 
@@ -100,11 +101,15 @@
     return jnp.concatenate(parts + [jnp.zeros((rows, LANES - 3 * TOP), BF)], axis=1)
 
 
+def expert_at(first, place):
+    return (first + place % PLANES * PLANE + place // PLANES).astype(jnp.float32)
+
+
 def place_kernel(first_ref, packed_ref, out_ref, held, sems, *, rows, experts, slots):
     total, wide = packed_ref.shape
     cols = wide - LANES
     ids = packed_ref[:, cols:].astype(jnp.float32).T
-    own = (first_ref[0] + lax.broadcasted_iota(jnp.int32, (experts, total), 0)).astype(jnp.float32)
+    own = expert_at(first_ref[0], lax.broadcasted_iota(jnp.int32, (experts, total), 0))
     named = own == ids[0:1]
     for k in range(1, TOP):
         named = named | (own == ids[k : k + 1])
@@ -151,7 +156,7 @@
     ids = columns[:, :TOP].astype(jnp.float32)
     high = columns[:, TOP : 2 * TOP].astype(jnp.float32)
     low = columns[:, 2 * TOP : 3 * TOP].astype(jnp.float32)
-    own = (first + jnp.arange(experts, dtype=jnp.int32)).astype(jnp.float32)
+    own = expert_at(first, jnp.arange(experts, dtype=jnp.int32))
     hit = ids[:, :, None] == own[None, None, :]
     named = jnp.any(hit, axis=1)
     w_high = jnp.sum(jnp.where(hit, high[:, :, None], 0.0), axis=1)

time: 168 us -> 168 us (level)
  the two profiles are of different devices: /device:TPU:33 before, /device:TPU:9 now
where the time goes in v5:
time: 168 us; the launch traced here: 167 us
  blocking collectives  58 us (35%)
  starting transfers between devices  57.4 us (34%)
  waiting for transfers between devices  35.7 us (21%)
  Pallas kernels  9.77 us (6%)
  local copies, waits for them, and re-layouts  3.48 us (2%)
  other arithmetic  1.76 us (1%)
    ppermute x9, starting transfers between devices, shift(): return lax.ppermute(array, 'tp', [(i, (i + by) % tp) for i in range(tp)])  27.1 us
    all_gather x1, blocking collectives, shards(): packed = lax.all_gather(packed, FAR, axis=0, tiled=True)  24.4 us
    all_to_all x1, blocking collectives, shards(): part = lax.all_to_all(part, 'tp', 0, 0, tiled=True)  18.1 us
    all_to_all x1, blocking collectives, shards(): hidden = lax.all_to_all(hidden_copies(part), 'tp', 0, 0, tiled=True)  15.4 us
    all_to_all x1, waiting for transfers between devices, shards(): lax.all_to_all(outgoing.reshape(near, slots, cols), NEAR, 0, 0, tiled=True)  13.3 us
    all_to_all x1, starting transfers between devices, shards(): lax.all_to_all(output.reshape(near, slots, cols), NEAR, 0, 0, tiled=True)  10.6 us
    all_to_all x1, waiting for transfers between devices, shards(): lax.all_to_all(output.reshape(near, slots, cols), NEAR, 0, 0, tiled=True)  10.2 us
    all_to_all x1, starting transfers between devices, shards(): lax.all_to_all(outgoing.reshape(near, slots, cols), NEAR, 0, 0, tiled=True)  9.14 us
  transfers between devices with their start and end apart: 13, of which 8 were waited for; matrix products, arithmetic and copies ran while one was open for 3% of the time, Pallas kernels for 3%

profile of v5, /device:TPU:9, one launch (start us, length us, event | category | flops | bytes accessed | tf_op | source)
XLA Modules:
  0.0 167.3 jit_solution(6311779685456520342)
XLA Ops:
  0.7 4.2 %all-to-all-start = ((bf16[4,896,256]{2,1,0:T(8,128)(2,1)}), bf16[4,896,256]{2,1,0:T(8,128)(2,1)S(1)}, u32[]{:S(2)}, u32[]{:S(2)}) async-start(bf16[4,896,256]{2,1,0:T(8,128)(2,1)} %bitcast.32), calls=%async_computation | async-start | bytes 3670016 | tf_op jit(solution)/shard_map/all_to_all | solution.py:346
  4.8 0.1 copy.26
  4.9 0.1 copy.28
  5.0 0.1 fusion.12
  5.1 0.1 concatenate.9
  5.2 24.4 %all_gather.3.packed_ref = bf16[128,1024]{1,0:T(8,128)(2,1)S(1)} all-gather(bf16[32,1024]{1,0:T(8,128)(2,1)S(1)} %concatenate.9), channel_id=1, replica_groups=mesh['zh'=4,'zl'=4,'y'=4,'c'=2,'tp'=4] {'zh'}, dimensions={0}, use_global_device_ids=true | all-gather | bytes 327680 | tf_op jit(solution)/shard_map/all_gather | solution.py:350
  29.6 1.4 placed_rows.1
  31.0 2.4 %dynamic-slice_bitcast_fusion = (bf16[256,896]{1,0:T(8,128)(2,1)}, bf16[256,896]{1,0:T(8,128)(2,1)}, bf16[256,896]{1,0:T(8,128)(2,1)}) fusion(bf16[1,256,3584]{2,1,0:T(8,128)(2,1)} %param.15, s32[]{:T(128)S(6)} %select_n.98, s32[]{:T(128)S(6)} %select_n.96, s32[]{:T(128)S(6)} %select_n.94), kind=kLoop, calls=%fused_computation.2 | loop fusion | bytes 2752524 | tf_op jit(solution)/shard_map/dynamic_slice | solution.py:355
  33.4 9.1 %all-to-all-start.1 = ((bf16[32,16,896]{2,1,0:T(8,128)(2,1)}), bf16[32,16,896]{2,1,0:T(8,128)(2,1)S(1)}, u32[]{:S(2)}, u32[]{:S(2)}) async-start(bf16[32,16,896]{2,1,0:T(8,128)(2,1)} %bitcast.6), calls=%async_computation.1 | async-start | bytes 1835008 | tf_op jit(solution)/shard_map/all_to_all | solution.py:358
  42.6 4.9 %collective-permute-start = (bf16[256,896]{1,0:T(8,128)(2,1)}, bf16[256,896]{1,0:T(8,128)(2,1)}, u32[]{:S(2)}, u32[]{:S(2)}) collective-permute-start(bf16[256,896]{1,0:T(8,128)(2,1)} %get-tuple-element.15), channel_id=1, source_target_pairs={{0,2},{1,3},{2,0},{3,1},{4,6},{5,7},{6,4},{7,5},{8,10},{9,11},{10,... | collective-permute-start | bytes 1376264 | tf_op jit(solution)/shard_map/ppermute | solution.py:333
  47.5 2.8 %collective-permute-start.1 = (bf16[256,896]{1,0:T(8,128)(2,1)}, bf16[256,896]{1,0:T(8,128)(2,1)}, u32[]{:S(2)}, u32[]{:S(2)}) collective-permute-start(bf16[256,896]{1,0:T(8,128)(2,1)} %get-tuple-element.16), channel_id=1, source_target_pairs={{0,3},{1,0},{2,1},{3,2},{4,7},{5,4},{6,5},{7,6},{8,11},{9,8},{10,9... | collective-permute-start | bytes 1376264 | tf_op jit(solution)/shard_map/ppermute | solution.py:333
  50.3 2.5 %collective-permute-start.2 = (bf16[256,896]{1,0:T(8,128)(2,1)}, bf16[256,896]{1,0:T(8,128)(2,1)}, u32[]{:S(2)}, u32[]{:S(2)}) collective-permute-start(bf16[256,896]{1,0:T(8,128)(2,1)} %get-tuple-element.17), channel_id=1, source_target_pairs={{0,1},{1,2},{2,3},{3,0},{4,5},{5,6},{6,7},{7,4},{8,9},{9,10},{10,1... | collective-permute-start | bytes 1376264 | tf_op jit(solution)/shard_map/ppermute | solution.py:333
  52.8 13.3 %all-to-all-done.1 = bf16[32,16,896]{2,1,0:T(8,128)(2,1)S(1)} async-done(((bf16[32,16,896]{2,1,0:T(8,128)(2,1)}), bf16[32,16,896]{2,1,0:T(8,128)(2,1)S(1)}, u32[]{:S(2)}, u32[]{:S(2)}) %all-to-all-start.1) | async-done | bytes 917536 | tf_op jit(solution)/shard_map/all_to_all | solution.py:358
  66.1 1.2 up_parts.1
  67.4 0.9 collective-permute-done.1.w1
  68.2 0.4 collective-permute-done.2.w3
  68.6 18.1 %all_to_all.30.part_ref = bf16[4,1024,128]{2,1,0:T(8,128)(2,1)S(1)} all-to-all(bf16[4,1024,128]{2,1,0:T(8,128)(2,1)S(1)} %up_parts.1), channel_id=1, replica_groups=mesh['zh'=4,'zl'=4,'y'=4,'c'=2,'tp'=4] {'tp'}, dimensions={0} | all-to-all | bytes 2097152 | tf_op jit(solution)/shard_map/all_to_all | solution.py:364
  86.7 0.2 hidden_copies.1
  87.0 15.4 %all_to_all.31.hidden_ref = bf16[4,1024,128]{2,1,0:T(8,128)(2,1)S(1)} all-to-all(bf16[4,1024,128]{2,1,0:T(8,128)(2,1)S(1)} %hidden_copies.1), channel_id=1, replica_groups=mesh['zh'=4,'zl'=4,'y'=4,'c'=2,'tp'=4] {'tp'}, dimensions={0} | all-to-all | bytes 2097152 | tf_op jit(solution)/shard_map/all_to_all | solution.py:365
  102.4 3.4 %down_rows.1 = bf16[512,896]{1,0:T(8,128)(2,1)} custom-call(s32[1]{0:T(128)} %bitcast.x_ref, bf16[4,1024,128]{2,1,0:T(8,128)(2,1)S(1)} %all_to_all.31.hidden_ref, bf16[256,3584]{1,0:T(8,128)(2,1)S(1)} %bitcast.28, bf16[256,896]{1,0:T(8,128)(2,1)} %collective-permute-done.1.w1, bf16[256,896]{1,0:T(8,128)(2,1)} %collective-permute-done.w2, ...), custom_call_target="tpu_custom_call" | custom-call | flops 939524096 | bytes 3801088 | tf_op jit(solution)/shard_map/down_rows/pallas_call | solution.py:262
  105.9 10.6 %all-to-all-start.4 = ((bf16[32,16,896]{2,1,0:T(8,128)(2,1)}), bf16[32,16,896]{2,1,0:T(8,128)(2,1)S(1)}, u32[]{:S(2)}, u32[]{:S(2)}) async-start(bf16[32,16,896]{2,1,0:T(8,128)(2,1)} %bitcast.9), calls=%async_computation.4 | async-start | bytes 1835008 | tf_op jit(solution)/shard_map/all_to_all | solution.py:368
  116.5 2.3 %collective-permute-start.3 = (bf16[2,32,576]{2,1,0:T(8,128)(2,1)S(1)}, bf16[2,32,576]{2,1,0:T(8,128)(2,1)S(1)}, u32[]{:S(2)}, u32[]{:S(2)}) collective-permute-start(bf16[2,32,576]{2,1,0:T(8,128)(2,1)S(1)} %copy-done.3), channel_id=1, source_target_pairs={{0,1},{1,2},{2,3},{3,0},{4,5},{5,6},{6,7},{7,4},{8,9},{9,10},{10,1... | collective-permute-start | bytes 221192 | tf_op jit(solution)/shard_map/ppermute | solution.py:333
  118.9 3.7 %collective-permute-start.4 = (bf16[2,32,576]{2,1,0:T(8,128)(2,1)S(1)}, bf16[2,32,576]{2,1,0:T(8,128)(2,1)S(1)}, u32[]{:S(2)}, u32[]{:S(2)}) collective-permute-start(bf16[2,32,576]{2,1,0:T(8,128)(2,1)S(1)} %copy-done.3), channel_id=1, source_target_pairs={{0,2},{1,3},{2,0},{3,1},{4,6},{5,7},{6,4},{7,5},{8,10},{9,11},{10,... | collective-permute-start | bytes 221192 | tf_op jit(solution)/shard_map/ppermute | solution.py:333
  122.6 2.5 %collective-permute-start.5 = (bf16[2,32,576]{2,1,0:T(8,128)(2,1)S(1)}, bf16[2,32,576]{2,1,0:T(8,128)(2,1)S(1)}, u32[]{:S(2)}, u32[]{:S(2)}) collective-permute-start(bf16[2,32,576]{2,1,0:T(8,128)(2,1)S(1)} %copy-done.3), channel_id=1, source_target_pairs={{0,3},{1,0},{2,1},{3,2},{4,7},{5,4},{6,5},{7,6},{8,11},{9,8},{10,9... | collective-permute-start | bytes 221192 | tf_op jit(solution)/shard_map/ppermute | solution.py:333
  125.1 0.1 slice_convert_fusion
  125.4 0.1 fusion.1
  125.5 0.1 copy.32
  125.7 0.1 compare_reduce_fusion
  125.8 0.2 fusion
  126.0 0.1 copy.30
  126.2 0.1 eq.62
  126.3 0.1 copy.34
  126.6 0.1 pad_add_fusion.place_ref
  126.6 1.4 collective-permute-done.5.q3
  128.0 1.7 attend_own.1
  129.7 10.2 %all-to-all-done.4 = bf16[32,16,896]{2,1,0:T(8,128)(2,1)S(1)} async-done(((bf16[32,16,896]{2,1,0:T(8,128)(2,1)}), bf16[32,16,896]{2,1,0:T(8,128)(2,1)S(1)}, u32[]{:S(2)}, u32[]{:S(2)}) %all-to-all-start.4) | async-done | bytes 917536 | tf_op jit(solution)/shard_map/all_to_all | solution.py:368
  139.9 1.1 mixed_rows.1
  141.0 6.4 %all-to-all-start.5 = ((bf16[4,224,128]{2,1,0:T(8,128)(2,1)}), bf16[4,224,128]{2,1,0:T(8,128)(2,1)S(1)}, u32[]{:S(2)}, u32[]{:S(2)}) async-start(bf16[4,224,128]{2,1,0:T(8,128)(2,1)} %mixed_rows.1), calls=%async_computation.5 | async-start | bytes 458752 | tf_op jit(solution)/shard_map/all_to_all | solution.py:376
  147.4 2.2 %collective-permute-start.8 = (bf16[2,32,640]{2,1,0:T(8,128)(2,1)S(1)}, bf16[2,32,640]{2,1,0:T(8,128)(2,1)S(1)}, u32[]{:S(2)}, u32[]{:S(2)}) collective-permute-start(bf16[2,32,640]{2,1,0:T(8,128)(2,1)S(1)} %get-tuple-element.41), channel_id=1, source_target_pairs={{0,1},{1,2},{2,3},{3,0},{4,5},{5,6},{6,7},{7,4},{8,9},{9,10},{10,1... | collective-permute-start | bytes 245768 | tf_op jit(solution)/shard_map/ppermute | solution.py:333
  149.7 3.7 %collective-permute-start.7 = (bf16[2,32,640]{2,1,0:T(8,128)(2,1)S(1)}, bf16[2,32,640]{2,1,0:T(8,128)(2,1)S(1)}, u32[]{:S(2)}, u32[]{:S(2)}) collective-permute-start(bf16[2,32,640]{2,1,0:T(8,128)(2,1)S(1)} %get-tuple-element.42), channel_id=1, source_target_pairs={{0,2},{1,3},{2,0},{3,1},{4,6},{5,7},{6,4},{7,5},{8,10},{9,11},{10,... | collective-permute-start | bytes 245768 | tf_op jit(solution)/shard_map/ppermute | solution.py:333
  153.3 2.5 %collective-permute-start.6 = (bf16[2,32,640]{2,1,0:T(8,128)(2,1)S(1)}, bf16[2,32,640]{2,1,0:T(8,128)(2,1)S(1)}, u32[]{:S(2)}, u32[]{:S(2)}) collective-permute-start(bf16[2,32,640]{2,1,0:T(8,128)(2,1)S(1)} %get-tuple-element.43), channel_id=1, source_target_pairs={{0,3},{1,0},{2,1},{3,2},{4,7},{5,4},{6,5},{7,6},{8,11},{9,8},{10,9... | collective-permute-start | bytes 245768 | tf_op jit(solution)/shard_map/ppermute | solution.py:333
  155.9 1.6 collective-permute-done.7
  157.5 1.9 %collective-permute-done.6 = bf16[2,32,640]{2,1,0:T(8,128)(2,1)S(1)} collective-permute-done((bf16[2,32,640]{2,1,0:T(8,128)(2,1)S(1)}, bf16[2,32,640]{2,1,0:T(8,128)(2,1)S(1)}, u32[]{:S(2)}, u32[]{:S(2)}) %collective-permute-start.6) | collective-permute-done | bytes 81952 | tf_op jit(solution)/shard_map/ppermute | solution.py:333
  159.4 0.2 add_add_fusion
  159.7 0.1 divide_reduce_fusion.3
  159.8 0.8 add_convert_fusion
  160.5 6.1 %all-to-all-done.5.parts_ref = bf16[4,224,128]{2,1,0:T(8,128)(2,1)S(1)} async-done(((bf16[4,224,128]{2,1,0:T(8,128)(2,1)}), bf16[4,224,128]{2,1,0:T(8,128)(2,1)S(1)}, u32[]{:S(2)}, u32[]{:S(2)}) %all-to-all-start.5) | async-done | bytes 229408 | tf_op jit(solution)/shard_map/all_to_all | solution.py:376
  166.7 0.7 summed.1
  (41 shorter events, 0.5 us)
Async XLA Ops:
  0.6 4.4 %copy-start = (bf16[32,3584]{1,0:T(8,128)(2,1)S(1)}, bf16[32,3584]{1,0:T(8,128)(2,1)}, u32[]{:S(2)}) copy-start(bf16[32,3584]{1,0:T(8,128)(2,1)} %param.11) | copy-start | bytes 688132
  0.6 4.2 %copy-start.4 = (f32[32,8]{0,1:T(8,128)S(1)}, f32[32,8]{0,1:T(8,128)}, u32[]{:S(2)}) copy-start(f32[32,8]{0,1:T(8,128)} %param.13) | copy-start | bytes 3076
  0.7 4.3 %copy-start.5 = (s32[32,8]{0,1:T(8,128)S(1)}, s32[32,8]{0,1:T(8,128)}, u32[]{:S(2)}) copy-start(s32[32,8]{0,1:T(8,128)} %param.12) | copy-start | bytes 3076
  0.7 32.8 %all-to-all-start = ((bf16[4,896,256]{2,1,0:T(8,128)(2,1)}), bf16[4,896,256]{2,1,0:T(8,128)(2,1)S(1)}, u32[]{:S(2)}, u32[]{:S(2)}) async-start(bf16[4,896,256]{2,1,0:T(8,128)(2,1)} %bitcast.32), calls=%async_computation | async-start | bytes 3670016 | tf_op jit(solution)/shard_map/all_to_all | solution.py:346
  33.4 32.6 %all-to-all-start.1 = ((bf16[32,16,896]{2,1,0:T(8,128)(2,1)}), bf16[32,16,896]{2,1,0:T(8,128)(2,1)S(1)}, u32[]{:S(2)}, u32[]{:S(2)}) async-start(bf16[32,16,896]{2,1,0:T(8,128)(2,1)} %bitcast.6), calls=%async_computation.1 | async-start | bytes 1835008 | tf_op jit(solution)/shard_map/all_to_all | solution.py:358
  42.6 24.8 %collective-permute-start = (bf16[256,896]{1,0:T(8,128)(2,1)}, bf16[256,896]{1,0:T(8,128)(2,1)}, u32[]{:S(2)}, u32[]{:S(2)}) collective-permute-start(bf16[256,896]{1,0:T(8,128)(2,1)} %get-tuple-element.15), channel_id=1, source_target_pairs={{0,2},{1,3},{2,0},{3,1},{4,6},{5,7},{6,4},{7,5},{8,10},{9,11},{10,... | collective-permute-start | bytes 1376264 | tf_op jit(solution)/shard_map/ppermute | solution.py:333
  47.5 20.7 %collective-permute-start.1 = (bf16[256,896]{1,0:T(8,128)(2,1)}, bf16[256,896]{1,0:T(8,128)(2,1)}, u32[]{:S(2)}, u32[]{:S(2)}) collective-permute-start(bf16[256,896]{1,0:T(8,128)(2,1)} %get-tuple-element.16), channel_id=1, source_target_pairs={{0,3},{1,0},{2,1},{3,2},{4,7},{5,4},{6,5},{7,6},{8,11},{9,8},{10,9... | collective-permute-start | bytes 1376264 | tf_op jit(solution)/shard_map/ppermute | solution.py:333
  50.3 18.3 %collective-permute-start.2 = (bf16[256,896]{1,0:T(8,128)(2,1)}, bf16[256,896]{1,0:T(8,128)(2,1)}, u32[]{:S(2)}, u32[]{:S(2)}) collective-permute-start(bf16[256,896]{1,0:T(8,128)(2,1)} %get-tuple-element.17), channel_id=1, source_target_pairs={{0,1},{1,2},{2,3},{3,0},{4,5},{5,6},{6,7},{7,4},{8,9},{9,10},{10,1... | collective-permute-start | bytes 1376264 | tf_op jit(solution)/shard_map/ppermute | solution.py:333
  86.7 15.7 %copy-start.1 = (bf16[1,256,3584]{2,1,0:T(8,128)(2,1)S(1)}, bf16[1,256,3584]{2,1,0:T(8,128)(2,1)}, u32[]{:S(2)}) copy-start(bf16[1,256,3584]{2,1,0:T(8,128)(2,1)} %param.15) | copy-start | bytes 5505028
  105.9 10.6 %copy-start.3 = (bf16[2,32,576]{2,1,0:T(8,128)(2,1)S(1)}, bf16[2,32,576]{2,1,0:T(8,128)(2,1)}, u32[]{:S(2)}) copy-start(bf16[2,32,576]{2,1,0:T(8,128)(2,1)} %q0.1) | copy-start | bytes 221188
  105.9 34.0 %all-to-all-start.4 = ((bf16[32,16,896]{2,1,0:T(8,128)(2,1)}), bf16[32,16,896]{2,1,0:T(8,128)(2,1)S(1)}, u32[]{:S(2)}, u32[]{:S(2)}) async-start(bf16[32,16,896]{2,1,0:T(8,128)(2,1)} %bitcast.9), calls=%async_computation.4 | async-start | bytes 1835008 | tf_op jit(solution)/shard_map/all_to_all | solution.py:368
  116.5 10.0 %copy-start.6 = (s32[2]{0:T(128)S(1)}, s32[2]{0:T(128)}, u32[]{:S(2)}) copy-start(s32[2]{0:T(128)} %param.10) | copy-start | bytes 28
  116.5 11.5 %copy-start.2 = (bf16[2,256,576]{1,2,0:T(8,128)(2,1)S(1)}, bf16[2,256,576]{1,2,0:T(8,128)(2,1)}, u32[]{:S(2)}) copy-start(bf16[2,256,576]{1,2,0:T(8,128)(2,1)} %param.9) | copy-start | bytes 1769476
  116.5 10.1 %collective-permute-start.3 = (bf16[2,32,576]{2,1,0:T(8,128)(2,1)S(1)}, bf16[2,32,576]{2,1,0:T(8,128)(2,1)S(1)}, u32[]{:S(2)}, u32[]{:S(2)}) collective-permute-start(bf16[2,32,576]{2,1,0:T(8,128)(2,1)S(1)} %copy-done.3), channel_id=1, source_target_pairs={{0,1},{1,2},{2,3},{3,0},{4,5},{5,6},{6,7},{7,4},{8,9},{9,10},{10,1... | collective-permute-start | bytes 221192 | tf_op jit(solution)/shard_map/ppermute | solution.py:333
  118.9 7.8 %collective-permute-start.4 = (bf16[2,32,576]{2,1,0:T(8,128)(2,1)S(1)}, bf16[2,32,576]{2,1,0:T(8,128)(2,1)S(1)}, u32[]{:S(2)}, u32[]{:S(2)}) collective-permute-start(bf16[2,32,576]{2,1,0:T(8,128)(2,1)S(1)} %copy-done.3), channel_id=1, source_target_pairs={{0,2},{1,3},{2,0},{3,1},{4,6},{5,7},{6,4},{7,5},{8,10},{9,11},{10,... | collective-permute-start | bytes 221192 | tf_op jit(solution)/shard_map/ppermute | solution.py:333
  122.6 5.5 %collective-permute-start.5 = (bf16[2,32,576]{2,1,0:T(8,128)(2,1)S(1)}, bf16[2,32,576]{2,1,0:T(8,128)(2,1)S(1)}, u32[]{:S(2)}, u32[]{:S(2)}) collective-permute-start(bf16[2,32,576]{2,1,0:T(8,128)(2,1)S(1)} %copy-done.3), channel_id=1, source_target_pairs={{0,3},{1,0},{2,1},{3,2},{4,7},{5,4},{6,5},{7,6},{8,11},{9,8},{10,9... | collective-permute-start | bytes 221192 | tf_op jit(solution)/shard_map/ppermute | solution.py:333
  141.0 25.6 %all-to-all-start.5 = ((bf16[4,224,128]{2,1,0:T(8,128)(2,1)}), bf16[4,224,128]{2,1,0:T(8,128)(2,1)S(1)}, u32[]{:S(2)}, u32[]{:S(2)}) async-start(bf16[4,224,128]{2,1,0:T(8,128)(2,1)} %mixed_rows.1), calls=%async_computation.5 | async-start | bytes 458752 | tf_op jit(solution)/shard_map/all_to_all | solution.py:376
  147.4 8.5 %collective-permute-start.8 = (bf16[2,32,640]{2,1,0:T(8,128)(2,1)S(1)}, bf16[2,32,640]{2,1,0:T(8,128)(2,1)S(1)}, u32[]{:S(2)}, u32[]{:S(2)}) collective-permute-start(bf16[2,32,640]{2,1,0:T(8,128)(2,1)S(1)} %get-tuple-element.41), channel_id=1, source_target_pairs={{0,1},{1,2},{2,3},{3,0},{4,5},{5,6},{6,7},{7,4},{8,9},{9,10},{10,1... | collective-permute-start | bytes 245768 | tf_op jit(solution)/shard_map/ppermute | solution.py:333
  149.7 7.8 %collective-permute-start.7 = (bf16[2,32,640]{2,1,0:T(8,128)(2,1)S(1)}, bf16[2,32,640]{2,1,0:T(8,128)(2,1)S(1)}, u32[]{:S(2)}, u32[]{:S(2)}) collective-permute-start(bf16[2,32,640]{2,1,0:T(8,128)(2,1)S(1)} %get-tuple-element.42), channel_id=1, source_target_pairs={{0,2},{1,3},{2,0},{3,1},{4,6},{5,7},{6,4},{7,5},{8,10},{9,11},{10,... | collective-permute-start | bytes 245768 | tf_op jit(solution)/shard_map/ppermute | solution.py:333
  153.3 6.1 %collective-permute-start.6 = (bf16[2,32,640]{2,1,0:T(8,128)(2,1)S(1)}, bf16[2,32,640]{2,1,0:T(8,128)(2,1)S(1)}, u32[]{:S(2)}, u32[]{:S(2)}) collective-permute-start(bf16[2,32,640]{2,1,0:T(8,128)(2,1)S(1)} %get-tuple-element.43), channel_id=1, source_target_pairs={{0,3},{1,0},{2,1},{3,2},{4,7},{5,4},{6,5},{7,6},{8,11},{9,8},{10,9... | collective-permute-start | bytes 245768 | tf_op jit(solution)/shard_map/ppermute | solution.py:333

commit v6 on v4

--- a/solution.py
+++ b/solution.py
@@ -221,12 +221,15 @@
     return weight_ref.at[:, pl.ds(pl.multiple_of(place * cols, LANES), cols)]
 
 
-def down_kernel(x_ref, hidden_ref, weight_ref, w1, w2, w3, out_ref, near, held, near_sems, sems):
+def down_kernel(x_ref, hidden_ref, weight_ref, w1, low, high, w3, out_ref, near, held, near_sems, sems):
     groups, count = hidden_ref.shape[0], held.shape[0]
     step = count // sems.shape[0]
     place = [lax.rem(x_ref[0] + k, groups) for k in range(groups)]
-    sources = [columns_at(weight_ref, x_ref[0], near.shape[2]), w1, w2, w3]
-    fetches = [pltpu.make_async_copy(source, near.at[k], near_sems.at[k]) for k, source in enumerate(sources)]
+    half = low.shape[0]
+    own = columns_at(weight_ref, x_ref[0], near.shape[2])
+    parts = [(own, near.at[0]), (w1, near.at[1]), (w3, near.at[3])]
+    parts = parts + [(low, near.at[2, pl.ds(0, half)]), (high, near.at[2, pl.ds(half, half)])]
+    fetches = [pltpu.make_async_copy(*pair, near_sems.at[i]) for i, pair in enumerate(parts)]
     for fetch in fetches:
         fetch.start()
     copies = []
@@ -239,9 +242,10 @@
     for i in range(sems.shape[0]):
         rows = pl.ds(i * step, step)
         total = None
-        for k in range(groups):
+        for step_at, k in enumerate((0, 1, 3, 2)):
             if i == 0:
-                fetches[k].wait()
+                for fetch in fetches[step_at:] if k == 2 else fetches[step_at : step_at + 1]:
+                    fetch.wait()
             total = part(k, i) if k == 0 else total + part(k, i)
         held[rows] = total.astype(BF)
         copies.append(pltpu.make_async_copy(held.at[rows], out_ref.at[rows], sems.at[i]))
@@ -250,25 +254,25 @@
         copy.wait()
 
 
-def down_rows(x, hidden, weight, after, far, before):
+def down_rows(x, hidden, weight, after, low, high, before):
     width, cols = after.shape
     groups, lines, _ = hidden.shape
     out = jax.ShapeDtypeStruct((lines * LANES // width, cols), BF)
     return pl.pallas_call(
         down_kernel,
         out_shape=out,
-        in_specs=[pl.BlockSpec(memory_space=pltpu.SMEM), INSIDE] + [OUTSIDE] * 4,
+        in_specs=[pl.BlockSpec(memory_space=pltpu.SMEM), INSIDE] + [OUTSIDE] * 5,
         out_specs=OUTSIDE,
         scratch_shapes=[
             pltpu.VMEM((groups, width, cols), BF),
             pltpu.VMEM(out.shape, BF),
-            pltpu.SemaphoreType.DMA((groups,)),
+            pltpu.SemaphoreType.DMA((groups + 1,)),
             pltpu.SemaphoreType.DMA((2,)),
         ],
         compiler_params=pltpu.CompilerParams(vmem_limit_bytes=VMEM),
         cost_estimate=cost(2 * hidden.size * cols, hidden, after, after, after, after, out),
         name="down_rows",
-    )(x.reshape(1), hidden, weight, after, far, before)
+    )(x.reshape(1), hidden, weight, after, low, high, before)
 
 
 def mix_kernel(take_ref, rows_ref, out_ref, held, sem):
@@ -347,18 +351,25 @@
     outgoing = placed_rows(first, packed, rows, near, slots)
 
     weight = down_weight[0]
-    cut = [lax.dynamic_slice_in_dim(weight, (x + k) % tp * cols, cols, 1) for k in (2, 1, tp - 1)]
+    half = group // 2
+
+    def columns_for(k, first_row, count):
+        return lax.dynamic_slice(weight, (first_row, (x + k) % tp * cols), (count, cols))
+
+    cut = [columns_for(2, 0, half), columns_for(2, half, half), columns_for(1, 0, group), columns_for(tp - 1, 0, group)]
     outgoing, up, cut = lax.optimization_barrier((outgoing, up, cut))
-    far, before, after = (shift(block, k, tp) for block, k in zip(cut, (2, 1, tp - 1)))
+    low, high = shift(cut[0], 1, tp), shift(cut[1], tp - 1, tp)
+    before, after = shift(cut[2], 1, tp), shift(cut[3], tp - 1, tp)
+    low, high = shift(low, 1, tp), shift(high, tp - 1, tp)
     received = lax.all_to_all(outgoing.reshape(near, slots, cols), NEAR, 0, 0, tiled=True)
     received = received.reshape(near * slots, cols)
     take = shares(packed[:, cols:], rows, first, near, away)
 
     part = up_parts(received, up)
-    part, far, after, before = lax.optimization_barrier((part, far, after, before))
+    part, low, high, after, before = lax.optimization_barrier((part, low, high, after, before))
     part = lax.all_to_all(part, "tp", 0, 0, tiled=True)
     hidden = lax.all_to_all(hidden_copies(part), "tp", 0, 0, tiled=True)
-    output = down_rows(x, hidden, weight, after, far, before)
+    output = down_rows(x, hidden, weight, after, low, high, before)
 
     returned = lax.all_to_all(output.reshape(near, slots, cols), NEAR, 0, 0, tiled=True)
 

time: 168 us -> 168 us (level)
  starting transfers between devices: 57.9 us -> 67.4 us
  waiting for transfers between devices: 35.4 us -> 30.2 us
  blocking collectives: 57.2 us -> 53 us
    all_to_all x1, waiting for transfers between devices: 13.8 us -> 5.65 us  [shards(): lax.all_to_all(outgoing.reshape(near, slots, cols), NEAR, 0, 0, tiled=True)]
    ppermute x9 -> x12, starting transfers between devices: 27.2 us -> 35.3 us  [shift(): return lax.ppermute(array, 'tp', [(i, (i + by) % tp) for i in range(tp)])]
    all_to_all x1, blocking collectives: 18.1 us -> 15.1 us  [shards(): part = lax.all_to_all(part, 'tp', 0, 0, tiled=True)]
    ppermute x9 -> x12, waiting for transfers between devices: 5.3 us -> 8.26 us  [shift(): return lax.ppermute(array, 'tp', [(i, (i + by) % tp) for i in range(tp)])]
  transfers between devices with their start and end apart: 13 -> 16, of which waited for: 8 -> 7; matrix products, arithmetic and copies ran while one was open for 3% -> 3% of each run, Pallas kernels for 3% -> 3%
where the time goes in v6:
time: 168 us; the launch traced here: 167 us
  starting transfers between devices  67.4 us (40%)
  blocking collectives  53 us (32%)
  waiting for transfers between devices  30.2 us (18%)
  Pallas kernels  9.77 us (6%)
  local copies, waits for them, and re-layouts  3.92 us (2%)
  other arithmetic  1.75 us (1%)
    ppermute x12, starting transfers between devices, shift(): return lax.ppermute(array, 'tp', [(i, (i + by) % tp) for i in range(tp)])  35.3 us
    all_gather x1, blocking collectives, shards(): packed = lax.all_gather(packed, FAR, axis=0, tiled=True)  23.8 us
    all_to_all x1, blocking collectives, shards(): part = lax.all_to_all(part, 'tp', 0, 0, tiled=True)  15.1 us
    all_to_all x1, blocking collectives, shards(): hidden = lax.all_to_all(hidden_copies(part), 'tp', 0, 0, tiled=True)  14.1 us
    all_to_all x1, starting transfers between devices, shards(): lax.all_to_all(output.reshape(near, slots, cols), NEAR, 0, 0, tiled=True)  12.1 us
    all_to_all x1, waiting for transfers between devices, shards(): lax.all_to_all(output.reshape(near, slots, cols), NEAR, 0, 0, tiled=True)  10.8 us
    all_to_all x1, starting transfers between devices, shards(): lax.all_to_all(outgoing.reshape(near, slots, cols), NEAR, 0, 0, tiled=True)  9.52 us
    ppermute x12, waiting for transfers between devices, shift(): return lax.ppermute(array, 'tp', [(i, (i + by) % tp) for i in range(tp)])  8.26 us
  transfers between devices with their start and end apart: 16, of which 7 were waited for; matrix products, arithmetic and copies ran while one was open for 3% of the time, Pallas kernels for 3%

profile of v6, /device:TPU:33, one launch (start us, length us, event | category | flops | bytes accessed | tf_op | source)
XLA Modules:
  0.0 167.3 jit_solution(2089014905209080451)
XLA Ops:
  0.7 4.2 %all-to-all-start = ((bf16[4,896,256]{2,1,0:T(8,128)(2,1)}), bf16[4,896,256]{2,1,0:T(8,128)(2,1)S(1)}, u32[]{:S(2)}, u32[]{:S(2)}) async-start(bf16[4,896,256]{2,1,0:T(8,128)(2,1)} %bitcast.34), calls=%async_computation | async-start | bytes 3670016 | tf_op jit(solution)/shard_map/all_to_all | solution.py:345
  4.9 0.1 copy.28
  5.0 0.1 fusion.12
  5.1 0.1 concatenate.9
  5.2 23.8 %all_gather.3.packed_ref = bf16[128,1024]{1,0:T(8,128)(2,1)S(1)} all-gather(bf16[32,1024]{1,0:T(8,128)(2,1)S(1)} %concatenate.9), channel_id=1, replica_groups=mesh['zh'=4,'zl'=4,'y'=4,'c'=2,'tp'=4] {'zh'}, dimensions={0}, use_global_device_ids=true | all-gather | bytes 327680 | tf_op jit(solution)/shard_map/all_gather | solution.py:349
  29.0 1.4 placed_rows.1
  30.4 1.8 %dynamic-slice_bitcast_fusion.2 = (bf16[128,896]{1,0:T(8,128)(2,1)}, bf16[128,896]{1,0:T(8,128)(2,1)S(1)}) fusion(bf16[1,256,3584]{2,1,0:T(8,128)(2,1)} %param.15, s32[]{:T(128)S(6)} %select_n.78), kind=kLoop, calls=%fused_computation.7 | loop fusion | bytes 917508 | tf_op jit(solution)/shard_map/dynamic_slice | solution.py:357
  32.2 1.1 dynamic-slice_bitcast_fusion
  33.3 9.5 %all-to-all-start.1 = ((bf16[32,16,896]{2,1,0:T(8,128)(2,1)}), bf16[32,16,896]{2,1,0:T(8,128)(2,1)S(1)}, u32[]{:S(2)}, u32[]{:S(2)}) async-start(bf16[32,16,896]{2,1,0:T(8,128)(2,1)} %bitcast.7), calls=%async_computation.1 | async-start | bytes 1835008 | tf_op jit(solution)/shard_map/all_to_all | solution.py:364
  42.8 3.4 %collective-permute-start = (bf16[128,896]{1,0:T(8,128)(2,1)S(1)}, bf16[128,896]{1,0:T(8,128)(2,1)}, u32[]{:S(2)}, u32[]{:S(2)}) collective-permute-start(bf16[128,896]{1,0:T(8,128)(2,1)S(1)} %get-tuple-element.17), channel_id=1, source_target_pairs={{0,1},{1,2},{2,3},{3,0},{4,5},{5,6},{6,7},{7,4},{8,9},{9,10},{10,1... | collective-permute-start | bytes 688136 | tf_op jit(solution)/shard_map/ppermute | solution.py:332
  46.2 3.1 %collective-permute-start.2 = (bf16[128,896]{1,0:T(8,128)(2,1)}, bf16[128,896]{1,0:T(8,128)(2,1)}, u32[]{:S(2)}, u32[]{:S(2)}) collective-permute-start(bf16[128,896]{1,0:T(8,128)(2,1)} %get-tuple-element.18), channel_id=1, source_target_pairs={{0,3},{1,0},{2,1},{3,2},{4,7},{5,4},{6,5},{7,6},{8,11},{9,8},{10,9... | collective-permute-start | bytes 688136 | tf_op jit(solution)/shard_map/ppermute | solution.py:332
  49.4 3.4 %collective-permute-start.4 = (bf16[256,896]{1,0:T(8,128)(2,1)}, bf16[256,896]{1,0:T(8,128)(2,1)}, u32[]{:S(2)}, u32[]{:S(2)}) collective-permute-start(bf16[256,896]{1,0:T(8,128)(2,1)} %get-tuple-element.19), channel_id=1, source_target_pairs={{0,3},{1,0},{2,1},{3,2},{4,7},{5,4},{6,5},{7,6},{8,11},{9,8},{10,9... | collective-permute-start | bytes 1376264 | tf_op jit(solution)/shard_map/ppermute | solution.py:332
  52.7 1.9 %collective-permute-start.5 = (bf16[256,896]{1,0:T(8,128)(2,1)}, bf16[256,896]{1,0:T(8,128)(2,1)}, u32[]{:S(2)}, u32[]{:S(2)}) collective-permute-start(bf16[256,896]{1,0:T(8,128)(2,1)} %get-tuple-element.20), channel_id=1, source_target_pairs={{0,1},{1,2},{2,3},{3,0},{4,5},{5,6},{6,7},{7,4},{8,9},{9,10},{10,1... | collective-permute-start | bytes 1376264 | tf_op jit(solution)/shard_map/ppermute | solution.py:332
  54.7 2.2 %collective-permute-start.1 = (bf16[128,896]{1,0:T(8,128)(2,1)}, bf16[128,896]{1,0:T(8,128)(2,1)S(1)}, u32[]{:S(2)}, u32[]{:S(2)}) collective-permute-start(bf16[128,896]{1,0:T(8,128)(2,1)} %collective-permute-done), channel_id=1, source_target_pairs={{0,1},{1,2},{2,3},{3,0},{4,5},{5,6},{6,7},{7,4},{8,9},{9,10},{10,1... | collective-permute-start | bytes 688136 | tf_op jit(solution)/shard_map/ppermute | solution.py:332
  56.8 4.3 %collective-permute-start.3 = (bf16[128,896]{1,0:T(8,128)(2,1)}, bf16[128,896]{1,0:T(8,128)(2,1)}, u32[]{:S(2)}, u32[]{:S(2)}) collective-permute-start(bf16[128,896]{1,0:T(8,128)(2,1)} %collective-permute-done.2), channel_id=1, source_target_pairs={{0,3},{1,0},{2,1},{3,2},{4,7},{5,4},{6,5},{7,6},{8,11},{9,8},{10,9... | collective-permute-start | bytes 688136 | tf_op jit(solution)/shard_map/ppermute | solution.py:332
  61.2 5.6 %all-to-all-done.1 = bf16[32,16,896]{2,1,0:T(8,128)(2,1)S(1)} async-done(((bf16[32,16,896]{2,1,0:T(8,128)(2,1)}), bf16[32,16,896]{2,1,0:T(8,128)(2,1)S(1)}, u32[]{:S(2)}, u32[]{:S(2)}) %all-to-all-start.1) | async-done | bytes 917536 | tf_op jit(solution)/shard_map/all_to_all | solution.py:364
  66.8 1.2 up_parts.1
  68.1 3.7 %collective-permute-done.1.low = bf16[128,896]{1,0:T(8,128)(2,1)S(1)} collective-permute-done((bf16[128,896]{1,0:T(8,128)(2,1)}, bf16[128,896]{1,0:T(8,128)(2,1)S(1)}, u32[]{:S(2)}, u32[]{:S(2)}) %collective-permute-start.1) | collective-permute-done | bytes 229408 | tf_op jit(solution)/shard_map/ppermute | solution.py:332
  71.8 15.1 %all_to_all.30.part_ref = bf16[4,1024,128]{2,1,0:T(8,128)(2,1)S(1)} all-to-all(bf16[4,1024,128]{2,1,0:T(8,128)(2,1)S(1)} %up_parts.1), channel_id=1, replica_groups=mesh['zh'=4,'zl'=4,'y'=4,'c'=2,'tp'=4] {'tp'}, dimensions={0} | all-to-all | bytes 2097152 | tf_op jit(solution)/shard_map/all_to_all | solution.py:370
  86.9 0.2 hidden_copies.1
  87.2 14.1 %all_to_all.31.hidden_ref = bf16[4,1024,128]{2,1,0:T(8,128)(2,1)S(1)} all-to-all(bf16[4,1024,128]{2,1,0:T(8,128)(2,1)S(1)} %hidden_copies.1), channel_id=1, replica_groups=mesh['zh'=4,'zl'=4,'y'=4,'c'=2,'tp'=4] {'tp'}, dimensions={0} | all-to-all | bytes 2097152 | tf_op jit(solution)/shard_map/all_to_all | solution.py:371
  101.2 3.5 %down_rows.1 = bf16[512,896]{1,0:T(8,128)(2,1)} custom-call(s32[1]{0:T(128)} %bitcast.x_ref, bf16[4,1024,128]{2,1,0:T(8,128)(2,1)S(1)} %all_to_all.31.hidden_ref, bf16[256,3584]{1,0:T(8,128)(2,1)S(1)} %bitcast.30, bf16[256,896]{1,0:T(8,128)(2,1)} %collective-permute-done.4.w1, bf16[128,896]{1,0:T(8,128)(2,1)S(1)} %collective-permute-done.1.low, ...), custom_call_target="tpu_custom_call" | custom-call | flops 939524096 | bytes 3801088 | tf_op jit(solution)/shard_map/down_rows/pallas_call | solution.py:261
  104.7 12.1 %all-to-all-start.4 = ((bf16[32,16,896]{2,1,0:T(8,128)(2,1)}), bf16[32,16,896]{2,1,0:T(8,128)(2,1)S(1)}, u32[]{:S(2)}, u32[]{:S(2)}) async-start(bf16[32,16,896]{2,1,0:T(8,128)(2,1)} %bitcast.10), calls=%async_computation.4 | async-start | bytes 1835008 | tf_op jit(solution)/shard_map/all_to_all | solution.py:374
  116.8 2.3 %collective-permute-start.6 = (bf16[2,32,576]{2,1,0:T(8,128)(2,1)S(1)}, bf16[2,32,576]{2,1,0:T(8,128)(2,1)S(1)}, u32[]{:S(2)}, u32[]{:S(2)}) collective-permute-start(bf16[2,32,576]{2,1,0:T(8,128)(2,1)S(1)} %copy-done.4), channel_id=1, source_target_pairs={{0,1},{1,2},{2,3},{3,0},{4,5},{5,6},{6,7},{7,4},{8,9},{9,10},{10,1... | collective-permute-start | bytes 221192 | tf_op jit(solution)/shard_map/ppermute | solution.py:332
  119.1 3.7 %collective-permute-start.7 = (bf16[2,32,576]{2,1,0:T(8,128)(2,1)S(1)}, bf16[2,32,576]{2,1,0:T(8,128)(2,1)S(1)}, u32[]{:S(2)}, u32[]{:S(2)}) collective-permute-start(bf16[2,32,576]{2,1,0:T(8,128)(2,1)S(1)} %copy-done.4), channel_id=1, source_target_pairs={{0,2},{1,3},{2,0},{3,1},{4,6},{5,7},{6,4},{7,5},{8,10},{9,11},{10,... | collective-permute-start | bytes 221192 | tf_op jit(solution)/shard_map/ppermute | solution.py:332
  122.8 2.5 %collective-permute-start.8 = (bf16[2,32,576]{2,1,0:T(8,128)(2,1)S(1)}, bf16[2,32,576]{2,1,0:T(8,128)(2,1)S(1)}, u32[]{:S(2)}, u32[]{:S(2)}) collective-permute-start(bf16[2,32,576]{2,1,0:T(8,128)(2,1)S(1)} %copy-done.4), channel_id=1, source_target_pairs={{0,3},{1,0},{2,1},{3,2},{4,7},{5,4},{6,5},{7,6},{8,11},{9,8},{10,9... | collective-permute-start | bytes 221192 | tf_op jit(solution)/shard_map/ppermute | solution.py:332
  125.4 0.1 slice_convert_fusion
  125.7 0.1 fusion.1
  125.8 0.1 copy.32
  125.9 0.1 compare_reduce_fusion
  126.0 0.2 fusion
  126.3 0.1 copy.30
  126.6 0.1 copy.34
  126.9 1.4 collective-permute-done.8.q3
  128.3 1.7 attend_own.1
  130.0 10.8 %all-to-all-done.4 = bf16[32,16,896]{2,1,0:T(8,128)(2,1)S(1)} async-done(((bf16[32,16,896]{2,1,0:T(8,128)(2,1)}), bf16[32,16,896]{2,1,0:T(8,128)(2,1)S(1)}, u32[]{:S(2)}, u32[]{:S(2)}) %all-to-all-start.4) | async-done | bytes 917536 | tf_op jit(solution)/shard_map/all_to_all | solution.py:374
  140.8 1.1 mixed_rows.1
  141.9 6.4 %all-to-all-start.5 = ((bf16[4,224,128]{2,1,0:T(8,128)(2,1)}), bf16[4,224,128]{2,1,0:T(8,128)(2,1)S(1)}, u32[]{:S(2)}, u32[]{:S(2)}) async-start(bf16[4,224,128]{2,1,0:T(8,128)(2,1)} %mixed_rows.1), calls=%async_computation.5 | async-start | bytes 458752 | tf_op jit(solution)/shard_map/all_to_all | solution.py:382
  148.3 2.2 %collective-permute-start.11 = (bf16[2,32,640]{2,1,0:T(8,128)(2,1)S(1)}, bf16[2,32,640]{2,1,0:T(8,128)(2,1)S(1)}, u32[]{:S(2)}, u32[]{:S(2)}) collective-permute-start(bf16[2,32,640]{2,1,0:T(8,128)(2,1)S(1)} %get-tuple-element.46), channel_id=1, source_target_pairs={{0,1},{1,2},{2,3},{3,0},{4,5},{5,6},{6,7},{7,4},{8,9},{9,10},{10,1... | collective-permute-start | bytes 245768 | tf_op jit(solution)/shard_map/ppermute | solution.py:332
  150.5 3.7 %collective-permute-start.10 = (bf16[2,32,640]{2,1,0:T(8,128)(2,1)S(1)}, bf16[2,32,640]{2,1,0:T(8,128)(2,1)S(1)}, u32[]{:S(2)}, u32[]{:S(2)}) collective-permute-start(bf16[2,32,640]{2,1,0:T(8,128)(2,1)S(1)} %get-tuple-element.47), channel_id=1, source_target_pairs={{0,2},{1,3},{2,0},{3,1},{4,6},{5,7},{6,4},{7,5},{8,10},{9,11},{10,... | collective-permute-start | bytes 245768 | tf_op jit(solution)/shard_map/ppermute | solution.py:332
  154.2 2.6 %collective-permute-start.9 = (bf16[2,32,640]{2,1,0:T(8,128)(2,1)S(1)}, bf16[2,32,640]{2,1,0:T(8,128)(2,1)S(1)}, u32[]{:S(2)}, u32[]{:S(2)}) collective-permute-start(bf16[2,32,640]{2,1,0:T(8,128)(2,1)S(1)} %get-tuple-element.48), channel_id=1, source_target_pairs={{0,3},{1,0},{2,1},{3,2},{4,7},{5,4},{6,5},{7,6},{8,11},{9,8},{10,9... | collective-permute-start | bytes 245768 | tf_op jit(solution)/shard_map/ppermute | solution.py:332
  156.8 1.3 collective-permute-done.10
  158.1 1.9 %collective-permute-done.9 = bf16[2,32,640]{2,1,0:T(8,128)(2,1)S(1)} collective-permute-done((bf16[2,32,640]{2,1,0:T(8,128)(2,1)S(1)}, bf16[2,32,640]{2,1,0:T(8,128)(2,1)S(1)}, u32[]{:S(2)}, u32[]{:S(2)}) %collective-permute-start.9) | collective-permute-done | bytes 81952 | tf_op jit(solution)/shard_map/ppermute | solution.py:332
  160.0 0.2 add_add_fusion
  160.2 0.1 divide_reduce_fusion.3
  160.4 0.8 add_convert_fusion
  161.1 5.5 %all-to-all-done.5.parts_ref = bf16[4,224,128]{2,1,0:T(8,128)(2,1)S(1)} async-done(((bf16[4,224,128]{2,1,0:T(8,128)(2,1)}), bf16[4,224,128]{2,1,0:T(8,128)(2,1)S(1)}, u32[]{:S(2)}, u32[]{:S(2)}) %all-to-all-start.5) | async-done | bytes 229408 | tf_op jit(solution)/shard_map/all_to_all | solution.py:382
  166.6 0.7 summed.1
  (50 shorter events, 0.8 us)
Async XLA Ops:
  0.6 4.4 %copy-start = (bf16[32,3584]{1,0:T(8,128)(2,1)S(1)}, bf16[32,3584]{1,0:T(8,128)(2,1)}, u32[]{:S(2)}) copy-start(bf16[32,3584]{1,0:T(8,128)(2,1)} %param.11) | copy-start | bytes 688132
  0.6 4.2 %copy-start.5 = (f32[32,8]{0,1:T(8,128)S(1)}, f32[32,8]{0,1:T(8,128)}, u32[]{:S(2)}) copy-start(f32[32,8]{0,1:T(8,128)} %param.13) | copy-start | bytes 3076
  0.7 4.3 %copy-start.6 = (s32[32,8]{0,1:T(8,128)S(1)}, s32[32,8]{0,1:T(8,128)}, u32[]{:S(2)}) copy-start(s32[32,8]{0,1:T(8,128)} %param.12) | copy-start | bytes 3076
  0.7 32.6 %all-to-all-start = ((bf16[4,896,256]{2,1,0:T(8,128)(2,1)}), bf16[4,896,256]{2,1,0:T(8,128)(2,1)S(1)}, u32[]{:S(2)}, u32[]{:S(2)}) async-start(bf16[4,896,256]{2,1,0:T(8,128)(2,1)} %bitcast.34), calls=%async_computation | async-start | bytes 3670016 | tf_op jit(solution)/shard_map/all_to_all | solution.py:345
  5.2 27.0 %copy-start.1 = (bf16[1,256,3584]{2,1,0:T(8,128)(2,1)S(1)}, bf16[1,256,3584]{2,1,0:T(8,128)(2,1)}, u32[]{:S(2)}) copy-start(bf16[1,256,3584]{2,1,0:T(8,128)(2,1)} %param.15) | copy-start | bytes 5505028
  33.3 33.5 %all-to-all-start.1 = ((bf16[32,16,896]{2,1,0:T(8,128)(2,1)}), bf16[32,16,896]{2,1,0:T(8,128)(2,1)S(1)}, u32[]{:S(2)}, u32[]{:S(2)}) async-start(bf16[32,16,896]{2,1,0:T(8,128)(2,1)} %bitcast.7), calls=%async_computation.1 | async-start | bytes 1835008 | tf_op jit(solution)/shard_map/all_to_all | solution.py:364
  42.8 11.8 %collective-permute-start = (bf16[128,896]{1,0:T(8,128)(2,1)S(1)}, bf16[128,896]{1,0:T(8,128)(2,1)}, u32[]{:S(2)}, u32[]{:S(2)}) collective-permute-start(bf16[128,896]{1,0:T(8,128)(2,1)S(1)} %get-tuple-element.17), channel_id=1, source_target_pairs={{0,1},{1,2},{2,3},{3,0},{4,5},{5,6},{6,7},{7,4},{8,9},{9,10},{10,1... | collective-permute-start | bytes 688136 | tf_op jit(solution)/shard_map/ppermute | solution.py:332
  46.2 10.6 %collective-permute-start.2 = (bf16[128,896]{1,0:T(8,128)(2,1)}, bf16[128,896]{1,0:T(8,128)(2,1)}, u32[]{:S(2)}, u32[]{:S(2)}) collective-permute-start(bf16[128,896]{1,0:T(8,128)(2,1)} %get-tuple-element.18), channel_id=1, source_target_pairs={{0,3},{1,0},{2,1},{3,2},{4,7},{5,4},{6,5},{7,6},{8,11},{9,8},{10,9... | collective-permute-start | bytes 688136 | tf_op jit(solution)/shard_map/ppermute | solution.py:332
  49.4 22.4 %collective-permute-start.4 = (bf16[256,896]{1,0:T(8,128)(2,1)}, bf16[256,896]{1,0:T(8,128)(2,1)}, u32[]{:S(2)}, u32[]{:S(2)}) collective-permute-start(bf16[256,896]{1,0:T(8,128)(2,1)} %get-tuple-element.19), channel_id=1, source_target_pairs={{0,3},{1,0},{2,1},{3,2},{4,7},{5,4},{6,5},{7,6},{8,11},{9,8},{10,9... | collective-permute-start | bytes 1376264 | tf_op jit(solution)/shard_map/ppermute | solution.py:332
  52.7 19.1 %collective-permute-start.5 = (bf16[256,896]{1,0:T(8,128)(2,1)}, bf16[256,896]{1,0:T(8,128)(2,1)}, u32[]{:S(2)}, u32[]{:S(2)}) collective-permute-start(bf16[256,896]{1,0:T(8,128)(2,1)} %get-tuple-element.20), channel_id=1, source_target_pairs={{0,1},{1,2},{2,3},{3,0},{4,5},{5,6},{6,7},{7,4},{8,9},{9,10},{10,1... | collective-permute-start | bytes 1376264 | tf_op jit(solution)/shard_map/ppermute | solution.py:332
  54.7 17.1 %collective-permute-start.1 = (bf16[128,896]{1,0:T(8,128)(2,1)}, bf16[128,896]{1,0:T(8,128)(2,1)S(1)}, u32[]{:S(2)}, u32[]{:S(2)}) collective-permute-start(bf16[128,896]{1,0:T(8,128)(2,1)} %collective-permute-done), channel_id=1, source_target_pairs={{0,1},{1,2},{2,3},{3,0},{4,5},{5,6},{6,7},{7,4},{8,9},{9,10},{10,1... | collective-permute-start | bytes 688136 | tf_op jit(solution)/shard_map/ppermute | solution.py:332
  56.8 14.9 %collective-permute-start.3 = (bf16[128,896]{1,0:T(8,128)(2,1)}, bf16[128,896]{1,0:T(8,128)(2,1)}, u32[]{:S(2)}, u32[]{:S(2)}) collective-permute-start(bf16[128,896]{1,0:T(8,128)(2,1)} %collective-permute-done.2), channel_id=1, source_target_pairs={{0,3},{1,0},{2,1},{3,2},{4,7},{5,4},{6,5},{7,6},{8,11},{9,8},{10,9... | collective-permute-start | bytes 688136 | tf_op jit(solution)/shard_map/ppermute | solution.py:332
  86.9 14.3 %copy-start.2 = (bf16[1,256,3584]{2,1,0:T(8,128)(2,1)S(1)}, bf16[1,256,3584]{2,1,0:T(8,128)(2,1)}, u32[]{:S(2)}) copy-start(bf16[1,256,3584]{2,1,0:T(8,128)(2,1)} %param.15) | copy-start | bytes 5505028
  104.7 12.1 %copy-start.4 = (bf16[2,32,576]{2,1,0:T(8,128)(2,1)S(1)}, bf16[2,32,576]{2,1,0:T(8,128)(2,1)}, u32[]{:S(2)}) copy-start(bf16[2,32,576]{2,1,0:T(8,128)(2,1)} %q0.1) | copy-start | bytes 221188
  104.7 36.1 %all-to-all-start.4 = ((bf16[32,16,896]{2,1,0:T(8,128)(2,1)}), bf16[32,16,896]{2,1,0:T(8,128)(2,1)S(1)}, u32[]{:S(2)}, u32[]{:S(2)}) async-start(bf16[32,16,896]{2,1,0:T(8,128)(2,1)} %bitcast.10), calls=%async_computation.4 | async-start | bytes 1835008 | tf_op jit(solution)/shard_map/all_to_all | solution.py:374
  116.8 10.0 %copy-start.7 = (s32[2]{0:T(128)S(1)}, s32[2]{0:T(128)}, u32[]{:S(2)}) copy-start(s32[2]{0:T(128)} %param.10) | copy-start | bytes 28
  116.8 11.5 %copy-start.3 = (bf16[2,256,576]{1,2,0:T(8,128)(2,1)S(1)}, bf16[2,256,576]{1,2,0:T(8,128)(2,1)}, u32[]{:S(2)}) copy-start(bf16[2,256,576]{1,2,0:T(8,128)(2,1)} %param.9) | copy-start | bytes 1769476
  116.8 10.1 %collective-permute-start.6 = (bf16[2,32,576]{2,1,0:T(8,128)(2,1)S(1)}, bf16[2,32,576]{2,1,0:T(8,128)(2,1)S(1)}, u32[]{:S(2)}, u32[]{:S(2)}) collective-permute-start(bf16[2,32,576]{2,1,0:T(8,128)(2,1)S(1)} %copy-done.4), channel_id=1, source_target_pairs={{0,1},{1,2},{2,3},{3,0},{4,5},{5,6},{6,7},{7,4},{8,9},{9,10},{10,1... | collective-permute-start | bytes 221192 | tf_op jit(solution)/shard_map/ppermute | solution.py:332
  119.1 7.8 %collective-permute-start.7 = (bf16[2,32,576]{2,1,0:T(8,128)(2,1)S(1)}, bf16[2,32,576]{2,1,0:T(8,128)(2,1)S(1)}, u32[]{:S(2)}, u32[]{:S(2)}) collective-permute-start(bf16[2,32,576]{2,1,0:T(8,128)(2,1)S(1)} %copy-done.4), channel_id=1, source_target_pairs={{0,2},{1,3},{2,0},{3,1},{4,6},{5,7},{6,4},{7,5},{8,10},{9,11},{10,... | collective-permute-start | bytes 221192 | tf_op jit(solution)/shard_map/ppermute | solution.py:332
  122.8 5.5 %collective-permute-start.8 = (bf16[2,32,576]{2,1,0:T(8,128)(2,1)S(1)}, bf16[2,32,576]{2,1,0:T(8,128)(2,1)S(1)}, u32[]{:S(2)}, u32[]{:S(2)}) collective-permute-start(bf16[2,32,576]{2,1,0:T(8,128)(2,1)S(1)} %copy-done.4), channel_id=1, source_target_pairs={{0,3},{1,0},{2,1},{3,2},{4,7},{5,4},{6,5},{7,6},{8,11},{9,8},{10,9... | collective-permute-start | bytes 221192 | tf_op jit(solution)/shard_map/ppermute | solution.py:332
  141.9 24.7 %all-to-all-start.5 = ((bf16[4,224,128]{2,1,0:T(8,128)(2,1)}), bf16[4,224,128]{2,1,0:T(8,128)(2,1)S(1)}, u32[]{:S(2)}, u32[]{:S(2)}) async-start(bf16[4,224,128]{2,1,0:T(8,128)(2,1)} %mixed_rows.1), calls=%async_computation.5 | async-start | bytes 458752 | tf_op jit(solution)/shard_map/all_to_all | solution.py:382
  148.3 8.5 %collective-permute-start.11 = (bf16[2,32,640]{2,1,0:T(8,128)(2,1)S(1)}, bf16[2,32,640]{2,1,0:T(8,128)(2,1)S(1)}, u32[]{:S(2)}, u32[]{:S(2)}) collective-permute-start(bf16[2,32,640]{2,1,0:T(8,128)(2,1)S(1)} %get-tuple-element.46), channel_id=1, source_target_pairs={{0,1},{1,2},{2,3},{3,0},{4,5},{5,6},{6,7},{7,4},{8,9},{9,10},{10,1... | collective-permute-start | bytes 245768 | tf_op jit(solution)/shard_map/ppermute | solution.py:332
  150.5 7.6 %collective-permute-start.10 = (bf16[2,32,640]{2,1,0:T(8,128)(2,1)S(1)}, bf16[2,32,640]{2,1,0:T(8,128)(2,1)S(1)}, u32[]{:S(2)}, u32[]{:S(2)}) collective-permute-start(bf16[2,32,640]{2,1,0:T(8,128)(2,1)S(1)} %get-tuple-element.47), channel_id=1, source_target_pairs={{0,2},{1,3},{2,0},{3,1},{4,6},{5,7},{6,4},{7,5},{8,10},{9,11},{10,... | collective-permute-start | bytes 245768 | tf_op jit(solution)/shard_map/ppermute | solution.py:332
  154.2 5.8 %collective-permute-start.9 = (bf16[2,32,640]{2,1,0:T(8,128)(2,1)S(1)}, bf16[2,32,640]{2,1,0:T(8,128)(2,1)S(1)}, u32[]{:S(2)}, u32[]{:S(2)}) collective-permute-start(bf16[2,32,640]{2,1,0:T(8,128)(2,1)S(1)} %get-tuple-element.48), channel_id=1, source_target_pairs={{0,3},{1,0},{2,1},{3,2},{4,7},{5,4},{6,5},{7,6},{8,11},{9,8},{10,9... | collective-permute-start | bytes 245768 | tf_op jit(solution)/shard_map/ppermute | solution.py:332
